TPU v7x, 32 devices: a whole 2x2x4 slice. The times are simulated.
32 devices in a mesh: inner: 4 (over x, core), outer: 8 (over z, y).
Axes of the slice: x: 2, y: 2, z: 4, core: 2. Of those that a mesh axis runs over, the one named last changes fastest.
Arguments:
- slices: float32 [8, 4, 256, 256], P('outer', 'inner'), may hold values from -1 to 1, as said below
- weight: float32 [8, 4, 256, 256], P('outer', 'inner'), may hold values from -6 to 6
Outputs:
- gradient: float32 [8, 4, 256, 256], P('outer', 'inner')
Inputs may be any that keep to these rules, and one draw needn't show every extreme that they name: `slices`: every slice is an orthogonal matrix up to float32 rounding (only up to rounding: products of its transpose with it differ from the identity by rounding errors).
All inputs are finite; a program needn't handle non-finite values.
Results may differ from a plain program's by a relative error of at most 0.0003.
Values sent between devices are 32-bit elements; how exact they have to be, the bound alone decides.
No kernel may reach another device: no remote copies, remote signals or barrier semaphores. Data moves between devices by JAX's collectives and lax.ppermute only.
A program may use at most 64 MiB of HBM per device.

v0:
```python
import jax
import jax.numpy as jnp
from jax import lax
from jax.sharding import PartitionSpec as P


def carried_in(value, axis, combine, identity, reverse):
    peers, mine = (lax.axis_size(axis), lax.axis_index(axis))
    everything = lax.all_gather(value, axis)
    start = jnp.broadcast_to(jnp.asarray(identity, value.dtype), value.shape)

    def turn(k, before):
        at = peers - 1 - k if reverse else k
        reached = at > mine if reverse else at < mine
        new = combine(before, everything[at])
        return jnp.where(reached, new, before)

    return lax.fori_loop(0, peers, turn, start)


def matmul(left, right):
    return jnp.dot(left, right, precision=lax.Precision.HIGHEST, preferred_element_type=jnp.float32)


def forward_join(earlier, later):
    return matmul(later, earlier)


def backward_join(earlier, later):
    return matmul(earlier, later)


def body(slices, weight):
    count = slices.shape[1]
    order = slices.shape[2]
    eye = jnp.eye(order, dtype=jnp.float32)
    running = slices[0, 0]
    before_inner = carried_in(running, "inner", forward_join, eye, False)
    upto_inner = matmul(running, before_inner)
    after_inner = carried_in(running, "inner", backward_join, eye, True)
    group = matmul(after_inner, upto_inner)
    before_outer = carried_in(group, "outer", forward_join, eye, False)
    earlier = matmul(before_inner, before_outer)
    after_outer = carried_in(group, "outer", backward_join, eye, True)
    later = matmul(after_outer, after_inner)
    tails = [None] * count
    tails[count - 1] = later
    forward = matmul(running, earlier)
    results = [matmul(matmul(tails[0].T, weight[0, 0]), forward)]
    return jnp.stack(results, axis=0)[None]


def solution(mesh):
    in_specs = (P("outer", "inner", None, None), P("outer", "inner", None, None))
    out_specs = P("outer", "inner", None, None)
    return jax.shard_map(body, mesh=mesh, in_specs=in_specs, out_specs=out_specs, check_vma=False)
```

profile of v0, /device:TPU:0, one launch (start us, length us, event | category | flops | bytes accessed | tf_op | source)
XLA Modules:
  0.0 126.0 jit_solution(18261292168767197408)
XLA Ops:
  7.5 20.8 %all-gather.5.cloned.1.call-done = f32[4,1,256,256]{3,2,1,0:T(8,128)} async-done(((f32[1,1,256,256]{3,2,1,0:T(8,128)}), f32[4,1,256,256]{3,2,1,0:T(8,128)}) %all-gather.5.cloned.1.call-update) | async-done | bytes 1048592 | tf_op jit(solution)/shard_map/all_gather | solution.py:9
  28.4 6.4 %while.56 = (s32[]{:T(128)}, f32[256,256]{0,1:T(8,128)S(1)}, s32[]{:T(128)}, f32[4,256,256]{2,1,0:T(8,128)}, s32[]{:T(128)}, /*index=5*/s32[]{:T(128)}, s32[]{:T(128)}, s32[]{:T(128)}) while((s32[]{:T(128)}, f32[256,256]{0,1:T(8,128)S(1)}, s32[]{:T(128)}, f32[4,256,256]{2,1,0:T(8,128)}, s32[]{:T(128)}, /*index=5*/s32[]{:T(128)}, s32[]{:T(128)}, ...), condition=%wide.region_1.2_spmd, body=%wide.region_0.1_spmd.sunk | while | flops 201392128 | bytes 1573009 | solution.py:18
  28.4 1.6 %fusion.51 = f32[256,256]{0,1:T(8,128)S(1)} fusion(f32[256,256]{0,1:T(8,128)S(1)} %copy.37, f32[4,256,256]{2,1,0:T(8,128)} %get-tuple-element.554, s32[]{:T(128)S(6)} %select_n.120, pred[]{:T(512)S(6)} %gt.22), kind=kOutput, calls=%fused_computation.1.clone.1 | convolution fusion | flops 201392128 | bytes 1048581 | tf_op jit(solution)/shard_map/while/body/eval_jaxpr/dot_general | solution.py:22
  30.0 1.6 %fusion.51 = f32[256,256]{0,1:T(8,128)S(1)} fusion(f32[256,256]{0,1:T(8,128)S(1)} %copy.37, f32[4,256,256]{2,1,0:T(8,128)} %get-tuple-element.554, s32[]{:T(128)S(6)} %select_n.120, pred[]{:T(512)S(6)} %gt.22), kind=kOutput, calls=%fused_computation.1.clone.1 | convolution fusion | flops 201392128 | bytes 1048581 | tf_op jit(solution)/shard_map/while/body/eval_jaxpr/dot_general | solution.py:22
  31.6 1.6 %fusion.51 = f32[256,256]{0,1:T(8,128)S(1)} fusion(f32[256,256]{0,1:T(8,128)S(1)} %copy.37, f32[4,256,256]{2,1,0:T(8,128)} %get-tuple-element.554, s32[]{:T(128)S(6)} %select_n.120, pred[]{:T(512)S(6)} %gt.22), kind=kOutput, calls=%fused_computation.1.clone.1 | convolution fusion | flops 201392128 | bytes 1048581 | tf_op jit(solution)/shard_map/while/body/eval_jaxpr/dot_general | solution.py:22
  33.2 1.6 %fusion.51 = f32[256,256]{0,1:T(8,128)S(1)} fusion(f32[256,256]{0,1:T(8,128)S(1)} %copy.37, f32[4,256,256]{2,1,0:T(8,128)} %get-tuple-element.554, s32[]{:T(128)S(6)} %select_n.120, pred[]{:T(512)S(6)} %gt.22), kind=kOutput, calls=%fused_computation.1.clone.1 | convolution fusion | flops 201392128 | bytes 1048581 | tf_op jit(solution)/shard_map/while/body/eval_jaxpr/dot_general | solution.py:22
  34.8 5.6 %while.57 = (s32[]{:T(128)}, f32[256,256]{1,0:T(8,128)S(1)}, s32[]{:T(128)}, f32[4,256,256]{2,1,0:T(8,128)}, s32[]{:T(128)}) while((s32[]{:T(128)}, f32[256,256]{1,0:T(8,128)S(1)}, s32[]{:T(128)}, f32[4,256,256]{2,1,0:T(8,128)}, s32[]{:T(128)}) %tuple.132), condition=%wide.region_3.4_spmd, body=%wide.region_2.3_spmd.sunk | while | flops 201392128 | bytes 1573447 | solution.py:18
  34.9 1.4 %convolution_select_fusion.4 = f32[256,256]{1,0:T(8,128)S(1)} fusion(f32[256,256]{1,0:T(8,128)S(1)} %copy.38, f32[4,256,256]{2,1,0:T(8,128)} %get-tuple-element.572, s32[]{:T(128)} %get-tuple-element.564, pred[]{:T(512)S(6)} %lt.77), kind=kOutput, calls=%fused_computation.5.clone.1 | convolution fusion | flops 201392128 | bytes 1049089 | tf_op jit(solution)/shard_map/while/body/eval_jaxpr/dot_general | solution.py:22
  42.4 49.5 %all-gather.7.cloned.1.call-done = f32[2048,256]{1,0:T(8,128)} async-done(((f32[256,256]{1,0:T(8,128)}), f32[2048,256]{1,0:T(8,128)}) %all-gather.7.cloned.1.call-update) | async-done | bytes 2097168 | tf_op jit(solution)/shard_map/all_gather | solution.py:9
  91.8 12.9 %while.58 = (s32[]{:T(128)}, f32[256,256]{0,1:T(8,128)S(1)}, s32[]{:T(128)}, f32[8,256,256]{2,1,0:T(8,128)}, s32[]{:T(128)}, /*index=5*/s32[]{:T(128)}, s32[]{:T(128)}, s32[]{:T(128)}) while((s32[]{:T(128)}, f32[256,256]{0,1:T(8,128)S(1)}, s32[]{:T(128)}, f32[8,256,256]{2,1,0:T(8,128)}, s32[]{:T(128)}, /*index=5*/s32[]{:T(128)}, s32[]{:T(128)}, ...), condition=%wide.region_5.6_spmd, body=%wide.region_4.5_spmd.sunk | while | flops 201392128 | bytes 1573009 | solution.py:18
  91.8 1.6 %fusion.56 = f32[256,256]{0,1:T(8,128)S(1)} fusion(f32[256,256]{0,1:T(8,128)S(1)} %copy.39, f32[8,256,256]{2,1,0:T(8,128)} %get-tuple-element.593, s32[]{:T(128)S(6)} %select_n.125, pred[]{:T(512)S(6)} %gt.23), kind=kOutput, calls=%fused_computation.10.clone.1 | convolution fusion | flops 201392128 | bytes 1048581 | tf_op jit(solution)/shard_map/while/body/eval_jaxpr/dot_general | solution.py:22
  93.5 1.6 %fusion.56 = f32[256,256]{0,1:T(8,128)S(1)} fusion(f32[256,256]{0,1:T(8,128)S(1)} %copy.39, f32[8,256,256]{2,1,0:T(8,128)} %get-tuple-element.593, s32[]{:T(128)S(6)} %select_n.125, pred[]{:T(512)S(6)} %gt.23), kind=kOutput, calls=%fused_computation.10.clone.1 | convolution fusion | flops 201392128 | bytes 1048581 | tf_op jit(solution)/shard_map/while/body/eval_jaxpr/dot_general | solution.py:22
  95.1 1.6 %fusion.56 = f32[256,256]{0,1:T(8,128)S(1)} fusion(f32[256,256]{0,1:T(8,128)S(1)} %copy.39, f32[8,256,256]{2,1,0:T(8,128)} %get-tuple-element.593, s32[]{:T(128)S(6)} %select_n.125, pred[]{:T(512)S(6)} %gt.23), kind=kOutput, calls=%fused_computation.10.clone.1 | convolution fusion | flops 201392128 | bytes 1048581 | tf_op jit(solution)/shard_map/while/body/eval_jaxpr/dot_general | solution.py:22
  96.7 1.6 %fusion.56 = f32[256,256]{0,1:T(8,128)S(1)} fusion(f32[256,256]{0,1:T(8,128)S(1)} %copy.39, f32[8,256,256]{2,1,0:T(8,128)} %get-tuple-element.593, s32[]{:T(128)S(6)} %select_n.125, pred[]{:T(512)S(6)} %gt.23), kind=kOutput, calls=%fused_computation.10.clone.1 | convolution fusion | flops 201392128 | bytes 1048581 | tf_op jit(solution)/shard_map/while/body/eval_jaxpr/dot_general | solution.py:22
  98.3 1.6 %fusion.56 = f32[256,256]{0,1:T(8,128)S(1)} fusion(f32[256,256]{0,1:T(8,128)S(1)} %copy.39, f32[8,256,256]{2,1,0:T(8,128)} %get-tuple-element.593, s32[]{:T(128)S(6)} %select_n.125, pred[]{:T(512)S(6)} %gt.23), kind=kOutput, calls=%fused_computation.10.clone.1 | convolution fusion | flops 201392128 | bytes 1048581 | tf_op jit(solution)/shard_map/while/body/eval_jaxpr/dot_general | solution.py:22
  99.9 1.6 %fusion.56 = f32[256,256]{0,1:T(8,128)S(1)} fusion(f32[256,256]{0,1:T(8,128)S(1)} %copy.39, f32[8,256,256]{2,1,0:T(8,128)} %get-tuple-element.593, s32[]{:T(128)S(6)} %select_n.125, pred[]{:T(512)S(6)} %gt.23), kind=kOutput, calls=%fused_computation.10.clone.1 | convolution fusion | flops 201392128 | bytes 1048581 | tf_op jit(solution)/shard_map/while/body/eval_jaxpr/dot_general | solution.py:22
  101.5 1.6 %fusion.56 = f32[256,256]{0,1:T(8,128)S(1)} fusion(f32[256,256]{0,1:T(8,128)S(1)} %copy.39, f32[8,256,256]{2,1,0:T(8,128)} %get-tuple-element.593, s32[]{:T(128)S(6)} %select_n.125, pred[]{:T(512)S(6)} %gt.23), kind=kOutput, calls=%fused_computation.10.clone.1 | convolution fusion | flops 201392128 | bytes 1048581 | tf_op jit(solution)/shard_map/while/body/eval_jaxpr/dot_general | solution.py:22
  103.2 1.6 %fusion.56 = f32[256,256]{0,1:T(8,128)S(1)} fusion(f32[256,256]{0,1:T(8,128)S(1)} %copy.39, f32[8,256,256]{2,1,0:T(8,128)} %get-tuple-element.593, s32[]{:T(128)S(6)} %select_n.125, pred[]{:T(512)S(6)} %gt.23), kind=kOutput, calls=%fused_computation.10.clone.1 | convolution fusion | flops 201392128 | bytes 1048581 | tf_op jit(solution)/shard_map/while/body/eval_jaxpr/dot_general | solution.py:22
  105.3 11.1 %while.59 = (s32[]{:T(128)}, f32[256,256]{1,0:T(8,128)S(1)}, s32[]{:T(128)}, f32[8,256,256]{2,1,0:T(8,128)}, s32[]{:T(128)}) while((s32[]{:T(128)}, f32[256,256]{1,0:T(8,128)S(1)}, s32[]{:T(128)}, f32[8,256,256]{2,1,0:T(8,128)}, s32[]{:T(128)}) %tuple.134), condition=%wide.region_7.8_spmd, body=%wide.region_6.7_spmd.sunk | while | flops 201392128 | bytes 1573447 | solution.py:18
  105.4 1.3 %convolution_select_fusion.5 = f32[256,256]{1,0:T(8,128)S(1)} fusion(f32[256,256]{1,0:T(8,128)S(1)} %copy.40, f32[8,256,256]{2,1,0:T(8,128)} %get-tuple-element.611, s32[]{:T(128)} %get-tuple-element.603, pred[]{:T(512)S(6)} %lt.79), kind=kOutput, calls=%fused_computation.14.clone.1 | convolution fusion | flops 201392128 | bytes 1049089 | tf_op jit(solution)/shard_map/while/body/eval_jaxpr/dot_general | solution.py:22
  106.8 1.3 %convolution_select_fusion.5 = f32[256,256]{1,0:T(8,128)S(1)} fusion(f32[256,256]{1,0:T(8,128)S(1)} %copy.40, f32[8,256,256]{2,1,0:T(8,128)} %get-tuple-element.611, s32[]{:T(128)} %get-tuple-element.603, pred[]{:T(512)S(6)} %lt.79), kind=kOutput, calls=%fused_computation.14.clone.1 | convolution fusion | flops 201392128 | bytes 1049089 | tf_op jit(solution)/shard_map/while/body/eval_jaxpr/dot_general | solution.py:22
  108.2 1.3 %convolution_select_fusion.5 = f32[256,256]{1,0:T(8,128)S(1)} fusion(f32[256,256]{1,0:T(8,128)S(1)} %copy.40, f32[8,256,256]{2,1,0:T(8,128)} %get-tuple-element.611, s32[]{:T(128)} %get-tuple-element.603, pred[]{:T(512)S(6)} %lt.79), kind=kOutput, calls=%fused_computation.14.clone.1 | convolution fusion | flops 201392128 | bytes 1049089 | tf_op jit(solution)/shard_map/while/body/eval_jaxpr/dot_general | solution.py:22
  109.5 1.3 %convolution_select_fusion.5 = f32[256,256]{1,0:T(8,128)S(1)} fusion(f32[256,256]{1,0:T(8,128)S(1)} %copy.40, f32[8,256,256]{2,1,0:T(8,128)} %get-tuple-element.611, s32[]{:T(128)} %get-tuple-element.603, pred[]{:T(512)S(6)} %lt.79), kind=kOutput, calls=%fused_computation.14.clone.1 | convolution fusion | flops 201392128 | bytes 1049089 | tf_op jit(solution)/shard_map/while/body/eval_jaxpr/dot_general | solution.py:22
  110.9 1.3 %convolution_select_fusion.5 = f32[256,256]{1,0:T(8,128)S(1)} fusion(f32[256,256]{1,0:T(8,128)S(1)} %copy.40, f32[8,256,256]{2,1,0:T(8,128)} %get-tuple-element.611, s32[]{:T(128)} %get-tuple-element.603, pred[]{:T(512)S(6)} %lt.79), kind=kOutput, calls=%fused_computation.14.clone.1 | convolution fusion | flops 201392128 | bytes 1049089 | tf_op jit(solution)/shard_map/while/body/eval_jaxpr/dot_general | solution.py:22
  (49 shorter events, 14.6 us)
Async XLA Ops:
  6.5 110.9 %copy-start = (f32[1,1,256,256]{3,2,1,0:T(8,128)S(1)}, f32[1,1,256,256]{3,2,1,0:T(8,128)}, u32[]{:S(2)}) copy-start(f32[1,1,256,256]{3,2,1,0:T(8,128)} %param.11) | copy-start | bytes 786436
  6.5 21.8 %all-gather.5.cloned.1.call-start = ((), (), s32[]{:S(2)}) async-start(), calls=%async_computation | async-start | bytes 1310720 | tf_op jit(solution)/shard_map/all_gather | solution.py:9
  7.3 84.6 %all-gather.7.cloned.1.call-start = ((), (), s32[]{:S(2)}) async-start(), calls=%async_computation.1 | async-start | bytes 2359296 | tf_op jit(solution)/shard_map/all_gather | solution.py:9
  34.8 5.6 %copy-start.1 = (f32[1,1,256,256]{3,2,1,0:T(8,128)S(1)}, f32[1,1,256,256]{3,2,1,0:T(8,128)}, u32[]{:S(2)}) copy-start(f32[1,1,256,256]{3,2,1,0:T(8,128)} %param.10) | copy-start | bytes 786436
Sparse Core Ops, SparseCore 0:
  8.9 19.4 all-gather.4
  42.5 49.2 all-gather.6
where the time goes:
time: 127 us; the launch traced here: 126 us
  waiting for transfers between devices  71 us (56%)
  matrix products  39.9 us (31%)
  between operations  13.5 us (11%)
    all_gather x2, waiting for transfers between devices, carried_in(): everything = lax.all_gather(value, axis)  70.3 us
    dot_general x31, matrix products, matmul(): jnp.dot(left, right, precision=lax.Precision.HIGHEST, preferred_element_t...  39.9 us
  transfers between devices with their start and end apart: 2, of which 2 were waited for; matrix products, arithmetic and copies ran while one was open for 0% of the time, Pallas kernels for 0%

commit v1 on v0

v1 whole, which is shorter than its diff:
```python
import jax
import jax.numpy as jnp
from jax import lax
from jax.sharding import PartitionSpec as P


def dot(left, right):
    return jnp.dot(left, right, precision=lax.Precision.HIGHEST, preferred_element_type=jnp.float32)


def dot_nt(left, right):
    dims = (((1,), (1,)), ((), ()))
    return lax.dot_general(left, right, dims, precision=lax.Precision.HIGHEST, preferred_element_type=jnp.float32)


def dot_tn(left, right):
    dims = (((0,), (0,)), ((), ()))
    return lax.dot_general(left, right, dims, precision=lax.Precision.HIGHEST, preferred_element_type=jnp.float32)


def ordered(first, a, b):
    return jnp.where(first, a, b), jnp.where(first, b, a)


class Group:
    def __init__(self, n_in, n_out):
        self.n = n_in * n_out
        self.place = [(k % n_in) * n_out + k // n_in for k in range(self.n)]
        self.index = lax.axis_index("outer") * n_in + lax.axis_index("inner")

    def bit(self, b):
        return (self.index >> b) & 1 == 1

    def send(self, value, even, odd=None):
        pairs = []
        for k in range(self.n):
            mask = odd if k & 1 else even
            if mask is not None:
                pairs.append((self.place[k], self.place[k ^ mask]))
        return lax.ppermute(value, ("inner", "outer"), pairs)

    def swap(self, value, mask):
        return self.send(value, mask, mask)


def join(group, b, by, before, after):
    flag = group.bit(b)
    new = dot(jnp.where(flag, before, by), jnp.where(flag, by, after))
    return jnp.where(flag, new, before), jnp.where(flag, after, new)


def pairwise(group, bits, total, before, after):
    for b in bits:
        by = group.swap(total, 1 << b)
        before, after = join(group, b, by, before, after)
        total = dot(*ordered(group.bit(b), total, by))
    return before, after


def body(n_in, n_out, slices, weight):
    group = Group(n_in, n_out)
    mine, w = slices[0, 0], weight[0, 0]
    order = mine.shape[0]
    part = order // 2
    eye = jnp.eye(order, dtype=jnp.float32)
    bits = group.n.bit_length() - 1
    if bits < 5:
        before, after = pairwise(group, range(bits), mine, mine, eye)
        return dot(dot_tn(after, w), before)[None, None]
    second = group.bit(0)

    def whole(piece):
        other = group.swap(piece, 1)
        return jnp.concatenate([jnp.where(second, other, piece), jnp.where(second, piece, other)], axis=0)

    def pair_of_pairs(product):
        other = group.swap(product, 1)
        return jnp.where(second, other, product), jnp.where(second, product, other)

    other = group.swap(mine, 1)
    chip = dot(*ordered(second, mine, other))
    wide = group.send(chip, 24, 6)
    close = group.send(chip, 2, 4)
    product = dot(*ordered(group.bit(1), jnp.where(second, close, chip), jnp.where(second, wide, close)))
    beside = group.send(wide, 2)
    near, far = pair_of_pairs(product)
    left, right = ordered(group.bit(2), near, far)
    four_piece = dot(lax.dynamic_slice_in_dim(left, (group.index & 1) * part, part, 0), right)
    one_piece, two_piece = group.swap(four_piece, 8), group.swap(four_piece, 16)
    flag = group.bit(1)
    left = jnp.where(second, near, jnp.where(flag, mine, close))
    right = jnp.where(second, jnp.where(flag, eye, chip.T), jnp.where(flag, close, other))
    new = dot(left, right)
    before = jnp.where(flag, new, jnp.where(second, chip, mine))
    after = jnp.where(flag, jnp.where(second, eye, other), new)
    before, after = join(group, 2, far, before, after)
    product = dot(*ordered(group.bit(1), wide, beside))
    across = group.send(product, 5)
    three = dot(*ordered(group.bit(2), *pair_of_pairs(jnp.where(second, across, product))))
    one, two = whole(one_piece), whole(two_piece)
    if bits > 5:
        four = dot(left, right)
        eight = dot(*ordered(group.bit(3), four, one))
        others = dot(*ordered(group.bit(3), two, three))
        before, after = join(group, 3, one, before, after)
        before, after = join(group, 4, others, before, after)
        total = dot(*ordered(group.bit(4), eight, others))
        before, after = pairwise(group, range(5, bits), total, before, after)
        return dot(dot_tn(after, w), before)[None, None]
    after_t = after.T
    wp = dot(w, before)

    def start0():
        return dot_nt(after_t, one), dot_tn(three, wp)

    def start1():
        return dot_nt(after_t, three), dot(wp, one)

    def start2():
        return dot(dot(dot_nt(after_t, one), wp), three), three

    def start3():
        return dot(dot(after_t, wp), one), three

    def end0():
        return dot(dot_nt(a, two), b)

    def end2():
        return dot(a, two)

    def end3():
        return dot(dot(a, two), b)

    which = (group.index >> 3) & 3
    a, b = lax.switch(which, [start0, start1, start2, start3])
    result = lax.switch(which, [end0, end0, end2, end3])
    return result[None, None]


def solution(mesh):
    spec = P("outer", "inner", None, None)
    n_in, n_out = mesh.shape["inner"], mesh.shape["outer"]

    def run(slices, weight):
        return body(n_in, n_out, slices, weight)

    return jax.shard_map(run, mesh=mesh, in_specs=(spec, spec), out_specs=spec, check_vma=False)
```

time: 127 us -> 35.6 us (0.28)
  waiting for transfers between devices: 71 us -> 10.2 us
  matrix products: 39.9 us -> 6.44 us
  starting transfers between devices: 0.04 us -> 17.5 us
  between operations: 13.5 us -> 0.23 us
    all_gather x2 -> x0, waiting for transfers between devices: 70.3 us -> none  [carried_in(): everything = lax.all_gather(value, axis)]
    dot_general x31 -> x12, matrix products: 39.9 us -> 6.44 us  [the longest x9 4.85 us: dot(): jnp.dot(left, right, precision=lax.Precision.HIGHEST, preferred_element_t...]
    ppermute x0 -> x11, starting transfers between devices: none -> 17.5 us  [send(): return lax.ppermute(value, ('inner', 'outer'), pairs)]
    ppermute x0 -> x11, waiting for transfers between devices: none -> 10.2 us  [send(): return lax.ppermute(value, ('inner', 'outer'), pairs)]
  transfers between devices with their start and end apart: 2 -> 11, of which waited for: 2 -> 8; matrix products, arithmetic and copies ran while one was open for 0% -> 7% of each run, Pallas kernels for 0% -> 0%
where the time goes in v1:
time: 35.6 us; the launch traced here: 35.5 us
  starting transfers between devices  17.5 us (49%)
  waiting for transfers between devices  10.2 us (29%)
  matrix products  6.44 us (18%)
  local copies, waits for them, and re-layouts  0.86 us (2%)
    ppermute x11, starting transfers between devices, send(): return lax.ppermute(value, ('inner', 'outer'), pairs)  17.5 us
    ppermute x11, waiting for transfers between devices, send(): return lax.ppermute(value, ('inner', 'outer'), pairs)  10.2 us
    dot_general x9, matrix products, dot(): jnp.dot(left, right, precision=lax.Precision.HIGHEST, preferred_element_t...  4.85 us
    dot_general x2, matrix products, dot_nt(): lax.dot_general(left, right, dims, precision=lax.Precision.HIGHEST, prefe...  1 us
  transfers between devices with their start and end apart: 11, of which 8 were waited for; matrix products, arithmetic and copies ran while one was open for 7% of the time, Pallas kernels for 0%

profile of v1, /device:TPU:0, one launch (start us, length us, event | category | flops | bytes accessed | tf_op | source)
XLA Modules:
  0.0 35.5 jit_solution(663089258089224234)
XLA Ops:
  0.0 0.5 %collective-permute-start = (f32[256,256]{1,0:T(8,128)}, f32[256,256]{1,0:T(8,128)S(1)}, u32[]{:S(2)}, u32[]{:S(2)}) collective-permute-start(f32[256,256]{1,0:T(8,128)} %bitcast.70), channel_id=1, source_target_pairs={{0,8},{8,0},{16,24},{24,16},{1,9},{9,1},{17,25},{25,17},{2,10},{10... | collective-permute-start | bytes 786440 | tf_op jit(solution)/shard_map/ppermute | solution.py:40
  0.5 1.4 %collective-permute-done = f32[256,256]{1,0:T(8,128)S(1)} collective-permute-done((f32[256,256]{1,0:T(8,128)}, f32[256,256]{1,0:T(8,128)S(1)}, u32[]{:S(2)}, u32[]{:S(2)}) %collective-permute-start) | collective-permute-done | bytes 262176 | tf_op jit(solution)/shard_map/ppermute | solution.py:40
  1.8 1.4 %fusion.28 = f32[256,256]{1,0:T(8,128)S(1)} fusion(f32[256,256]{1,0:T(8,128)S(1)} %collective-permute-done, pred[]{:T(512)S(6)} %eq.20, f32[1,1,256,256]{3,2,1,0:T(8,128)} %param.10), kind=kOutput, calls=%fused_computation.38 | convolution fusion | flops 201457664 | bytes 786433 | tf_op jit(solution)/shard_map/dot_general | solution.py:8
  3.3 5.0 %collective-permute-start.2 = (f32[256,256]{1,0:T(8,128)S(1)}, f32[256,256]{1,0:T(8,128)S(1)}, u32[]{:S(2)}, u32[]{:S(2)}) collective-permute-start(f32[256,256]{1,0:T(8,128)S(1)} %fusion.28), channel_id=1, source_target_pairs={{0,6},{8,25},{16,22},{24,9},{1,7},{9,24},{17,23},{25,8},{2,4},{10,... | collective-permute-start | bytes 786440 | tf_op jit(solution)/shard_map/ppermute | solution.py:40
  8.3 1.5 %collective-permute-start.1 = (f32[256,256]{1,0:T(8,128)S(1)}, f32[256,256]{1,0:T(8,128)S(1)}, u32[]{:S(2)}, u32[]{:S(2)}) collective-permute-start(f32[256,256]{1,0:T(8,128)S(1)} %fusion.28), channel_id=1, source_target_pairs={{0,16},{8,9},{16,0},{24,25},{1,17},{9,8},{17,1},{25,24},{2,18},{10... | collective-permute-start | bytes 786440 | tf_op jit(solution)/shard_map/ppermute | solution.py:40
  9.8 3.0 %collective-permute-done.2 = f32[256,256]{1,0:T(8,128)S(1)} collective-permute-done((f32[256,256]{1,0:T(8,128)S(1)}, f32[256,256]{1,0:T(8,128)S(1)}, u32[]{:S(2)}, u32[]{:S(2)}) %collective-permute-start.2) | collective-permute-done | bytes 262176 | tf_op jit(solution)/shard_map/ppermute | solution.py:40
  12.8 1.9 %collective-permute-done.1 = f32[256,256]{1,0:T(8,128)S(1)} collective-permute-done((f32[256,256]{1,0:T(8,128)S(1)}, f32[256,256]{1,0:T(8,128)S(1)}, u32[]{:S(2)}, u32[]{:S(2)}) %collective-permute-start.1) | collective-permute-done | bytes 262176 | tf_op jit(solution)/shard_map/ppermute | solution.py:40
  15.3 3.4 %collective-permute-start.6 = (f32[256,256]{1,0:T(8,128)S(1)}, f32[256,256]{1,0:T(8,128)S(1)}, u32[]{:S(2)}, u32[]{:S(2)}) collective-permute-start(f32[256,256]{1,0:T(8,128)S(1)} %collective-permute-done.2), channel_id=1, source_target_pairs={{0,16},{16,0},{1,17},{17,1},{2,18},{18,2},{3,19},{19,3},{4,20},{20... | collective-permute-start | bytes 786440 | tf_op jit(solution)/shard_map/ppermute | solution.py:40
  19.1 1.0 %collective-permute-start.4 = (f32[128,256]{1,0:T(8,128)S(1)}, f32[128,256]{1,0:T(8,128)S(1)}, u32[]{:S(2)}, u32[]{:S(2)}) collective-permute-start(f32[128,256]{1,0:T(8,128)S(1)} %fusion.15), channel_id=1, source_target_pairs={{0,2},{8,10},{16,18},{24,26},{1,3},{9,11},{17,19},{25,27},{2,0},{1... | collective-permute-start | bytes 393224 | tf_op jit(solution)/shard_map/ppermute | solution.py:40
  20.1 2.6 %collective-permute-start.9 = (f32[128,256]{1,0:T(8,128)S(1)}, f32[128,256]{1,0:T(8,128)S(1)}, u32[]{:S(2)}, u32[]{:S(2)}) collective-permute-start(f32[128,256]{1,0:T(8,128)S(1)} %fusion.15), channel_id=1, source_target_pairs={{0,4},{8,12},{16,20},{24,28},{1,5},{9,13},{17,21},{25,29},{2,6},{1... | collective-permute-start | bytes 393224 | tf_op jit(solution)/shard_map/ppermute | solution.py:40
  22.7 0.9 %collective-permute-done.6 = f32[256,256]{1,0:T(8,128)S(1)} collective-permute-done((f32[256,256]{1,0:T(8,128)S(1)}, f32[256,256]{1,0:T(8,128)S(1)}, u32[]{:S(2)}, u32[]{:S(2)}) %collective-permute-start.6) | collective-permute-done | bytes 262176 | tf_op jit(solution)/shard_map/ppermute | solution.py:40
  24.0 1.3 %collective-permute-start.7 = (f32[256,256]{1,0:T(8,128)S(1)}, f32[256,256]{1,0:T(8,128)S(1)}, u32[]{:S(2)}, u32[]{:S(2)}) collective-permute-start(f32[256,256]{1,0:T(8,128)S(1)} %fusion.12), channel_id=1, source_target_pairs={{0,9},{16,25},{1,8},{17,24},{2,11},{18,27},{3,10},{19,26},{4,13},{... | collective-permute-start | bytes 786440 | tf_op jit(solution)/shard_map/ppermute | solution.py:40
  25.3 0.4 %fusion.2 = f32[256,256]{1,0:T(8,128)S(1)} fusion(f32[256,256]{0,1:T(8,128)S(1)} %copy.7, f32[256,256]{1,0:T(8,128)S(1)} %collective-permute-done.1, f32[256,256]{1,0:T(8,128)S(1)} %collective-permute-done, f32[256,256]{1,0:T(8,128)S(1)} %get-tuple-element.113, pred[]{:T(512)S(6)} %eq.20, pred[]{:T(512)S(6)} %eq.19, f32[1,1,256,256]{3,2,1,0:T(8,128)S(1)} %copy-done.1), kind=kOutput, calls=%fused_computation.9 | convolution fusion | flops 201785344 | bytes 1572866 | tf_op jit(solution)/shard_map/dot_general | solution.py:8
  25.8 0.5 %fusion.17 = f32[256,256]{1,0:T(8,128)S(1)} fusion(f32[256,256]{1,0:T(8,128)S(1)} %get-tuple-element.114, pred[]{:T(512)S(6)} %eq.18, f32[256,256]{1,0:T(8,128)S(1)} %fusion.2, f32[256,256]{1,0:T(8,128)S(1)} %collective-permute-done, pred[]{:T(512)S(6)} %eq.20, pred[]{:T(512)S(6)} %eq.19, f32[256,256]{1,0:T(8,128)S(1)} %fusion.28, ...), kind=kOutput, calls=%fused_computation.26 | convolution fusion | flops 201850880 | bytes 1572867 | tf_op jit(solution)/shard_map/dot_general | solution.py:8
  26.2 0.6 %convolution_bitcast_fusion.4 = f32[256,256]{0,1:T(8,128)S(1)} fusion(f32[1,1,256,256]{3,2,1,0:T(8,128)S(1)} %copy-done, f32[256,256]{1,0:T(8,128)S(1)} %fusion.17, pred[]{:T(512)S(6)} %eq.18, f32[256,256]{1,0:T(8,128)S(1)} %fusion.2, f32[256,256]{1,0:T(8,128)S(1)} %fusion.28, pred[]{:T(512)S(6)} %eq.20, pred[]{:T(512)S(6)} %eq.19, ...), kind=kOutput, calls=%fused_computation.4 | convolution fusion | flops 201523200 | bytes 1572867 | tf_op jit(solution)/shard_map/dot_general | solution.py:8
  27.6 0.7 %collective-permute-done.5 = f32[128,256]{1,0:T(8,128)S(1)} collective-permute-done((f32[128,256]{1,0:T(8,128)S(1)}, f32[128,256]{1,0:T(8,128)S(1)}, u32[]{:S(2)}, u32[]{:S(2)}) %collective-permute-start.5) | collective-permute-done | bytes 131104 | tf_op jit(solution)/shard_map/ppermute | solution.py:40
  28.3 0.8 %collective-permute-done.7 = f32[256,256]{1,0:T(8,128)S(1)} collective-permute-done((f32[256,256]{1,0:T(8,128)S(1)}, f32[256,256]{1,0:T(8,128)S(1)}, u32[]{:S(2)}, u32[]{:S(2)}) %collective-permute-start.7) | collective-permute-done | bytes 262176 | tf_op jit(solution)/shard_map/ppermute | solution.py:40
  29.2 1.9 %collective-permute-start.8 = (f32[256,256]{1,0:T(8,128)S(1)}, f32[256,256]{1,0:T(8,128)S(1)}, u32[]{:S(2)}, u32[]{:S(2)}) collective-permute-start(f32[256,256]{1,0:T(8,128)S(1)} %broadcast_select_fusion.1), channel_id=1, source_target_pairs={{0,8},{8,0},{16,24},{24,16},{1,9},{9,1},{17,25},{25,17},{2,10},{10... | collective-permute-start | bytes 786440 | tf_op jit(solution)/shard_map/ppermute | solution.py:40
  31.1 1.1 %collective-permute-done.8 = f32[256,256]{1,0:T(8,128)S(1)} collective-permute-done((f32[256,256]{1,0:T(8,128)S(1)}, f32[256,256]{1,0:T(8,128)S(1)}, u32[]{:S(2)}, u32[]{:S(2)}) %collective-permute-start.8) | collective-permute-done | bytes 262176 | tf_op jit(solution)/shard_map/ppermute | solution.py:40
  32.6 1.3 %conditional.2 = (f32[256,256]{1,0:T(8,128)S(1)}, f32[256,256]{1,0:T(8,128)S(1)}) conditional(s32[]{:T(128)} %clamp.4, (f32[256,256]{0,1:T(8,128)S(1)}, f32[256,256]{1,0:T(8,128)S(1)}, f32[256,256]{1,0:T(8,128)S(1)}, f32[256,256]{0,1:T(8,128)S(1)}) %tuple.37, (f32[256,256]{0,1:T(8,128)S(1)}, ...), branch_computations={%region_0.1_spmd, %region_1.2_spmd, %region_2.3_spmd, %region_3.4_... | conditional | flops 603979776 | bytes 2359312 | solution.py:135
  32.7 0.6 %fusion.48 = f32[256,256]{1,0:T(8,128)S(1)} fusion(f32[256,256]{0,1:T(8,128)S(1)} %get-tuple-element.97, f32[256,256]{1,0:T(8,128)S(1)} %get-tuple-element.66), kind=kOutput, calls=%fused_computation.66 | convolution fusion | flops 201326592 | bytes 786432 | tf_op jit(solution)/shard_map/cond/branch_0_fun/dot_general | solution.py:13
  33.3 0.6 %fusion.49 = f32[256,256]{1,0:T(8,128)S(1)} fusion(f32[256,256]{1,0:T(8,128)S(1)} %copy.36, f32[256,256]{0,1:T(8,128)S(1)} %get-tuple-element.100), kind=kOutput, calls=%fused_computation.67 | convolution fusion | flops 201326592 | bytes 786432 | tf_op jit(solution)/shard_map/cond/branch_0_fun/dot_general | solution.py:18
  33.9 0.8 %conditional.3 = (f32[1,1,256,256]{3,2,1,0:T(8,128)S(1)}) conditional(s32[]{:T(128)} %clamp.4, (f32[256,256]{1,0:T(8,128)S(1)}, f32[256,256]{1,0:T(8,128)S(1)}, f32[256,256]{1,0:T(8,128)S(1)}) %tuple.41, (f32[256,256]{1,0:T(8,128)S(1)}, f32[256,256]{1,0:T(8,128)S(1)}, f32[256,256]{1,0:T(8,128)S(1)}) %tuple.41, ...), branch_computations={%region_4.5_spmd, %region_5.6_spmd, %region_6.7_spmd, %region_7.8_... | conditional | flops 402653184 | bytes 1572872 | solution.py:136
  34.8 0.7 %copy-done.2 = f32[1,1,256,256]{3,2,1,0:T(8,128)} copy-done((f32[1,1,256,256]{3,2,1,0:T(8,128)}, f32[1,1,256,256]{3,2,1,0:T(8,128)S(1)}, u32[]{:S(2)}) %copy-start.2) | copy-done | bytes 262168
  (27 shorter events, 3.4 us)
Async XLA Ops:
  0.0 26.2 %copy-start = (f32[1,1,256,256]{3,2,1,0:T(8,128)S(1)}, f32[1,1,256,256]{3,2,1,0:T(8,128)}, u32[]{:S(2)}) copy-start(f32[1,1,256,256]{3,2,1,0:T(8,128)} %param.11) | copy-start | bytes 786436
  0.0 1.8 %collective-permute-start = (f32[256,256]{1,0:T(8,128)}, f32[256,256]{1,0:T(8,128)S(1)}, u32[]{:S(2)}, u32[]{:S(2)}) collective-permute-start(f32[256,256]{1,0:T(8,128)} %bitcast.70), channel_id=1, source_target_pairs={{0,8},{8,0},{16,24},{24,16},{1,9},{9,1},{17,25},{25,17},{2,10},{10... | collective-permute-start | bytes 786440 | tf_op jit(solution)/shard_map/ppermute | solution.py:40
  3.3 9.5 %collective-permute-start.2 = (f32[256,256]{1,0:T(8,128)S(1)}, f32[256,256]{1,0:T(8,128)S(1)}, u32[]{:S(2)}, u32[]{:S(2)}) collective-permute-start(f32[256,256]{1,0:T(8,128)S(1)} %fusion.28), channel_id=1, source_target_pairs={{0,6},{8,25},{16,22},{24,9},{1,7},{9,24},{17,23},{25,8},{2,4},{10,... | collective-permute-start | bytes 786440 | tf_op jit(solution)/shard_map/ppermute | solution.py:40
  8.3 6.4 %collective-permute-start.1 = (f32[256,256]{1,0:T(8,128)S(1)}, f32[256,256]{1,0:T(8,128)S(1)}, u32[]{:S(2)}, u32[]{:S(2)}) collective-permute-start(f32[256,256]{1,0:T(8,128)S(1)} %fusion.28), channel_id=1, source_target_pairs={{0,16},{8,9},{16,0},{24,25},{1,17},{9,8},{17,1},{25,24},{2,18},{10... | collective-permute-start | bytes 786440 | tf_op jit(solution)/shard_map/ppermute | solution.py:40
  15.1 3.6 %collective-permute-start.3 = (f32[256,256]{1,0:T(8,128)S(1)}, f32[256,256]{1,0:T(8,128)S(1)}, u32[]{:S(2)}, u32[]{:S(2)}) collective-permute-start(f32[256,256]{1,0:T(8,128)S(1)} %fusion.23), channel_id=1, source_target_pairs={{0,8},{8,0},{16,24},{24,16},{1,9},{9,1},{17,25},{25,17},{2,10},{10... | collective-permute-start | bytes 786440 | tf_op jit(solution)/shard_map/ppermute | solution.py:40
  15.3 8.3 %collective-permute-start.6 = (f32[256,256]{1,0:T(8,128)S(1)}, f32[256,256]{1,0:T(8,128)S(1)}, u32[]{:S(2)}, u32[]{:S(2)}) collective-permute-start(f32[256,256]{1,0:T(8,128)S(1)} %collective-permute-done.2), channel_id=1, source_target_pairs={{0,16},{16,0},{1,17},{17,1},{2,18},{18,2},{3,19},{19,3},{4,20},{20... | collective-permute-start | bytes 786440 | tf_op jit(solution)/shard_map/ppermute | solution.py:40
  19.1 6.2 %copy-start.1 = (f32[1,1,256,256]{3,2,1,0:T(8,128)S(1)}, f32[1,1,256,256]{3,2,1,0:T(8,128)}, u32[]{:S(2)}) copy-start(f32[1,1,256,256]{3,2,1,0:T(8,128)} %param.10) | copy-start | bytes 786436
  19.1 7.8 %collective-permute-start.4 = (f32[128,256]{1,0:T(8,128)S(1)}, f32[128,256]{1,0:T(8,128)S(1)}, u32[]{:S(2)}, u32[]{:S(2)}) collective-permute-start(f32[128,256]{1,0:T(8,128)S(1)} %fusion.15), channel_id=1, source_target_pairs={{0,2},{8,10},{16,18},{24,26},{1,3},{9,11},{17,19},{25,27},{2,0},{1... | collective-permute-start | bytes 393224 | tf_op jit(solution)/shard_map/ppermute | solution.py:40
  20.1 7.3 %collective-permute-start.9 = (f32[128,256]{1,0:T(8,128)S(1)}, f32[128,256]{1,0:T(8,128)S(1)}, u32[]{:S(2)}, u32[]{:S(2)}) collective-permute-start(f32[128,256]{1,0:T(8,128)S(1)} %fusion.15), channel_id=1, source_target_pairs={{0,4},{8,12},{16,20},{24,28},{1,5},{9,13},{17,21},{25,29},{2,6},{1... | collective-permute-start | bytes 393224 | tf_op jit(solution)/shard_map/ppermute | solution.py:40
  24.0 5.2 %collective-permute-start.7 = (f32[256,256]{1,0:T(8,128)S(1)}, f32[256,256]{1,0:T(8,128)S(1)}, u32[]{:S(2)}, u32[]{:S(2)}) collective-permute-start(f32[256,256]{1,0:T(8,128)S(1)} %fusion.12), channel_id=1, source_target_pairs={{0,9},{16,25},{1,8},{17,24},{2,11},{18,27},{3,10},{19,26},{4,13},{... | collective-permute-start | bytes 786440 | tf_op jit(solution)/shard_map/ppermute | solution.py:40
  26.9 1.4 %collective-permute-start.5 = (f32[128,256]{1,0:T(8,128)S(1)}, f32[128,256]{1,0:T(8,128)S(1)}, u32[]{:S(2)}, u32[]{:S(2)}) collective-permute-start(f32[128,256]{1,0:T(8,128)S(1)} %collective-permute-done.4), channel_id=1, source_target_pairs={{0,8},{8,0},{16,24},{24,16},{1,9},{9,1},{17,25},{25,17},{2,10},{10... | collective-permute-start | bytes 393224 | tf_op jit(solution)/shard_map/ppermute | solution.py:40
  27.4 3.7 %collective-permute-start.10 = (f32[128,256]{1,0:T(8,128)S(1)}, f32[128,256]{1,0:T(8,128)S(1)}, u32[]{:S(2)}, u32[]{:S(2)}) collective-permute-start(f32[128,256]{1,0:T(8,128)S(1)} %collective-permute-done.9), channel_id=1, source_target_pairs={{0,8},{8,0},{16,24},{24,16},{1,9},{9,1},{17,25},{25,17},{2,10},{10... | collective-permute-start | bytes 393224 | tf_op jit(solution)/shard_map/ppermute | solution.py:40
  29.2 3.0 %collective-permute-start.8 = (f32[256,256]{1,0:T(8,128)S(1)}, f32[256,256]{1,0:T(8,128)S(1)}, u32[]{:S(2)}, u32[]{:S(2)}) collective-permute-start(f32[256,256]{1,0:T(8,128)S(1)} %broadcast_select_fusion.1), channel_id=1, source_target_pairs={{0,8},{8,0},{16,24},{24,16},{1,9},{9,1},{17,25},{25,17},{2,10},{10... | collective-permute-start | bytes 786440 | tf_op jit(solution)/shard_map/ppermute | solution.py:40
  34.7 0.7 %copy-start.2 = (f32[1,1,256,256]{3,2,1,0:T(8,128)}, f32[1,1,256,256]{3,2,1,0:T(8,128)S(1)}, u32[]{:S(2)}) copy-start(f32[1,1,256,256]{3,2,1,0:T(8,128)S(1)} %get-tuple-element.143) | copy-start | bytes 786436

commit v2 on v0

v2 whole, which is shorter than its diff:
```python
import functools

import jax
import jax.numpy as jnp
from jax import lax
from jax.experimental import pallas as pl
from jax.experimental.pallas import tpu as pltpu
from jax.sharding import PartitionSpec as P


FAR = 200


def halves(value):
    high = value.astype(jnp.bfloat16)
    return high, (value - high.astype(jnp.float32)).astype(jnp.bfloat16)


def product(left, right, dims):
    def one_pass(a, b):
        return lax.dot_general(a, b, (dims, ((), ())), preferred_element_type=jnp.float32)

    (left_high, left_low), (right_high, right_low) = halves(left), halves(right)
    cross = one_pass(left_high, right_low) + one_pass(left_low, right_high)
    return one_pass(left_high, right_high) + cross


def mul(left, right):
    return product(left, right, ((1,), (0,)))


def mul_nt(left, right):
    return product(left, right, ((1,), (1,)))


def mul_tn(left, right):
    return product(left.T, right, ((1,), (0,)))


def dot(left, right):
    return jnp.dot(left, right, precision=lax.Precision.HIGHEST, preferred_element_type=jnp.float32)


def ordered(first, a, b):
    return jnp.where(first, a, b), jnp.where(first, b, a)


class Group:
    def __init__(self, n_in, n_out):
        self.n_in, self.n = n_in, n_in * n_out
        self.place = [(k % n_in) * n_out + k // n_in for k in range(self.n)]

    def bit(self, b):
        return ((lax.axis_index("outer") * self.n_in + lax.axis_index("inner")) >> b) & 1 == 1

    def send(self, value, even, odd):
        pairs = [(self.place[k], self.place[k ^ (odd if k & 1 else even)]) for k in range(self.n)]
        return lax.ppermute(value, ("inner", "outer"), pairs)

    def swap(self, value, mask):
        return self.send(value, mask, mask)


def run(body, group, shapes, *operands, scratch=(), weight=1):
    order = operands[0].shape[-1]
    whole = pl.BlockSpec(memory_space=pltpu.VMEM)
    return pl.pallas_call(
        functools.partial(body, group),
        out_shape=[jax.ShapeDtypeStruct(shape, jnp.float32) for shape in shapes],
        in_specs=[whole] * len(operands),
        out_specs=[whole] * len(shapes),
        scratch_shapes=[pltpu.VMEM(shape, jnp.float32) for shape in scratch],
        compiler_params=pltpu.CompilerParams(vmem_limit_bytes=16 * 2**20),
        cost_estimate=pl.CostEstimate(flops=6 * weight * order**3, bytes_accessed=0, transcendentals=0),
    )(*operands)


def when(flag, then, other):
    pl.when(flag)(then)
    pl.when(jnp.logical_not(flag))(other)


def in_order(flag, out, a, b):
    def first():
        out[...] = mul(a[...], b[...])

    def last():
        out[...] = mul(b[...], a[...])

    when(flag, first, last)


def chip_kernel(group, mine, other, chip):
    in_order(group.bit(0), chip, mine, other)


def pair_kernel(group, chip, close, wide, pair, sent):
    def first():
        in_order(group.bit(1), pair, chip, close)
        sent[...] = wide[...]

    def second():
        in_order(group.bit(1), pair, close, wide)
        sent[...] = pair[...]

    when(group.bit(0), second, first)


def four_kernel(group, pair, given, to_d, to_y, to_x):
    def first():
        in_order(group.bit(2), to_d, pair, given)
        to_y[...] = to_d[...]
        to_x[...] = pair[...]

    def second():
        for out in (to_d, to_y, to_x):
            out[...] = given[...]

    when(group.bit(0), second, first)


def own_kernel(group, mine, other, chip, close, pair, given, by_x, w, after, wp, before, far):
    @pl.when(jnp.logical_not(group.bit(0)))
    def _():
        far[...] = given[...]

        def late():
            before[...] = mul(mine[...], close[...])
            after[...] = other[...]

        def early():
            before[...] = mine[...]
            after[...] = mul(close[...], other[...])

        when(group.bit(1), late, early)

    @pl.when(group.bit(0))
    def _():
        far[...] = pair[...]

        def late():
            before[...] = by_x[...]
            row = lax.broadcasted_iota(jnp.int32, after.shape, 0)
            column = lax.broadcasted_iota(jnp.int32, after.shape, 1)
            after[...] = jnp.where(row == column, 1.0, 0.0)

        def early():
            before[...] = chip[...]
            after[...] = mul_nt(by_x[...], chip[...])

        when(group.bit(1), late, early)

    def late():
        before[...] = mul(before[...], far[...])

    def early():
        after[...] = mul(far[...], after[...])

    when(group.bit(2), late, early)
    wp[...] = mul(w[...], before[...])


def near_kernel(group, wide, by_x, by_y, both):
    def first():
        in_order(group.bit(1), both.at[0], wide, by_x)

    def second():
        both[0] = wide[...]

    when(group.bit(0), second, first)
    both[1] = by_y[...]


def far_kernel(group, by_y, by_d, far):
    def first():
        far[...] = by_d[...]

    def second():
        in_order(group.bit(1), far, by_y, by_d)

    when(group.bit(0), second, first)


def held_kernel(group, both, far, held):
    def first():
        held[...] = far[...]

    def second():
        in_order(group.bit(2), held, both.at[0], far)

    when(group.bit(0), second, first)


def sides_kernel(group, after, wp, by_y, both, held, a, b, one):
    second, odd, upper = group.bit(0), group.bit(3), group.bit(4)
    one[...] = jnp.where(second, both[1], by_y[...])

    @pl.when(jnp.logical_not(odd))
    def _():
        a[...] = mul(one[...], after[...]).T

    @pl.when(jnp.logical_not(upper))
    def _():
        def later():
            a[...] = after[...].T
            b[...] = mul(wp[...], one[...])

        def first():
            b[...] = wp[...]

        when(odd, later, first)

        def left():
            a[...] = mul_nt(a[...], held[...])

        def right():
            b[...] = mul_tn(held[...], b[...])

        when(odd == second, left, right)

    @pl.when(upper)
    def _():
        def later():
            a[...] = mul(mul_tn(after[...], wp[...]), one[...])

        def first():
            a[...] = mul(a[...], wp[...])

        when(odd, later, first)

        def left():
            a[...] = mul(a[...], held[...])

        def right():
            b[...] = held[...]

        when(odd != second, left, right)


def result_kernel(group, a, come, b, result):
    upper, whole = group.bit(4), group.bit(4) & (group.bit(3) != group.bit(0))

    @pl.when(jnp.logical_not(upper))
    def _():
        result[...] = mul(mul_nt(a[...], come[...]), b[...])

    @pl.when(whole)
    def _():
        result[...] = mul(a[...], come[...])

    @pl.when(upper & jnp.logical_not(whole))
    def _():
        result[...] = mul(mul(a[...], come[...]), b[...])


def join(group, b, by, wp, after):
    flag = group.bit(b)
    new = dot(jnp.where(flag, wp, by), jnp.where(flag, by, after))
    return jnp.where(flag, new, wp), jnp.where(flag, after, new)


def pairwise(group, bits, total, wp, after):
    for b in bits:
        by = group.swap(total, 1 << b)
        wp, after = join(group, b, by, wp, after)
        total = dot(*ordered(group.bit(b), total, by))
    return dot(after.T, wp)


def body(n_in, n_out, slices, weight):
    group = Group(n_in, n_out)
    mine, w = slices[0, 0], weight[0, 0]
    square = mine.shape
    bits = group.n.bit_length() - 1
    if bits < 5:
        return pairwise(group, range(bits), mine, dot(w, mine), jnp.eye(square[0], dtype=jnp.float32))[None, None]
    other = group.swap(mine, 1)
    mine = lax.optimization_barrier(jnp.where(lax.axis_index("inner") < n_in, mine, 0.0))
    (chip,) = run(chip_kernel, group, [square], mine, other)
    wide = group.send(chip, 24, 6)
    close = group.send(chip, 2, 4)
    pair, sent = run(pair_kernel, group, [square] * 2, chip, close, wide)
    given = group.swap(sent, 1)
    to_d, to_y, to_x = run(four_kernel, group, [square] * 3, pair, given)
    by_d, by_x, by_y = group.send(to_d, 16, 6), group.send(to_x, 1, 3), group.send(to_y, 8, 4)
    after, wp = run(
        own_kernel, group, [square] * 2, mine, other, chip, close, pair, given, by_x, w, scratch=[square] * 2, weight=3
    )
    by_x, by_y, after, wp = lax.optimization_barrier((by_x, by_y, after, wp))
    (both,) = run(near_kernel, group, [(2, *square)], wide, by_x, by_y)
    both = group.swap(both, 1)
    (far,) = run(far_kernel, group, [square], by_y, by_d, weight=FAR)
    (held,) = run(held_kernel, group, [square], both, far)
    come = group.swap(held, 1)
    if bits > 5:
        second = group.bit(0)
        one = jnp.where(second, both[1], by_y)
        two, three = jnp.where(second, come, held), jnp.where(second, held, come)
        four = jnp.where(second, group.swap(to_d, 1), to_d)
        eight = dot(*ordered(group.bit(3), four, one))
        others = dot(*ordered(group.bit(3), two, three))
        wp, after = join(group, 3, one, wp, after)
        wp, after = join(group, 4, others, wp, after)
        total = dot(*ordered(group.bit(4), eight, others))
        return pairwise(group, range(5, bits), total, wp, after)[None, None]
    a, b = run(sides_kernel, group, [square] * 2, after, wp, by_y, both, held, scratch=[square], weight=3)
    (result,) = run(result_kernel, group, [square], a, come, b, weight=2)
    return result[None, None]


def solution(mesh):
    spec = P("outer", "inner", None, None)
    n_in, n_out = mesh.shape["inner"], mesh.shape["outer"]

    def gradient(slices, weight):
        return body(n_in, n_out, slices, weight)

    return jax.shard_map(gradient, mesh=mesh, in_specs=(spec, spec), out_specs=spec, check_vma=False)
```

time: 127 us -> 30.7 us (0.24)
  waiting for transfers between devices: 71 us -> 13.3 us
  matrix products: 39.9 us -> 0 us
  between operations: 13.5 us -> 0.08 us
  starting transfers between devices: 0.04 us -> 12.1 us
  Pallas kernels: 0 us -> 4.13 us
    all_gather x2 -> x0, waiting for transfers between devices: 70.3 us -> none  [carried_in(): everything = lax.all_gather(value, axis)]
    dot_general x31 -> x0, matrix products: 39.9 us -> none  [matmul(): jnp.dot(left, right, precision=lax.Precision.HIGHEST, preferred_element_t...]
    ppermute x0 -> x9, waiting for transfers between devices: none -> 13.3 us  [send(): return lax.ppermute(value, ('inner', 'outer'), pairs)]
    ppermute x0 -> x9, starting transfers between devices: none -> 12.1 us  [send(): return lax.ppermute(value, ('inner', 'outer'), pairs)]
    pallas_call x0 -> x9, Pallas kernels: none -> 4.13 us  [run(): pl.pallas_call(functools.partial(body, group), out_shape=[jax.ShapeDtypeS...]
  transfers between devices with their start and end apart: 2 -> 9, of which waited for: 2 -> 9; matrix products, arithmetic and copies ran while one was open for 0% -> 3% of each run, Pallas kernels for 0% -> 6%
where the time goes in v2:
time: 30.7 us; the launch traced here: 30.6 us
  waiting for transfers between devices  13.3 us (43%)
  starting transfers between devices  12.1 us (39%)
  Pallas kernels  4.13 us (13%)
  other arithmetic  0.97 us (3%)
    ppermute x9, waiting for transfers between devices, send(): return lax.ppermute(value, ('inner', 'outer'), pairs)  13.3 us
    ppermute x9, starting transfers between devices, send(): return lax.ppermute(value, ('inner', 'outer'), pairs)  12.1 us
    pallas_call x9, Pallas kernels, run(): pl.pallas_call(functools.partial(body, group), out_shape=[jax.ShapeDtypeS...  4.13 us
    select_n x1, other arithmetic, body(): jnp.where(lax.axis_index('inner') < n_in, mine, 0.0)  0.97 us
  transfers between devices with their start and end apart: 9, of which 9 were waited for; matrix products, arithmetic and copies ran while one was open for 3% of the time, Pallas kernels for 6%

profile of v2, /device:TPU:0, one launch (start us, length us, event | category | flops | bytes accessed | tf_op | source)
XLA Modules:
  0.0 30.6 jit_solution(13857874191854692040)
XLA Ops:
  0.0 0.5 %collective-permute-start = (f32[256,256]{1,0:T(8,128)}, f32[256,256]{1,0:T(8,128)S(1)}, u32[]{:S(2)}, u32[]{:S(2)}) collective-permute-start(f32[256,256]{1,0:T(8,128)} %bitcast.5), channel_id=1, source_target_pairs={{0,8},{8,0},{16,24},{24,16},{1,9},{9,1},{17,25},{25,17},{2,10},{10... | collective-permute-start | bytes 786440 | tf_op jit(solution)/shard_map/ppermute | solution.py:58
  0.5 1.0 %broadcast_select_fusion.mine = f32[256,256]{1,0:T(8,128)S(1)} fusion(pred[]{:T(512)S(6)} %lt.3, f32[1,1,256,256]{3,2,1,0:T(8,128)} %param.2), kind=kLoop, calls=%fused_computation | loop fusion | flops 65536 | bytes 524289 | tf_op jit(solution)/shard_map/jit(_where)/select_n | solution.py:278
  1.4 0.4 %collective-permute-done.other = f32[256,256]{1,0:T(8,128)S(1)} collective-permute-done((f32[256,256]{1,0:T(8,128)}, f32[256,256]{1,0:T(8,128)S(1)}, u32[]{:S(2)}, u32[]{:S(2)}) %collective-permute-start) | collective-permute-done | bytes 262176 | tf_op jit(solution)/shard_map/ppermute | solution.py:58
  1.8 0.3 shard_map.28.chip
  2.1 5.0 %collective-permute-start.2 = (f32[256,256]{1,0:T(8,128)S(1)}, f32[256,256]{1,0:T(8,128)S(1)}, u32[]{:S(2)}, u32[]{:S(2)}) collective-permute-start(f32[256,256]{1,0:T(8,128)S(1)} %shard_map.28.chip), channel_id=1, source_target_pairs={{0,6},{8,25},{16,22},{24,9},{1,7},{9,24},{17,23},{25,8},{2,4},{10,... | collective-permute-start | bytes 786440 | tf_op jit(solution)/shard_map/ppermute | solution.py:58
  7.1 1.5 %collective-permute-start.1 = (f32[256,256]{1,0:T(8,128)S(1)}, f32[256,256]{1,0:T(8,128)S(1)}, u32[]{:S(2)}, u32[]{:S(2)}) collective-permute-start(f32[256,256]{1,0:T(8,128)S(1)} %shard_map.28.chip), channel_id=1, source_target_pairs={{0,16},{8,9},{16,0},{24,25},{1,17},{9,8},{17,1},{25,24},{2,18},{10... | collective-permute-start | bytes 786440 | tf_op jit(solution)/shard_map/ppermute | solution.py:58
  8.6 3.0 %collective-permute-done.2.wide = f32[256,256]{1,0:T(8,128)S(1)} collective-permute-done((f32[256,256]{1,0:T(8,128)S(1)}, f32[256,256]{1,0:T(8,128)S(1)}, u32[]{:S(2)}, u32[]{:S(2)}) %collective-permute-start.2) | collective-permute-done | bytes 262176 | tf_op jit(solution)/shard_map/ppermute | solution.py:58
  11.6 1.9 %collective-permute-done.1.close = f32[256,256]{1,0:T(8,128)S(1)} collective-permute-done((f32[256,256]{1,0:T(8,128)S(1)}, f32[256,256]{1,0:T(8,128)S(1)}, u32[]{:S(2)}, u32[]{:S(2)}) %collective-permute-start.1) | collective-permute-done | bytes 262176 | tf_op jit(solution)/shard_map/ppermute | solution.py:58
  13.5 0.3 shard_map.29
  13.9 1.5 %collective-permute-done.3.given = f32[256,256]{1,0:T(8,128)S(1)} collective-permute-done((f32[256,256]{1,0:T(8,128)S(1)}, f32[256,256]{1,0:T(8,128)S(1)}, u32[]{:S(2)}, u32[]{:S(2)}) %collective-permute-start.3) | collective-permute-done | bytes 262176 | tf_op jit(solution)/shard_map/ppermute | solution.py:58
  15.4 0.3 %shard_map.30 = (f32[256,256]{1,0:T(8,128)S(1)}, f32[256,256]{1,0:T(8,128)S(1)}, f32[256,256]{1,0:T(8,128)S(1)}) custom-call(f32[256,256]{1,0:T(8,128)S(1)} %get-tuple-element.18.pair, f32[256,256]{1,0:T(8,128)S(1)} %collective-permute-done.3.given), custom_call_target="tpu_custom_call" | custom-call | flops 100663296 | tf_op jit(solution)/shard_map/pallas_call | solution.py:67
  15.8 1.0 %collective-permute-start.5 = (f32[256,256]{1,0:T(8,128)S(1)}, f32[256,256]{1,0:T(8,128)S(1)}, u32[]{:S(2)}, u32[]{:S(2)}) collective-permute-start(f32[256,256]{1,0:T(8,128)S(1)} %get-tuple-element.21), channel_id=1, source_target_pairs={{0,2},{8,9},{16,18},{24,25},{1,3},{9,8},{17,19},{25,24},{2,0},{10,... | collective-permute-start | bytes 786440 | tf_op jit(solution)/shard_map/ppermute | solution.py:58
  16.8 2.5 %collective-permute-start.7 = (f32[256,256]{1,0:T(8,128)S(1)}, f32[256,256]{1,0:T(8,128)S(1)}, u32[]{:S(2)}, u32[]{:S(2)}) collective-permute-start(f32[256,256]{1,0:T(8,128)S(1)} %get-tuple-element.28), channel_id=1, source_target_pairs={{0,4},{8,25},{16,20},{24,9},{1,5},{9,24},{17,21},{25,8},{2,6},{10,... | collective-permute-start | bytes 786440 | tf_op jit(solution)/shard_map/ppermute | solution.py:58
  19.3 2.3 %collective-permute-done.4.by_x = f32[256,256]{1,0:T(8,128)S(1)} collective-permute-done((f32[256,256]{1,0:T(8,128)S(1)}, f32[256,256]{1,0:T(8,128)S(1)}, u32[]{:S(2)}, u32[]{:S(2)}) %collective-permute-start.4) | collective-permute-done | bytes 262176 | tf_op jit(solution)/shard_map/ppermute | solution.py:58
  21.6 0.9 %shard_map.31 = (f32[256,256]{1,0:T(8,128)S(1)}, f32[256,256]{1,0:T(8,128)S(1)}) custom-call(f32[256,256]{1,0:T(8,128)S(1)} %broadcast_select_fusion.mine, f32[256,256]{1,0:T(8,128)S(1)} %collective-permute-done.other, f32[256,256]{1,0:T(8,128)S(1)} %shard_map.28.chip, f32[256,256]{1,0:T(8,128)S(1)} %collective-permute-done.1.close, ...), custom_call_target="tpu_custom_call" | custom-call | flops 301989888 | tf_op jit(solution)/shard_map/pallas_call | solution.py:67
  22.5 2.2 %collective-permute-done.5.by_y = f32[256,256]{1,0:T(8,128)S(1)} collective-permute-done((f32[256,256]{1,0:T(8,128)S(1)}, f32[256,256]{1,0:T(8,128)S(1)}, u32[]{:S(2)}, u32[]{:S(2)}) %collective-permute-start.5) | collective-permute-done | bytes 262176 | tf_op jit(solution)/shard_map/ppermute | solution.py:58
  24.7 0.3 shard_map.32
  25.0 0.9 %collective-permute-start.6 = (f32[2,256,256]{2,1,0:T(8,128)S(1)}, f32[2,256,256]{2,1,0:T(8,128)S(1)}, u32[]{:S(2)}, u32[]{:S(2)}) collective-permute-start(f32[2,256,256]{2,1,0:T(8,128)S(1)} %shard_map.32), channel_id=1, source_target_pairs={{0,8},{8,0},{16,24},{24,16},{1,9},{9,1},{17,25},{25,17},{2,10},{10... | collective-permute-start | bytes 1572872 | tf_op jit(solution)/shard_map/ppermute | solution.py:58
  25.8 1.1 %collective-permute-done.7.by_d = f32[256,256]{1,0:T(8,128)S(1)} collective-permute-done((f32[256,256]{1,0:T(8,128)S(1)}, f32[256,256]{1,0:T(8,128)S(1)}, u32[]{:S(2)}, u32[]{:S(2)}) %collective-permute-start.7) | collective-permute-done | bytes 262176 | tf_op jit(solution)/shard_map/ppermute | solution.py:58
  26.9 0.4 %collective-permute-done.6.both = f32[2,256,256]{2,1,0:T(8,128)S(1)} collective-permute-done((f32[2,256,256]{2,1,0:T(8,128)S(1)}, f32[2,256,256]{2,1,0:T(8,128)S(1)}, u32[]{:S(2)}, u32[]{:S(2)}) %collective-permute-start.6) | collective-permute-done | bytes 524320 | tf_op jit(solution)/shard_map/ppermute | solution.py:58
  27.4 0.7 %collective-permute-start.8 = (f32[256,256]{1,0:T(8,128)S(1)}, f32[256,256]{1,0:T(8,128)S(1)}, u32[]{:S(2)}, u32[]{:S(2)}) collective-permute-start(f32[256,256]{1,0:T(8,128)S(1)} %shard_map.34.held), channel_id=1, source_target_pairs={{0,8},{8,0},{16,24},{24,16},{1,9},{9,1},{17,25},{25,17},{2,10},{10... | collective-permute-start | bytes 786440 | tf_op jit(solution)/shard_map/ppermute | solution.py:58
  28.1 0.7 %shard_map.35 = (f32[256,256]{1,0:T(8,128)S(1)}, f32[256,256]{1,0:T(8,128)S(1)}) custom-call(f32[256,256]{1,0:T(8,128)S(1)} %get-tuple-element.24.after, f32[256,256]{1,0:T(8,128)S(1)} %get-tuple-element.25.wp, f32[256,256]{1,0:T(8,128)S(1)} %collective-permute-done.5.by_y, f32[2,256,256]{2,1,0:T(8,128)S(1)} %collective-permute-done.6.both, ...), custom_call_target="tpu_custom_call" | custom-call | flops 301989888 | tf_op jit(solution)/shard_map/pallas_call | solution.py:67
  28.8 0.4 %collective-permute-done.8.come = f32[256,256]{1,0:T(8,128)S(1)} collective-permute-done((f32[256,256]{1,0:T(8,128)S(1)}, f32[256,256]{1,0:T(8,128)S(1)}, u32[]{:S(2)}, u32[]{:S(2)}) %collective-permute-start.8) | collective-permute-done | bytes 262176 | tf_op jit(solution)/shard_map/ppermute | solution.py:58
  29.2 1.3 %shard_map.36 = f32[256,256]{1,0:T(8,128)} custom-call(f32[256,256]{1,0:T(8,128)S(1)} %get-tuple-element.29.a, f32[256,256]{1,0:T(8,128)S(1)} %collective-permute-done.8.come, f32[256,256]{1,0:T(8,128)S(1)} %get-tuple-element.30.b), custom_call_target="tpu_custom_call" | custom-call | flops 201326592 | tf_op jit(solution)/shard_map/pallas_call | solution.py:67
  (6 shorter events, 0.2 us)
Async XLA Ops:
  0.0 1.8 %collective-permute-start = (f32[256,256]{1,0:T(8,128)}, f32[256,256]{1,0:T(8,128)S(1)}, u32[]{:S(2)}, u32[]{:S(2)}) collective-permute-start(f32[256,256]{1,0:T(8,128)} %bitcast.5), channel_id=1, source_target_pairs={{0,8},{8,0},{16,24},{24,16},{1,9},{9,1},{17,25},{25,17},{2,10},{10... | collective-permute-start | bytes 786440 | tf_op jit(solution)/shard_map/ppermute | solution.py:58
  2.1 9.5 %collective-permute-start.2 = (f32[256,256]{1,0:T(8,128)S(1)}, f32[256,256]{1,0:T(8,128)S(1)}, u32[]{:S(2)}, u32[]{:S(2)}) collective-permute-start(f32[256,256]{1,0:T(8,128)S(1)} %shard_map.28.chip), channel_id=1, source_target_pairs={{0,6},{8,25},{16,22},{24,9},{1,7},{9,24},{17,23},{25,8},{2,4},{10,... | collective-permute-start | bytes 786440 | tf_op jit(solution)/shard_map/ppermute | solution.py:58
  7.1 6.4 %collective-permute-start.1 = (f32[256,256]{1,0:T(8,128)S(1)}, f32[256,256]{1,0:T(8,128)S(1)}, u32[]{:S(2)}, u32[]{:S(2)}) collective-permute-start(f32[256,256]{1,0:T(8,128)S(1)} %shard_map.28.chip), channel_id=1, source_target_pairs={{0,16},{8,9},{16,0},{24,25},{1,17},{9,8},{17,1},{25,24},{2,18},{10... | collective-permute-start | bytes 786440 | tf_op jit(solution)/shard_map/ppermute | solution.py:58
  13.8 1.6 %collective-permute-start.3 = (f32[256,256]{1,0:T(8,128)S(1)}, f32[256,256]{1,0:T(8,128)S(1)}, u32[]{:S(2)}, u32[]{:S(2)}) collective-permute-start(f32[256,256]{1,0:T(8,128)S(1)} %get-tuple-element.19), channel_id=1, source_target_pairs={{0,8},{8,0},{16,24},{24,16},{1,9},{9,1},{17,25},{25,17},{2,10},{10... | collective-permute-start | bytes 786440 | tf_op jit(solution)/shard_map/ppermute | solution.py:58
  15.4 6.2 %copy-start = (f32[1,1,256,256]{3,2,1,0:T(8,128)S(1)}, f32[1,1,256,256]{3,2,1,0:T(8,128)}, u32[]{:S(2)}) copy-start(f32[1,1,256,256]{3,2,1,0:T(8,128)} %param.3) | copy-start | bytes 786436
  15.7 5.8 %collective-permute-start.4 = (f32[256,256]{1,0:T(8,128)S(1)}, f32[256,256]{1,0:T(8,128)S(1)}, u32[]{:S(2)}, u32[]{:S(2)}) collective-permute-start(f32[256,256]{1,0:T(8,128)S(1)} %get-tuple-element.20), channel_id=1, source_target_pairs={{0,8},{8,16},{16,24},{24,0},{1,9},{9,17},{17,25},{25,1},{2,10},{10... | collective-permute-start | bytes 786440 | tf_op jit(solution)/shard_map/ppermute | solution.py:58
  15.8 8.9 %collective-permute-start.5 = (f32[256,256]{1,0:T(8,128)S(1)}, f32[256,256]{1,0:T(8,128)S(1)}, u32[]{:S(2)}, u32[]{:S(2)}) collective-permute-start(f32[256,256]{1,0:T(8,128)S(1)} %get-tuple-element.21), channel_id=1, source_target_pairs={{0,2},{8,9},{16,18},{24,25},{1,3},{9,8},{17,19},{25,24},{2,0},{10,... | collective-permute-start | bytes 786440 | tf_op jit(solution)/shard_map/ppermute | solution.py:58
  16.8 10.1 %collective-permute-start.7 = (f32[256,256]{1,0:T(8,128)S(1)}, f32[256,256]{1,0:T(8,128)S(1)}, u32[]{:S(2)}, u32[]{:S(2)}) collective-permute-start(f32[256,256]{1,0:T(8,128)S(1)} %get-tuple-element.28), channel_id=1, source_target_pairs={{0,4},{8,25},{16,20},{24,9},{1,5},{9,24},{17,21},{25,8},{2,6},{10,... | collective-permute-start | bytes 786440 | tf_op jit(solution)/shard_map/ppermute | solution.py:58
  25.0 2.4 %collective-permute-start.6 = (f32[2,256,256]{2,1,0:T(8,128)S(1)}, f32[2,256,256]{2,1,0:T(8,128)S(1)}, u32[]{:S(2)}, u32[]{:S(2)}) collective-permute-start(f32[2,256,256]{2,1,0:T(8,128)S(1)} %shard_map.32), channel_id=1, source_target_pairs={{0,8},{8,0},{16,24},{24,16},{1,9},{9,1},{17,25},{25,17},{2,10},{10... | collective-permute-start | bytes 1572872 | tf_op jit(solution)/shard_map/ppermute | solution.py:58
  27.4 1.9 %collective-permute-start.8 = (f32[256,256]{1,0:T(8,128)S(1)}, f32[256,256]{1,0:T(8,128)S(1)}, u32[]{:S(2)}, u32[]{:S(2)}) collective-permute-start(f32[256,256]{1,0:T(8,128)S(1)} %shard_map.34.held), channel_id=1, source_target_pairs={{0,8},{8,0},{16,24},{24,16},{1,9},{9,1},{17,25},{25,17},{2,10},{10... | collective-permute-start | bytes 786440 | tf_op jit(solution)/shard_map/ppermute | solution.py:58

commit v3 on v2

--- a/solution.py
+++ b/solution.py
@@ -6,9 +6,6 @@
 from jax.experimental import pallas as pl
 from jax.experimental.pallas import tpu as pltpu
 from jax.sharding import PartitionSpec as P
-
-
-FAR = 200
 
 
 def halves(value):
@@ -106,17 +103,21 @@
     when(group.bit(0), second, first)
 
 
-def four_kernel(group, pair, given, to_d, to_y, to_x):
+def four_kernel(group, pair, given, four, to_y, to_x):
     def first():
-        in_order(group.bit(2), to_d, pair, given)
-        to_y[...] = to_d[...]
+        in_order(group.bit(2), four, pair, given)
         to_x[...] = pair[...]
 
     def second():
-        for out in (to_d, to_y, to_x):
-            out[...] = given[...]
+        four[...] = given[...]
+        to_x[...] = given[...]
 
     when(group.bit(0), second, first)
+    to_y[...] = four[...]
+
+
+def keep_kernel(group, value, kept):
+    kept[...] = value[...]
 
 
 def own_kernel(group, mine, other, chip, close, pair, given, by_x, w, after, wp, before, far):
@@ -160,97 +161,172 @@
     wp[...] = mul(w[...], before[...])
 
 
-def near_kernel(group, wide, by_x, by_y, both):
+def near_kernel(group, wide, by_x, near):
     def first():
-        in_order(group.bit(1), both.at[0], wide, by_x)
+        in_order(group.bit(1), near, wide, by_x)
 
     def second():
-        both[0] = wide[...]
+        near[...] = wide[...]
 
     when(group.bit(0), second, first)
-    both[1] = by_y[...]
-
-
-def far_kernel(group, by_y, by_d, far):
-    def first():
-        far[...] = by_d[...]
-
-    def second():
-        in_order(group.bit(1), far, by_y, by_d)
-
-    when(group.bit(0), second, first)
-
-
-def held_kernel(group, both, far, held):
-    def first():
-        held[...] = far[...]
-
-    def second():
-        in_order(group.bit(2), held, both.at[0], far)
-
-    when(group.bit(0), second, first)
-
-
-def sides_kernel(group, after, wp, by_y, both, held, a, b, one):
-    second, odd, upper = group.bit(0), group.bit(3), group.bit(4)
-    one[...] = jnp.where(second, both[1], by_y[...])
-
-    @pl.when(jnp.logical_not(odd))
-    def _():
-        a[...] = mul(one[...], after[...]).T
-
-    @pl.when(jnp.logical_not(upper))
-    def _():
-        def later():
-            a[...] = after[...].T
-            b[...] = mul(wp[...], one[...])
-
-        def first():
-            b[...] = wp[...]
-
-        when(odd, later, first)
-
-        def left():
-            a[...] = mul_nt(a[...], held[...])
-
-        def right():
-            b[...] = mul_tn(held[...], b[...])
-
-        when(odd == second, left, right)
-
-    @pl.when(upper)
-    def _():
-        def later():
-            a[...] = mul(mul_tn(after[...], wp[...]), one[...])
-
-        def first():
-            a[...] = mul(a[...], wp[...])
-
-        when(odd, later, first)
-
-        def left():
-            a[...] = mul(a[...], held[...])
-
-        def right():
-            b[...] = held[...]
-
-        when(odd != second, left, right)
-
-
-def result_kernel(group, a, come, b, result):
-    upper, whole = group.bit(4), group.bit(4) & (group.bit(3) != group.bit(0))
-
-    @pl.when(jnp.logical_not(upper))
-    def _():
-        result[...] = mul(mul_nt(a[...], come[...]), b[...])
-
-    @pl.when(whole)
-    def _():
-        result[...] = mul(a[...], come[...])
-
-    @pl.when(upper & jnp.logical_not(whole))
-    def _():
-        result[...] = mul(mul(a[...], come[...]), b[...])
+
+
+def sides_kernel(group, after, wp, near, their_near, by_d, by_y, a, b, three, held):
+    second, near_left, odd, upper = group.bit(0), group.bit(2), group.bit(3), group.bit(4)
+
+    def on_first():
+        two, one = by_d, by_y
+
+        @pl.when(jnp.logical_not(odd))
+        def _():
+            held[...] = mul(one[...], after[...])
+
+        def early():
+            def odd_four():
+                a[...] = mul(mul(mul_tn(after[...], wp[...]), one[...]), two[...])
+
+            def even_four():
+                a[...] = mul_tn(held[...], wp[...])
+                b[...] = two[...]
+
+            when(odd, odd_four, even_four)
+
+            def left():
+                a[...] = mul(a[...], near[...])
+
+            def right():
+                def odd_four():
+                    b[...] = near[...]
+
+                def even_four():
+                    b[...] = mul(near[...], two[...])
+
+                when(odd, odd_four, even_four)
+
+            when(near_left, left, right)
+
+        def late():
+            def odd_four():
+                a[...] = after[...].T
+                b[...] = mul_tn(two[...], mul(wp[...], one[...]))
+
+            def even_four():
+                a[...] = mul(two[...], held[...]).T
+                b[...] = wp[...]
+
+            when(odd, odd_four, even_four)
+
+            def right():
+                b[...] = mul_tn(near[...], b[...])
+
+            def left():
+                a[...] = mul_nt(a[...], near[...])
+
+            when(near_left, right, left)
+
+        when(upper, early, late)
+
+    def on_second():
+        in_order(group.bit(1), held, by_y, by_d)
+        in_order(near_left, three, their_near, held)
+
+        def early():
+            def odd_four():
+                a[...] = mul_tn(after[...], wp[...])
+                b[...] = three[...]
+
+            def even_four():
+                a[...] = after[...].T
+                b[...] = mul(wp[...], three[...])
+
+            when(odd, odd_four, even_four)
+
+        def late():
+            def odd_four():
+                a[...] = mul(three[...], after[...]).T
+                b[...] = wp[...]
+
+            def even_four():
+                a[...] = after[...].T
+                b[...] = mul_tn(three[...], wp[...])
+
+            when(odd, odd_four, even_four)
+
+        when(upper, early, late)
+
+    when(second, on_second, on_first)
+
+
+def closer_kernel(group, a, b, come, new_a, new_b):
+    second, x_bit, near_left, odd, upper = (group.bit(k) for k in range(5))
+    new_a[...] = a[...]
+    new_b[...] = b[...]
+
+    def on_first():
+        def early():
+            def right():
+                def alone():
+                    new_b[...] = come[...]
+
+                def beside():
+                    new_b[...] = mul(come[...], b[...])
+
+                when(odd & near_left, alone, beside)
+
+            def left():
+                new_a[...] = mul(a[...], come[...])
+
+            when(x_bit, right, left)
+
+        def late():
+            def left():
+                new_a[...] = mul_nt(a[...], come[...])
+
+            def right():
+                new_b[...] = mul_tn(come[...], b[...])
+
+            when(x_bit, left, right)
+
+        when(upper, early, late)
+
+    def on_second():
+        def early():
+            in_order(odd, new_b, come, b)
+
+        def late():
+            def odd_four():
+                new_a[...] = mul(mul_nt(a[...], come[...]), b[...])
+
+            def even_four():
+                new_b[...] = mul_tn(come[...], b[...])
+
+            when(odd, odd_four, even_four)
+
+        when(upper, early, late)
+
+    when(second, on_second, on_first)
+
+
+def result_kernel(group, a, b, come, result, mid):
+    second, x_bit, near_left, odd, upper = (group.bit(k) for k in range(5))
+    plain = jnp.where(second, odd, upper)
+    alone = odd & jnp.where(second, jnp.logical_not(upper), upper & near_left & jnp.logical_not(x_bit))
+
+    def as_is():
+        mid[...] = mul(a[...], come[...])
+
+    def transposed():
+        mid[...] = mul_nt(a[...], come[...])
+
+    when(plain, as_is, transposed)
+
+    def last():
+        result[...] = mid[...]
+
+    def one_more():
+        result[...] = mul(mid[...], b[...])
+
+    when(alone, last, one_more)
 
 
 def join(group, b, by, wp, after):
@@ -281,30 +357,34 @@
     close = group.send(chip, 2, 4)
     pair, sent = run(pair_kernel, group, [square] * 2, chip, close, wide)
     given = group.swap(sent, 1)
-    to_d, to_y, to_x = run(four_kernel, group, [square] * 3, pair, given)
-    by_d, by_x, by_y = group.send(to_d, 16, 6), group.send(to_x, 1, 3), group.send(to_y, 8, 4)
+    four, to_y, to_x = run(four_kernel, group, [square] * 3, pair, given)
+    by_x, by_d, by_y = group.send(to_x, 1, 3), group.send(four, 16, 6), group.send(to_y, 8, 4)
     after, wp = run(
         own_kernel, group, [square] * 2, mine, other, chip, close, pair, given, by_x, w, scratch=[square] * 2, weight=3
     )
-    by_x, by_y, after, wp = lax.optimization_barrier((by_x, by_y, after, wp))
-    (both,) = run(near_kernel, group, [(2, *square)], wide, by_x, by_y)
-    both = group.swap(both, 1)
-    (far,) = run(far_kernel, group, [square], by_y, by_d, weight=FAR)
-    (held,) = run(held_kernel, group, [square], both, far)
-    come = group.swap(held, 1)
+    by_x, after, wp = lax.optimization_barrier((by_x, after, wp))
+    (near,) = run(near_kernel, group, [square], wide, by_x)
+    their_near = group.swap(near, 1)
+    their_d = group.swap(by_d, 1)
+    by_y, by_d = lax.optimization_barrier((by_y, *run(keep_kernel, group, [square], by_d)))
+    their_y = group.swap(by_y, 1)
     if bits > 5:
         second = group.bit(0)
-        one = jnp.where(second, both[1], by_y)
-        two, three = jnp.where(second, come, held), jnp.where(second, held, come)
-        four = jnp.where(second, group.swap(to_d, 1), to_d)
+        one, two = jnp.where(second, their_y, by_y), jnp.where(second, their_d, by_d)
+        far = dot(*ordered(group.bit(1), jnp.where(second, by_y, their_y), jnp.where(second, by_d, their_d)))
+        three = dot(*ordered(group.bit(2), jnp.where(second, their_near, near), far))
+        four = jnp.where(second, group.swap(four, 1), four)
         eight = dot(*ordered(group.bit(3), four, one))
         others = dot(*ordered(group.bit(3), two, three))
         wp, after = join(group, 3, one, wp, after)
         wp, after = join(group, 4, others, wp, after)
         total = dot(*ordered(group.bit(4), eight, others))
         return pairwise(group, range(5, bits), total, wp, after)[None, None]
-    a, b = run(sides_kernel, group, [square] * 2, after, wp, by_y, both, held, scratch=[square], weight=3)
-    (result,) = run(result_kernel, group, [square], a, come, b, weight=2)
+    a, b = run(
+        sides_kernel, group, [square] * 2, after, wp, near, their_near, by_d, by_y, scratch=[square] * 2, weight=4
+    )
+    a, b = run(closer_kernel, group, [square] * 2, a, b, their_d)
+    (result,) = run(result_kernel, group, [square], a, b, their_y, scratch=[square], weight=2)
     return result[None, None]
 
 

time: 30.7 us -> 29.5 us (0.961)
  starting transfers between devices: 12.1 us -> 10.8 us
  Pallas kernels: 4.13 us -> 4.65 us
  waiting for transfers between devices: 13.3 us -> 12.9 us
    ppermute x9 -> x10, starting transfers between devices: 12.1 us -> 10.8 us  [send(): return lax.ppermute(value, ('inner', 'outer'), pairs)]
    pallas_call x9, Pallas kernels: 4.13 us -> 4.65 us  [run(): pl.pallas_call(functools.partial(body, group), out_shape=[jax.ShapeDtypeS...]
    ppermute x9 -> x10, waiting for transfers between devices: 13.3 us -> 12.9 us  [send(): return lax.ppermute(value, ('inner', 'outer'), pairs)]
  transfers between devices with their start and end apart: 9 -> 10, of which waited for: 9 -> 8; matrix products, arithmetic and copies ran while one was open for 3% -> 3% of each run, Pallas kernels for 6% -> 8%
where the time goes in v3:
time: 29.5 us; the launch traced here: 29.3 us
  waiting for transfers between devices  12.9 us (44%)
  starting transfers between devices  10.8 us (37%)
  Pallas kernels  4.65 us (16%)
  other arithmetic  0.97 us (3%)
    ppermute x10, waiting for transfers between devices, send(): return lax.ppermute(value, ('inner', 'outer'), pairs)  12.9 us
    ppermute x10, starting transfers between devices, send(): return lax.ppermute(value, ('inner', 'outer'), pairs)  10.8 us
    pallas_call x9, Pallas kernels, run(): pl.pallas_call(functools.partial(body, group), out_shape=[jax.ShapeDtypeS...  4.65 us
    select_n x1, other arithmetic, body(): jnp.where(lax.axis_index('inner') < n_in, mine, 0.0)  0.97 us
  transfers between devices with their start and end apart: 10, of which 8 were waited for; matrix products, arithmetic and copies ran while one was open for 3% of the time, Pallas kernels for 8%

profile of v3, /device:TPU:0, one launch (start us, length us, event | category | flops | bytes accessed | tf_op | source)
XLA Modules:
  0.0 29.3 jit_solution(9330293192403381029)
XLA Ops:
  0.0 0.5 %collective-permute-start = (f32[256,256]{1,0:T(8,128)}, f32[256,256]{1,0:T(8,128)S(1)}, u32[]{:S(2)}, u32[]{:S(2)}) collective-permute-start(f32[256,256]{1,0:T(8,128)} %bitcast.5), channel_id=1, source_target_pairs={{0,8},{8,0},{16,24},{24,16},{1,9},{9,1},{17,25},{25,17},{2,10},{10... | collective-permute-start | bytes 786440 | tf_op jit(solution)/shard_map/ppermute | solution.py:55
  0.5 1.0 %broadcast_select_fusion.mine = f32[256,256]{1,0:T(8,128)S(1)} fusion(pred[]{:T(512)S(6)} %lt.3, f32[1,1,256,256]{3,2,1,0:T(8,128)} %param.2), kind=kLoop, calls=%fused_computation | loop fusion | flops 65536 | bytes 524289 | tf_op jit(solution)/shard_map/jit(_where)/select_n | solution.py:354
  1.4 0.4 %collective-permute-done.other = f32[256,256]{1,0:T(8,128)S(1)} collective-permute-done((f32[256,256]{1,0:T(8,128)}, f32[256,256]{1,0:T(8,128)S(1)}, u32[]{:S(2)}, u32[]{:S(2)}) %collective-permute-start) | collective-permute-done | bytes 262176 | tf_op jit(solution)/shard_map/ppermute | solution.py:55
  1.8 0.3 shard_map.28.chip
  2.1 5.0 %collective-permute-start.2 = (f32[256,256]{1,0:T(8,128)S(1)}, f32[256,256]{1,0:T(8,128)S(1)}, u32[]{:S(2)}, u32[]{:S(2)}) collective-permute-start(f32[256,256]{1,0:T(8,128)S(1)} %shard_map.28.chip), channel_id=1, source_target_pairs={{0,6},{8,25},{16,22},{24,9},{1,7},{9,24},{17,23},{25,8},{2,4},{10,... | collective-permute-start | bytes 786440 | tf_op jit(solution)/shard_map/ppermute | solution.py:55
  7.1 1.5 %collective-permute-start.1 = (f32[256,256]{1,0:T(8,128)S(1)}, f32[256,256]{1,0:T(8,128)S(1)}, u32[]{:S(2)}, u32[]{:S(2)}) collective-permute-start(f32[256,256]{1,0:T(8,128)S(1)} %shard_map.28.chip), channel_id=1, source_target_pairs={{0,16},{8,9},{16,0},{24,25},{1,17},{9,8},{17,1},{25,24},{2,18},{10... | collective-permute-start | bytes 786440 | tf_op jit(solution)/shard_map/ppermute | solution.py:55
  8.6 3.0 %collective-permute-done.2.wide = f32[256,256]{1,0:T(8,128)S(1)} collective-permute-done((f32[256,256]{1,0:T(8,128)S(1)}, f32[256,256]{1,0:T(8,128)S(1)}, u32[]{:S(2)}, u32[]{:S(2)}) %collective-permute-start.2) | collective-permute-done | bytes 262176 | tf_op jit(solution)/shard_map/ppermute | solution.py:55
  11.6 1.9 %collective-permute-done.1.close = f32[256,256]{1,0:T(8,128)S(1)} collective-permute-done((f32[256,256]{1,0:T(8,128)S(1)}, f32[256,256]{1,0:T(8,128)S(1)}, u32[]{:S(2)}, u32[]{:S(2)}) %collective-permute-start.1) | collective-permute-done | bytes 262176 | tf_op jit(solution)/shard_map/ppermute | solution.py:55
  13.5 0.3 shard_map.29
  13.8 0.1 collective-permute-start.3
  13.9 1.5 %collective-permute-done.3.given = f32[256,256]{1,0:T(8,128)S(1)} collective-permute-done((f32[256,256]{1,0:T(8,128)S(1)}, f32[256,256]{1,0:T(8,128)S(1)}, u32[]{:S(2)}, u32[]{:S(2)}) %collective-permute-start.3) | collective-permute-done | bytes 262176 | tf_op jit(solution)/shard_map/ppermute | solution.py:55
  15.4 0.3 %shard_map.30 = (f32[256,256]{1,0:T(8,128)S(1)}, f32[256,256]{1,0:T(8,128)S(1)}, f32[256,256]{1,0:T(8,128)S(1)}) custom-call(f32[256,256]{1,0:T(8,128)S(1)} %get-tuple-element.21.pair, f32[256,256]{1,0:T(8,128)S(1)} %collective-permute-done.3.given), custom_call_target="tpu_custom_call" | custom-call | flops 100663296 | tf_op jit(solution)/shard_map/pallas_call | solution.py:64
  15.8 2.0 %collective-permute-start.7 = (f32[256,256]{1,0:T(8,128)S(1)}, f32[256,256]{1,0:T(8,128)S(1)}, u32[]{:S(2)}, u32[]{:S(2)}) collective-permute-start(f32[256,256]{1,0:T(8,128)S(1)} %get-tuple-element.30), channel_id=1, source_target_pairs={{0,4},{8,25},{16,20},{24,9},{1,5},{9,24},{17,21},{25,8},{2,6},{10,... | collective-permute-start | bytes 786440 | tf_op jit(solution)/shard_map/ppermute | solution.py:55
  17.8 1.5 %collective-permute-start.6 = (f32[256,256]{1,0:T(8,128)S(1)}, f32[256,256]{1,0:T(8,128)S(1)}, u32[]{:S(2)}, u32[]{:S(2)}) collective-permute-start(f32[256,256]{1,0:T(8,128)S(1)} %get-tuple-element.29), channel_id=1, source_target_pairs={{0,2},{8,9},{16,18},{24,25},{1,3},{9,8},{17,19},{25,24},{2,0},{10,... | collective-permute-start | bytes 786440 | tf_op jit(solution)/shard_map/ppermute | solution.py:55
  19.3 2.3 %collective-permute-done.4.by_x = f32[256,256]{1,0:T(8,128)S(1)} collective-permute-done((f32[256,256]{1,0:T(8,128)S(1)}, f32[256,256]{1,0:T(8,128)S(1)}, u32[]{:S(2)}, u32[]{:S(2)}) %collective-permute-start.4) | collective-permute-done | bytes 262176 | tf_op jit(solution)/shard_map/ppermute | solution.py:55
  21.6 0.9 %shard_map.31 = (f32[256,256]{1,0:T(8,128)S(1)}, f32[256,256]{1,0:T(8,128)S(1)}) custom-call(f32[256,256]{1,0:T(8,128)S(1)} %broadcast_select_fusion.mine, f32[256,256]{1,0:T(8,128)S(1)} %collective-permute-done.other, f32[256,256]{1,0:T(8,128)S(1)} %shard_map.28.chip, f32[256,256]{1,0:T(8,128)S(1)} %collective-permute-done.1.close, ...), custom_call_target="tpu_custom_call" | custom-call | flops 301989888 | tf_op jit(solution)/shard_map/pallas_call | solution.py:64
  22.5 0.3 %shard_map.32.near = f32[256,256]{1,0:T(8,128)S(1)} custom-call(f32[256,256]{1,0:T(8,128)S(1)} %collective-permute-done.2.wide, f32[256,256]{1,0:T(8,128)S(1)} %collective-permute-done.4.by_x), custom_call_target="tpu_custom_call" | custom-call | flops 100663296 | tf_op jit(solution)/shard_map/pallas_call | solution.py:64
  22.9 3.2 %collective-permute-done.7.value = f32[256,256]{1,0:T(8,128)S(1)} collective-permute-done((f32[256,256]{1,0:T(8,128)S(1)}, f32[256,256]{1,0:T(8,128)S(1)}, u32[]{:S(2)}, u32[]{:S(2)}) %collective-permute-start.7) | collective-permute-done | bytes 262176 | tf_op jit(solution)/shard_map/ppermute | solution.py:55
  26.1 0.4 %collective-permute-done.6.by_y = f32[256,256]{1,0:T(8,128)S(1)} collective-permute-done((f32[256,256]{1,0:T(8,128)S(1)}, f32[256,256]{1,0:T(8,128)S(1)}, u32[]{:S(2)}, u32[]{:S(2)}) %collective-permute-start.6) | collective-permute-done | bytes 262176 | tf_op jit(solution)/shard_map/ppermute | solution.py:55
  26.5 0.1 collective-permute-start.9
  26.7 0.9 %shard_map.34 = (f32[256,256]{1,0:T(8,128)S(1)}, f32[256,256]{1,0:T(8,128)S(1)}) custom-call(f32[256,256]{1,0:T(8,128)S(1)} %get-tuple-element.26.after, f32[256,256]{1,0:T(8,128)S(1)} %get-tuple-element.27.wp, f32[256,256]{1,0:T(8,128)S(1)} %shard_map.32.near, f32[256,256]{1,0:T(8,128)S(1)} %collective-permute-done.5.their_near, ...), custom_call_target="tpu_custom_call" | custom-call | flops 402653184 | tf_op jit(solution)/shard_map/pallas_call | solution.py:64
  27.6 0.4 %shard_map.35 = (f32[256,256]{1,0:T(8,128)S(1)}, f32[256,256]{1,0:T(8,128)S(1)}) custom-call(f32[256,256]{1,0:T(8,128)S(1)} %get-tuple-element.33.a, f32[256,256]{1,0:T(8,128)S(1)} %get-tuple-element.34.b, f32[256,256]{1,0:T(8,128)S(1)} %collective-permute-done.8.come), custom_call_target="tpu_custom_call" | custom-call | flops 100663296 | tf_op jit(solution)/shard_map/pallas_call | solution.py:64
  28.0 0.1 collective-permute-done.9.come
  28.1 1.3 %shard_map.36 = f32[256,256]{1,0:T(8,128)} custom-call(f32[256,256]{1,0:T(8,128)S(1)} %get-tuple-element.35.a, f32[256,256]{1,0:T(8,128)S(1)} %get-tuple-element.36.b, f32[256,256]{1,0:T(8,128)S(1)} %collective-permute-done.9.come), custom_call_target="tpu_custom_call" | custom-call | flops 201326592 | tf_op jit(solution)/shard_map/pallas_call | solution.py:64
  (8 shorter events, 0.2 us)
Async XLA Ops:
  0.0 1.8 %collective-permute-start = (f32[256,256]{1,0:T(8,128)}, f32[256,256]{1,0:T(8,128)S(1)}, u32[]{:S(2)}, u32[]{:S(2)}) collective-permute-start(f32[256,256]{1,0:T(8,128)} %bitcast.5), channel_id=1, source_target_pairs={{0,8},{8,0},{16,24},{24,16},{1,9},{9,1},{17,25},{25,17},{2,10},{10... | collective-permute-start | bytes 786440 | tf_op jit(solution)/shard_map/ppermute | solution.py:55
  2.1 9.5 %collective-permute-start.2 = (f32[256,256]{1,0:T(8,128)S(1)}, f32[256,256]{1,0:T(8,128)S(1)}, u32[]{:S(2)}, u32[]{:S(2)}) collective-permute-start(f32[256,256]{1,0:T(8,128)S(1)} %shard_map.28.chip), channel_id=1, source_target_pairs={{0,6},{8,25},{16,22},{24,9},{1,7},{9,24},{17,23},{25,8},{2,4},{10,... | collective-permute-start | bytes 786440 | tf_op jit(solution)/shard_map/ppermute | solution.py:55
  7.1 6.4 %collective-permute-start.1 = (f32[256,256]{1,0:T(8,128)S(1)}, f32[256,256]{1,0:T(8,128)S(1)}, u32[]{:S(2)}, u32[]{:S(2)}) collective-permute-start(f32[256,256]{1,0:T(8,128)S(1)} %shard_map.28.chip), channel_id=1, source_target_pairs={{0,16},{8,9},{16,0},{24,25},{1,17},{9,8},{17,1},{25,24},{2,18},{10... | collective-permute-start | bytes 786440 | tf_op jit(solution)/shard_map/ppermute | solution.py:55
  13.8 1.6 %collective-permute-start.3 = (f32[256,256]{1,0:T(8,128)S(1)}, f32[256,256]{1,0:T(8,128)S(1)}, u32[]{:S(2)}, u32[]{:S(2)}) collective-permute-start(f32[256,256]{1,0:T(8,128)S(1)} %get-tuple-element.22), channel_id=1, source_target_pairs={{0,8},{8,0},{16,24},{24,16},{1,9},{9,1},{17,25},{25,17},{2,10},{10... | collective-permute-start | bytes 786440 | tf_op jit(solution)/shard_map/ppermute | solution.py:55
  15.4 6.2 %copy-start = (f32[1,1,256,256]{3,2,1,0:T(8,128)S(1)}, f32[1,1,256,256]{3,2,1,0:T(8,128)}, u32[]{:S(2)}) copy-start(f32[1,1,256,256]{3,2,1,0:T(8,128)} %param.3) | copy-start | bytes 786436
  15.7 5.8 %collective-permute-start.4 = (f32[256,256]{1,0:T(8,128)S(1)}, f32[256,256]{1,0:T(8,128)S(1)}, u32[]{:S(2)}, u32[]{:S(2)}) collective-permute-start(f32[256,256]{1,0:T(8,128)S(1)} %get-tuple-element.23), channel_id=1, source_target_pairs={{0,8},{8,16},{16,24},{24,0},{1,9},{9,17},{17,25},{25,1},{2,10},{10... | collective-permute-start | bytes 786440 | tf_op jit(solution)/shard_map/ppermute | solution.py:55
  15.8 10.2 %collective-permute-start.7 = (f32[256,256]{1,0:T(8,128)S(1)}, f32[256,256]{1,0:T(8,128)S(1)}, u32[]{:S(2)}, u32[]{:S(2)}) collective-permute-start(f32[256,256]{1,0:T(8,128)S(1)} %get-tuple-element.30), channel_id=1, source_target_pairs={{0,4},{8,25},{16,20},{24,9},{1,5},{9,24},{17,21},{25,8},{2,6},{10,... | collective-permute-start | bytes 786440 | tf_op jit(solution)/shard_map/ppermute | solution.py:55
  17.8 8.7 %collective-permute-start.6 = (f32[256,256]{1,0:T(8,128)S(1)}, f32[256,256]{1,0:T(8,128)S(1)}, u32[]{:S(2)}, u32[]{:S(2)}) collective-permute-start(f32[256,256]{1,0:T(8,128)S(1)} %get-tuple-element.29), channel_id=1, source_target_pairs={{0,2},{8,9},{16,18},{24,25},{1,3},{9,8},{17,19},{25,24},{2,0},{10,... | collective-permute-start | bytes 786440 | tf_op jit(solution)/shard_map/ppermute | solution.py:55
  22.8 3.9 %collective-permute-start.5 = (f32[256,256]{1,0:T(8,128)S(1)}, f32[256,256]{1,0:T(8,128)S(1)}, u32[]{:S(2)}, u32[]{:S(2)}) collective-permute-start(f32[256,256]{1,0:T(8,128)S(1)} %shard_map.32.near), channel_id=1, source_target_pairs={{0,8},{8,0},{16,24},{24,16},{1,9},{9,1},{17,25},{25,17},{2,10},{10... | collective-permute-start | bytes 786440 | tf_op jit(solution)/shard_map/ppermute | solution.py:55
  26.1 1.6 %collective-permute-start.8 = (f32[256,256]{1,0:T(8,128)S(1)}, f32[256,256]{1,0:T(8,128)S(1)}, u32[]{:S(2)}, u32[]{:S(2)}) collective-permute-start(f32[256,256]{1,0:T(8,128)S(1)} %collective-permute-done.7.value), channel_id=1, source_target_pairs={{0,8},{8,0},{16,24},{24,16},{1,9},{9,1},{17,25},{25,17},{2,10},{10... | collective-permute-start | bytes 786440 | tf_op jit(solution)/shard_map/ppermute | solution.py:55
  26.5 1.5 %collective-permute-start.9 = (f32[256,256]{1,0:T(8,128)S(1)}, f32[256,256]{1,0:T(8,128)S(1)}, u32[]{:S(2)}, u32[]{:S(2)}) collective-permute-start(f32[256,256]{1,0:T(8,128)S(1)} %collective-permute-done.6.by_y), channel_id=1, source_target_pairs={{0,8},{8,0},{16,24},{24,16},{1,9},{9,1},{17,25},{25,17},{2,10},{10... | collective-permute-start | bytes 786440 | tf_op jit(solution)/shard_map/ppermute | solution.py:55

commit v4 on v3

--- a/solution.py
+++ b/solution.py
@@ -91,65 +91,63 @@
     in_order(group.bit(0), chip, mine, other)
 
 
-def pair_kernel(group, chip, close, wide, pair, sent):
+def near_kernel(group, chip, by_x, near):
     def first():
-        in_order(group.bit(1), pair, chip, close)
-        sent[...] = wide[...]
+        in_order(group.bit(1), near, chip, by_x)
 
     def second():
-        in_order(group.bit(1), pair, close, wide)
-        sent[...] = pair[...]
+        near[...] = chip[...]
 
     when(group.bit(0), second, first)
 
 
-def four_kernel(group, pair, given, four, to_y, to_x):
+def four_kernel(group, wide, close, near, four, to_y, sent):
     def first():
-        in_order(group.bit(2), four, pair, given)
-        to_x[...] = pair[...]
+        in_order(group.bit(1), sent, close, wide)
+        in_order(group.bit(2), four, near, sent)
+        to_y[...] = four[...]
 
     def second():
-        four[...] = given[...]
-        to_x[...] = given[...]
+        for out in (four, to_y, sent):
+            out[...] = wide[...]
 
     when(group.bit(0), second, first)
-    to_y[...] = four[...]
 
 
 def keep_kernel(group, value, kept):
     kept[...] = value[...]
 
 
-def own_kernel(group, mine, other, chip, close, pair, given, by_x, w, after, wp, before, far):
-    @pl.when(jnp.logical_not(group.bit(0)))
-    def _():
-        far[...] = given[...]
-
-        def late():
-            before[...] = mul(mine[...], close[...])
+def own_kernel(group, mine, other, chip, close, by_x, sent, crossed, w, after, wp, before, far):
+    def first():
+        far[...] = sent[...]
+
+        def late():
+            before[...] = mul(mine[...], by_x[...])
             after[...] = other[...]
 
         def early():
             before[...] = mine[...]
-            after[...] = mul(close[...], other[...])
+            after[...] = mul(by_x[...], other[...])
 
         when(group.bit(1), late, early)
 
-    @pl.when(group.bit(0))
-    def _():
-        far[...] = pair[...]
-
-        def late():
-            before[...] = by_x[...]
+    def second():
+        far[...] = crossed[...]
+
+        def late():
+            before[...] = mul(chip[...], close[...])
             row = lax.broadcasted_iota(jnp.int32, after.shape, 0)
             column = lax.broadcasted_iota(jnp.int32, after.shape, 1)
             after[...] = jnp.where(row == column, 1.0, 0.0)
 
         def early():
             before[...] = chip[...]
-            after[...] = mul_nt(by_x[...], chip[...])
+            after[...] = close[...]
 
         when(group.bit(1), late, early)
+
+    when(group.bit(0), second, first)
 
     def late():
         before[...] = mul(before[...], far[...])
@@ -161,20 +159,24 @@
     wp[...] = mul(w[...], before[...])
 
 
-def near_kernel(group, wide, by_x, near):
+def raw_kernel(group, wide, crossed, raw):
     def first():
-        in_order(group.bit(1), near, wide, by_x)
+        raw[...] = crossed[...]
 
     def second():
-        near[...] = wide[...]
+        raw[...] = wide[...]
 
     when(group.bit(0), second, first)
 
 
-def sides_kernel(group, after, wp, near, their_near, by_d, by_y, a, b, three, held):
-    second, near_left, odd, upper = group.bit(0), group.bit(2), group.bit(3), group.bit(4)
-
-    def on_first():
+def opposite_near_kernel(group, raw, come, near):
+    in_order(group.bit(1) == group.bit(0), near, raw, come)
+
+
+def sides_kernel(group, after, wp, near, by_d, by_y, a, b, three, held):
+    second, near_left, odd, upper = jnp.logical_not(group.bit(0)), group.bit(2), group.bit(3), group.bit(4)
+
+    def four_side():
         two, one = by_d, by_y
 
         @pl.when(jnp.logical_not(odd))
@@ -226,9 +228,9 @@
 
         when(upper, early, late)
 
-    def on_second():
+    def opposite_side():
         in_order(group.bit(1), held, by_y, by_d)
-        in_order(near_left, three, their_near, held)
+        in_order(near_left, three, near, held)
 
         def early():
             def odd_four():
@@ -254,15 +256,16 @@
 
         when(upper, early, late)
 
-    when(second, on_second, on_first)
+    when(second, four_side, opposite_side)
 
 
 def closer_kernel(group, a, b, come, new_a, new_b):
-    second, x_bit, near_left, odd, upper = (group.bit(k) for k in range(5))
+    first, x_bit, near_left, odd, upper = (group.bit(k) for k in range(5))
+    second = jnp.logical_not(first)
     new_a[...] = a[...]
     new_b[...] = b[...]
 
-    def on_first():
+    def four_side():
         def early():
             def right():
                 def alone():
@@ -289,7 +292,7 @@
 
         when(upper, early, late)
 
-    def on_second():
+    def opposite_side():
         def early():
             in_order(odd, new_b, come, b)
 
@@ -304,13 +307,14 @@
 
         when(upper, early, late)
 
-    when(second, on_second, on_first)
+    when(second, four_side, opposite_side)
 
 
 def result_kernel(group, a, b, come, result, mid):
-    second, x_bit, near_left, odd, upper = (group.bit(k) for k in range(5))
-    plain = jnp.where(second, odd, upper)
-    alone = odd & jnp.where(second, jnp.logical_not(upper), upper & near_left & jnp.logical_not(x_bit))
+    first, x_bit, near_left, odd, upper = (group.bit(k) for k in range(5))
+    second = jnp.logical_not(first)
+    plain = jnp.where(second, upper, odd)
+    alone = odd & jnp.where(second, upper & near_left & jnp.logical_not(x_bit), jnp.logical_not(upper))
 
     def as_is():
         mid[...] = mul(a[...], come[...])
@@ -353,27 +357,31 @@
     other = group.swap(mine, 1)
     mine = lax.optimization_barrier(jnp.where(lax.axis_index("inner") < n_in, mine, 0.0))
     (chip,) = run(chip_kernel, group, [square], mine, other)
-    wide = group.send(chip, 24, 6)
-    close = group.send(chip, 2, 4)
-    pair, sent = run(pair_kernel, group, [square] * 2, chip, close, wide)
-    given = group.swap(sent, 1)
-    four, to_y, to_x = run(four_kernel, group, [square] * 3, pair, given)
-    by_x, by_d, by_y = group.send(to_x, 1, 3), group.send(four, 16, 6), group.send(to_y, 8, 4)
+    by_x, wide = group.send(chip, 2, 4), group.send(chip, 6, 24)
+    wide, close = lax.optimization_barrier((wide, group.swap(by_x, 1)))
+    (near,) = run(near_kernel, group, [square], chip, by_x)
+    four, to_y, sent = run(four_kernel, group, [square] * 3, wide, close, near)
+    crossed, by_d, far_y = group.send(sent, 1, 3), group.send(four, 16, 6), group.send(to_y, 8, 4)
     after, wp = run(
-        own_kernel, group, [square] * 2, mine, other, chip, close, pair, given, by_x, w, scratch=[square] * 2, weight=3
+        own_kernel,
+        group,
+        [square] * 2,
+        *(mine, other, chip, close, by_x, sent, crossed, w),
+        scratch=[square] * 2,
+        weight=3,
     )
-    by_x, after, wp = lax.optimization_barrier((by_x, after, wp))
-    (near,) = run(near_kernel, group, [square], wide, by_x)
-    their_near = group.swap(near, 1)
+    crossed, after, wp = lax.optimization_barrier((crossed, after, wp))
+    (raw,) = run(raw_kernel, group, [square], wide, crossed)
+    (near,) = run(opposite_near_kernel, group, [square], raw, group.swap(raw, 1))
     their_d = group.swap(by_d, 1)
-    by_y, by_d = lax.optimization_barrier((by_y, *run(keep_kernel, group, [square], by_d)))
+    by_y, by_d = lax.optimization_barrier((far_y, *run(keep_kernel, group, [square], by_d)))
     their_y = group.swap(by_y, 1)
     if bits > 5:
-        second = group.bit(0)
-        one, two = jnp.where(second, their_y, by_y), jnp.where(second, their_d, by_d)
-        far = dot(*ordered(group.bit(1), jnp.where(second, by_y, their_y), jnp.where(second, by_d, their_d)))
-        three = dot(*ordered(group.bit(2), jnp.where(second, their_near, near), far))
-        four = jnp.where(second, group.swap(four, 1), four)
+        second = jnp.logical_not(group.bit(0))
+        one, two = jnp.where(second, by_y, their_y), jnp.where(second, by_d, their_d)
+        far = dot(*ordered(group.bit(1), jnp.where(second, their_y, by_y), jnp.where(second, their_d, by_d)))
+        three = dot(*ordered(group.bit(2), near, far))
+        four = jnp.where(second, four, group.swap(four, 1))
         eight = dot(*ordered(group.bit(3), four, one))
         others = dot(*ordered(group.bit(3), two, three))
         wp, after = join(group, 3, one, wp, after)
@@ -381,7 +389,7 @@
         total = dot(*ordered(group.bit(4), eight, others))
         return pairwise(group, range(5, bits), total, wp, after)[None, None]
     a, b = run(
-        sides_kernel, group, [square] * 2, after, wp, near, their_near, by_d, by_y, scratch=[square] * 2, weight=4
+        sides_kernel, group, [square] * 2, after, wp, near, by_d, by_y, scratch=[square] * 2, weight=4
     )
     a, b = run(closer_kernel, group, [square] * 2, a, b, their_d)
     (result,) = run(result_kernel, group, [square], a, b, their_y, scratch=[square], weight=2)

time: 29.5 us -> 28.3 us (0.959)
  starting transfers between devices: 10.8 us -> 9.37 us
  Pallas kernels: 4.65 us -> 4.95 us
    ppermute x10, starting transfers between devices: 10.8 us -> 9.37 us  [send(): return lax.ppermute(value, ('inner', 'outer'), pairs)]
    pallas_call x9 -> x10, Pallas kernels: 4.65 us -> 4.95 us  [run(): pl.pallas_call(functools.partial(body, group), out_shape=[jax.ShapeDtypeS...]
  transfers between devices with their start and end apart: 10 -> 10, of which waited for: 8 -> 6; matrix products, arithmetic and copies ran while one was open for 3% -> 3% of each run, Pallas kernels for 8% -> 10%
where the time goes in v4:
time: 28.3 us; the launch traced here: 28.1 us
  waiting for transfers between devices  12.7 us (45%)
  starting transfers between devices  9.37 us (33%)
  Pallas kernels  4.95 us (17%)
  other arithmetic  0.97 us (3%)
    ppermute x10, waiting for transfers between devices, send(): return lax.ppermute(value, ('inner', 'outer'), pairs)  12.7 us
    ppermute x10, starting transfers between devices, send(): return lax.ppermute(value, ('inner', 'outer'), pairs)  9.37 us
    pallas_call x10, Pallas kernels, run(): pl.pallas_call(functools.partial(body, group), out_shape=[jax.ShapeDtypeS...  4.95 us
    select_n x1, other arithmetic, body(): jnp.where(lax.axis_index('inner') < n_in, mine, 0.0)  0.97 us
  transfers between devices with their start and end apart: 10, of which 6 were waited for; matrix products, arithmetic and copies ran while one was open for 3% of the time, Pallas kernels for 10%

profile of v4, /device:TPU:0, one launch (start us, length us, event | category | flops | bytes accessed | tf_op | source)
XLA Modules:
  0.0 28.1 jit_solution(3738832693610430223)
XLA Ops:
  0.0 0.5 %collective-permute-start = (f32[256,256]{1,0:T(8,128)}, f32[256,256]{1,0:T(8,128)S(1)}, u32[]{:S(2)}, u32[]{:S(2)}) collective-permute-start(f32[256,256]{1,0:T(8,128)} %bitcast.5), channel_id=1, source_target_pairs={{0,8},{8,0},{16,24},{24,16},{1,9},{9,1},{17,25},{25,17},{2,10},{10... | collective-permute-start | bytes 786440 | tf_op jit(solution)/shard_map/ppermute | solution.py:55
  0.5 1.0 %broadcast_select_fusion.mine = f32[256,256]{1,0:T(8,128)S(1)} fusion(pred[]{:T(512)S(6)} %lt.3, f32[1,1,256,256]{3,2,1,0:T(8,128)} %param.2), kind=kLoop, calls=%fused_computation | loop fusion | flops 65536 | bytes 524289 | tf_op jit(solution)/shard_map/jit(_where)/select_n | solution.py:358
  1.4 0.4 %collective-permute-done.other = f32[256,256]{1,0:T(8,128)S(1)} collective-permute-done((f32[256,256]{1,0:T(8,128)}, f32[256,256]{1,0:T(8,128)S(1)}, u32[]{:S(2)}, u32[]{:S(2)}) %collective-permute-start) | collective-permute-done | bytes 262176 | tf_op jit(solution)/shard_map/ppermute | solution.py:55
  1.8 0.3 shard_map.28.chip
  2.1 2.9 %collective-permute-start.2 = (f32[256,256]{1,0:T(8,128)S(1)}, f32[256,256]{1,0:T(8,128)S(1)}, u32[]{:S(2)}, u32[]{:S(2)}) collective-permute-start(f32[256,256]{1,0:T(8,128)S(1)} %shard_map.28.chip), channel_id=1, source_target_pairs={{0,16},{8,9},{16,0},{24,25},{1,17},{9,8},{17,1},{25,24},{2,18},{10... | collective-permute-start | bytes 786440 | tf_op jit(solution)/shard_map/ppermute | solution.py:55
  5.0 1.5 %collective-permute-start.1 = (f32[256,256]{1,0:T(8,128)S(1)}, f32[256,256]{1,0:T(8,128)S(1)}, u32[]{:S(2)}, u32[]{:S(2)}) collective-permute-start(f32[256,256]{1,0:T(8,128)S(1)} %shard_map.28.chip), channel_id=1, source_target_pairs={{0,17},{8,14},{16,1},{24,30},{1,16},{9,15},{17,0},{25,31},{2,19},{... | collective-permute-start | bytes 786440 | tf_op jit(solution)/shard_map/ppermute | solution.py:55
  6.5 2.9 %collective-permute-done.2.by_x = f32[256,256]{1,0:T(8,128)S(1)} collective-permute-done((f32[256,256]{1,0:T(8,128)S(1)}, f32[256,256]{1,0:T(8,128)S(1)}, u32[]{:S(2)}, u32[]{:S(2)}) %collective-permute-start.2) | collective-permute-done | bytes 262176 | tf_op jit(solution)/shard_map/ppermute | solution.py:55
  9.4 0.3 shard_map.29.near
  9.7 0.0 copy-start
  9.7 4.0 %collective-permute-done.1.wide = f32[256,256]{1,0:T(8,128)S(1)} collective-permute-done((f32[256,256]{1,0:T(8,128)S(1)}, f32[256,256]{1,0:T(8,128)S(1)}, u32[]{:S(2)}, u32[]{:S(2)}) %collective-permute-start.1) | collective-permute-done | bytes 262176 | tf_op jit(solution)/shard_map/ppermute | solution.py:55
  13.7 0.6 %shard_map.30 = (f32[256,256]{1,0:T(8,128)S(1)}, f32[256,256]{1,0:T(8,128)S(1)}, f32[256,256]{1,0:T(8,128)S(1)}) custom-call(f32[256,256]{1,0:T(8,128)S(1)} %collective-permute-done.1.wide, f32[256,256]{1,0:T(8,128)S(1)} %collective-permute-done.3.close, f32[256,256]{1,0:T(8,128)S(1)} %shard_map.29.near), custom_call_target="tpu_custom_call" | custom-call | flops 100663296 | tf_op jit(solution)/shard_map/pallas_call | solution.py:64
  14.3 0.1 collective-permute-start.4
  14.3 2.6 %collective-permute-start.7 = (f32[256,256]{1,0:T(8,128)S(1)}, f32[256,256]{1,0:T(8,128)S(1)}, u32[]{:S(2)}, u32[]{:S(2)}) collective-permute-start(f32[256,256]{1,0:T(8,128)S(1)} %get-tuple-element.30), channel_id=1, source_target_pairs={{0,4},{8,25},{16,20},{24,9},{1,5},{9,24},{17,21},{25,8},{2,6},{10,... | collective-permute-start | bytes 786440 | tf_op jit(solution)/shard_map/ppermute | solution.py:55
  17.0 1.6 %collective-permute-start.6 = (f32[256,256]{1,0:T(8,128)S(1)}, f32[256,256]{1,0:T(8,128)S(1)}, u32[]{:S(2)}, u32[]{:S(2)}) collective-permute-start(f32[256,256]{1,0:T(8,128)S(1)} %get-tuple-element.29), channel_id=1, source_target_pairs={{0,2},{8,9},{16,18},{24,25},{1,3},{9,8},{17,19},{25,24},{2,0},{10,... | collective-permute-start | bytes 786440 | tf_op jit(solution)/shard_map/ppermute | solution.py:55
  18.6 1.6 %collective-permute-done.4.crossed = f32[256,256]{1,0:T(8,128)S(1)} collective-permute-done((f32[256,256]{1,0:T(8,128)S(1)}, f32[256,256]{1,0:T(8,128)S(1)}, u32[]{:S(2)}, u32[]{:S(2)}) %collective-permute-start.4) | collective-permute-done | bytes 262176 | tf_op jit(solution)/shard_map/ppermute | solution.py:55
  20.1 0.9 %shard_map.31 = (f32[256,256]{1,0:T(8,128)S(1)}, f32[256,256]{1,0:T(8,128)S(1)}) custom-call(f32[256,256]{1,0:T(8,128)S(1)} %broadcast_select_fusion.mine, f32[256,256]{1,0:T(8,128)S(1)} %collective-permute-done.other, f32[256,256]{1,0:T(8,128)S(1)} %shard_map.28.chip, f32[256,256]{1,0:T(8,128)S(1)} %collective-permute-done.3.close, ...), custom_call_target="tpu_custom_call" | custom-call | flops 301989888 | tf_op jit(solution)/shard_map/pallas_call | solution.py:64
  21.0 0.1 collective-permute-start.5
  21.1 3.5 %collective-permute-done.7.value = f32[256,256]{1,0:T(8,128)S(1)} collective-permute-done((f32[256,256]{1,0:T(8,128)S(1)}, f32[256,256]{1,0:T(8,128)S(1)}, u32[]{:S(2)}, u32[]{:S(2)}) %collective-permute-start.7) | collective-permute-done | bytes 262176 | tf_op jit(solution)/shard_map/ppermute | solution.py:55
  24.6 0.4 %collective-permute-done.6.by_y = f32[256,256]{1,0:T(8,128)S(1)} collective-permute-done((f32[256,256]{1,0:T(8,128)S(1)}, f32[256,256]{1,0:T(8,128)S(1)}, u32[]{:S(2)}, u32[]{:S(2)}) %collective-permute-start.6) | collective-permute-done | bytes 262176 | tf_op jit(solution)/shard_map/ppermute | solution.py:55
  25.0 0.1 collective-permute-start.9
  25.2 0.3 shard_map.33.near
  25.5 1.0 %shard_map.35 = (f32[256,256]{1,0:T(8,128)S(1)}, f32[256,256]{1,0:T(8,128)S(1)}) custom-call(f32[256,256]{1,0:T(8,128)S(1)} %get-tuple-element.26.after, f32[256,256]{1,0:T(8,128)S(1)} %get-tuple-element.27.wp, f32[256,256]{1,0:T(8,128)S(1)} %shard_map.33.near, f32[256,256]{1,0:T(8,128)S(1)} %shard_map.34.by_d, f32[256,256]{1,0:T(8,128)S(1)} %collective-permute-done.6.by_y), custom_call_target="tpu_custom_call" | custom-call | flops 402653184 | tf_op jit(solution)/shard_map/pallas_call | solution.py:64
  26.4 0.4 %shard_map.36 = (f32[256,256]{1,0:T(8,128)S(1)}, f32[256,256]{1,0:T(8,128)S(1)}) custom-call(f32[256,256]{1,0:T(8,128)S(1)} %get-tuple-element.33.a, f32[256,256]{1,0:T(8,128)S(1)} %get-tuple-element.34.b, f32[256,256]{1,0:T(8,128)S(1)} %collective-permute-done.8.come), custom_call_target="tpu_custom_call" | custom-call | flops 100663296 | tf_op jit(solution)/shard_map/pallas_call | solution.py:64
  26.8 1.3 %shard_map.37 = f32[256,256]{1,0:T(8,128)} custom-call(f32[256,256]{1,0:T(8,128)S(1)} %get-tuple-element.35.a, f32[256,256]{1,0:T(8,128)S(1)} %get-tuple-element.36.b, f32[256,256]{1,0:T(8,128)S(1)} %collective-permute-done.9.come), custom_call_target="tpu_custom_call" | custom-call | flops 201326592 | tf_op jit(solution)/shard_map/pallas_call | solution.py:64
  (9 shorter events, 0.1 us)
Async XLA Ops:
  0.0 1.8 %collective-permute-start = (f32[256,256]{1,0:T(8,128)}, f32[256,256]{1,0:T(8,128)S(1)}, u32[]{:S(2)}, u32[]{:S(2)}) collective-permute-start(f32[256,256]{1,0:T(8,128)} %bitcast.5), channel_id=1, source_target_pairs={{0,8},{8,0},{16,24},{24,16},{1,9},{9,1},{17,25},{25,17},{2,10},{10... | collective-permute-start | bytes 786440 | tf_op jit(solution)/shard_map/ppermute | solution.py:55
  2.1 7.3 %collective-permute-start.2 = (f32[256,256]{1,0:T(8,128)S(1)}, f32[256,256]{1,0:T(8,128)S(1)}, u32[]{:S(2)}, u32[]{:S(2)}) collective-permute-start(f32[256,256]{1,0:T(8,128)S(1)} %shard_map.28.chip), channel_id=1, source_target_pairs={{0,16},{8,9},{16,0},{24,25},{1,17},{9,8},{17,1},{25,24},{2,18},{10... | collective-permute-start | bytes 786440 | tf_op jit(solution)/shard_map/ppermute | solution.py:55
  5.0 8.6 %collective-permute-start.1 = (f32[256,256]{1,0:T(8,128)S(1)}, f32[256,256]{1,0:T(8,128)S(1)}, u32[]{:S(2)}, u32[]{:S(2)}) collective-permute-start(f32[256,256]{1,0:T(8,128)S(1)} %shard_map.28.chip), channel_id=1, source_target_pairs={{0,17},{8,14},{16,1},{24,30},{1,16},{9,15},{17,0},{25,31},{2,19},{... | collective-permute-start | bytes 786440 | tf_op jit(solution)/shard_map/ppermute | solution.py:55
  9.4 4.3 %collective-permute-start.3 = (f32[256,256]{1,0:T(8,128)S(1)}, f32[256,256]{1,0:T(8,128)S(1)}, u32[]{:S(2)}, u32[]{:S(2)}) collective-permute-start(f32[256,256]{1,0:T(8,128)S(1)} %collective-permute-done.2.by_x), channel_id=1, source_target_pairs={{0,8},{8,0},{16,24},{24,16},{1,9},{9,1},{17,25},{25,17},{2,10},{10... | collective-permute-start | bytes 786440 | tf_op jit(solution)/shard_map/ppermute | solution.py:55
  9.7 10.4 %copy-start = (f32[1,1,256,256]{3,2,1,0:T(8,128)S(1)}, f32[1,1,256,256]{3,2,1,0:T(8,128)}, u32[]{:S(2)}) copy-start(f32[1,1,256,256]{3,2,1,0:T(8,128)} %param.3) | copy-start | bytes 786436
  14.3 5.8 %collective-permute-start.4 = (f32[256,256]{1,0:T(8,128)S(1)}, f32[256,256]{1,0:T(8,128)S(1)}, u32[]{:S(2)}, u32[]{:S(2)}) collective-permute-start(f32[256,256]{1,0:T(8,128)S(1)} %get-tuple-element.23.sent), channel_id=1, source_target_pairs={{0,8},{8,16},{16,24},{24,0},{1,9},{9,17},{17,25},{25,1},{2,10},{10... | collective-permute-start | bytes 786440 | tf_op jit(solution)/shard_map/ppermute | solution.py:55
  14.3 10.3 %collective-permute-start.7 = (f32[256,256]{1,0:T(8,128)S(1)}, f32[256,256]{1,0:T(8,128)S(1)}, u32[]{:S(2)}, u32[]{:S(2)}) collective-permute-start(f32[256,256]{1,0:T(8,128)S(1)} %get-tuple-element.30), channel_id=1, source_target_pairs={{0,4},{8,25},{16,20},{24,9},{1,5},{9,24},{17,21},{25,8},{2,6},{10,... | collective-permute-start | bytes 786440 | tf_op jit(solution)/shard_map/ppermute | solution.py:55
  17.0 8.1 %collective-permute-start.6 = (f32[256,256]{1,0:T(8,128)S(1)}, f32[256,256]{1,0:T(8,128)S(1)}, u32[]{:S(2)}, u32[]{:S(2)}) collective-permute-start(f32[256,256]{1,0:T(8,128)S(1)} %get-tuple-element.29), channel_id=1, source_target_pairs={{0,2},{8,9},{16,18},{24,25},{1,3},{9,8},{17,19},{25,24},{2,0},{10,... | collective-permute-start | bytes 786440 | tf_op jit(solution)/shard_map/ppermute | solution.py:55
  21.0 4.2 %collective-permute-start.5 = (f32[256,256]{1,0:T(8,128)S(1)}, f32[256,256]{1,0:T(8,128)S(1)}, u32[]{:S(2)}, u32[]{:S(2)}) collective-permute-start(f32[256,256]{1,0:T(8,128)S(1)} %shard_map.32.raw), channel_id=1, source_target_pairs={{0,8},{8,0},{16,24},{24,16},{1,9},{9,1},{17,25},{25,17},{2,10},{10... | collective-permute-start | bytes 786440 | tf_op jit(solution)/shard_map/ppermute | solution.py:55
  24.6 1.9 %collective-permute-start.8 = (f32[256,256]{1,0:T(8,128)S(1)}, f32[256,256]{1,0:T(8,128)S(1)}, u32[]{:S(2)}, u32[]{:S(2)}) collective-permute-start(f32[256,256]{1,0:T(8,128)S(1)} %collective-permute-done.7.value), channel_id=1, source_target_pairs={{0,8},{8,0},{16,24},{24,16},{1,9},{9,1},{17,25},{25,17},{2,10},{10... | collective-permute-start | bytes 786440 | tf_op jit(solution)/shard_map/ppermute | solution.py:55
  25.0 1.8 %collective-permute-start.9 = (f32[256,256]{1,0:T(8,128)S(1)}, f32[256,256]{1,0:T(8,128)S(1)}, u32[]{:S(2)}, u32[]{:S(2)}) collective-permute-start(f32[256,256]{1,0:T(8,128)S(1)} %collective-permute-done.6.by_y), channel_id=1, source_target_pairs={{0,8},{8,0},{16,24},{24,16},{1,9},{9,1},{17,25},{25,17},{2,10},{10... | collective-permute-start | bytes 786440 | tf_op jit(solution)/shard_map/ppermute | solution.py:55

commit v5 on v4

--- a/solution.py
+++ b/solution.py
@@ -91,25 +91,44 @@
     in_order(group.bit(0), chip, mine, other)
 
 
-def near_kernel(group, chip, by_x, near):
+def in_pieces(value, number):
+    rows = value.shape[0] // number
+    return [value[k * rows : (k + 1) * rows] for k in range(number)]
+
+
+def near_kernel(group, chip, by_x, top, bottom, near, three, close):
+    rows = top.shape[0]
+    close[pl.ds(0, rows)] = top[...]
+    close[pl.ds(rows, rows)] = bottom[...]
+
     def first():
         in_order(group.bit(1), near, chip, by_x)
 
+        @pl.when(group.bit(1) == group.bit(2))
+        def _():
+            in_order(group.bit(1), three, near, close)
+
     def second():
         near[...] = chip[...]
 
     when(group.bit(0), second, first)
 
 
-def four_kernel(group, wide, close, near, four, to_y, sent):
+def four_kernel(group, wide, close, near, three, four, to_y, far):
     def first():
-        in_order(group.bit(1), sent, close, wide)
-        in_order(group.bit(2), four, near, sent)
+        def at_end():
+            in_order(group.bit(1), four, three, wide)
+
+        def inside():
+            in_order(group.bit(1), far, close, wide)
+            in_order(group.bit(2), four, near, far)
+
+        when(group.bit(1) == group.bit(2), at_end, inside)
         to_y[...] = four[...]
 
     def second():
-        for out in (four, to_y, sent):
-            out[...] = wide[...]
+        four[...] = wide[...]
+        to_y[...] = wide[...]
 
     when(group.bit(0), second, first)
 
@@ -118,9 +137,9 @@
     kept[...] = value[...]
 
 
-def own_kernel(group, mine, other, chip, close, by_x, sent, crossed, w, after, wp, before, far):
+def own_kernel(group, mine, other, chip, close, by_x, wide, crossed, w, after, wp, before, far):
     def first():
-        far[...] = sent[...]
+        in_order(group.bit(1), far, close, wide)
 
         def late():
             before[...] = mul(mine[...], by_x[...])
@@ -133,7 +152,7 @@
         when(group.bit(1), late, early)
 
     def second():
-        far[...] = crossed[...]
+        in_order(group.bit(1), far, by_x, crossed)
 
         def late():
             before[...] = mul(chip[...], close[...])
@@ -358,15 +377,17 @@
     mine = lax.optimization_barrier(jnp.where(lax.axis_index("inner") < n_in, mine, 0.0))
     (chip,) = run(chip_kernel, group, [square], mine, other)
     by_x, wide = group.send(chip, 2, 4), group.send(chip, 6, 24)
-    wide, close = lax.optimization_barrier((wide, group.swap(by_x, 1)))
-    (near,) = run(near_kernel, group, [square], chip, by_x)
-    four, to_y, sent = run(four_kernel, group, [square] * 3, wide, close, near)
-    crossed, by_d, far_y = group.send(sent, 1, 3), group.send(four, 16, 6), group.send(to_y, 8, 4)
+    pieces = [group.swap(piece, 1) for piece in in_pieces(by_x, 2)]
+    near, three, close = run(near_kernel, group, [square] * 3, chip, by_x, *pieces)
+    wide, near, three, close = lax.optimization_barrier((wide, near, three, close))
+    crossed = group.send(wide, 1, 3)
+    four, to_y = run(four_kernel, group, [square] * 2, wide, close, near, three, scratch=[square])
+    by_d, far_y = group.send(four, 16, 6), group.send(to_y, 8, 4)
     after, wp = run(
         own_kernel,
         group,
         [square] * 2,
-        *(mine, other, chip, close, by_x, sent, crossed, w),
+        *(mine, other, chip, close, by_x, wide, crossed, w),
         scratch=[square] * 2,
         weight=3,
     )

time: 28.3 us -> 27.9 us (0.986)
  waiting for transfers between devices: 12.7 us -> 11.6 us
  starting transfers between devices: 9.37 us -> 9.88 us
  Pallas kernels: 4.95 us -> 5.24 us
    ppermute x10 -> x11, waiting for transfers between devices: 12.7 us -> 11.6 us  [send(): return lax.ppermute(value, ('inner', 'outer'), pairs)]
    ppermute x10 -> x11, starting transfers between devices: 9.37 us -> 9.88 us  [send(): return lax.ppermute(value, ('inner', 'outer'), pairs)]
    pallas_call x10, Pallas kernels: 4.95 us -> 5.24 us  [run(): pl.pallas_call(functools.partial(body, group), out_shape=[jax.ShapeDtypeS...]
  transfers between devices with their start and end apart: 10 -> 11, of which waited for: 6 -> 8; matrix products, arithmetic and copies ran while one was open for 3% -> 4% of each run, Pallas kernels for 10% -> 13%
where the time goes in v5:
time: 27.9 us; the launch traced here: 27.8 us
  waiting for transfers between devices  11.6 us (42%)
  starting transfers between devices  9.88 us (35%)
  Pallas kernels  5.24 us (19%)
  other arithmetic  0.97 us (3%)
    ppermute x11, waiting for transfers between devices, send(): return lax.ppermute(value, ('inner', 'outer'), pairs)  11.6 us
    ppermute x11, starting transfers between devices, send(): return lax.ppermute(value, ('inner', 'outer'), pairs)  9.88 us
    pallas_call x10, Pallas kernels, run(): pl.pallas_call(functools.partial(body, group), out_shape=[jax.ShapeDtypeS...  5.24 us
    select_n x1, other arithmetic, body(): jnp.where(lax.axis_index('inner') < n_in, mine, 0.0)  0.97 us
  transfers between devices with their start and end apart: 11, of which 8 were waited for; matrix products, arithmetic and copies ran while one was open for 4% of the time, Pallas kernels for 13%

profile of v5, /device:TPU:0, one launch (start us, length us, event | category | flops | bytes accessed | tf_op | source)
XLA Modules:
  0.0 27.8 jit_solution(1780110808558868129)
XLA Ops:
  0.0 0.5 %collective-permute-start = (f32[256,256]{1,0:T(8,128)}, f32[256,256]{1,0:T(8,128)S(1)}, u32[]{:S(2)}, u32[]{:S(2)}) collective-permute-start(f32[256,256]{1,0:T(8,128)} %bitcast.5), channel_id=1, source_target_pairs={{0,8},{8,0},{16,24},{24,16},{1,9},{9,1},{17,25},{25,17},{2,10},{10... | collective-permute-start | bytes 786440 | tf_op jit(solution)/shard_map/ppermute | solution.py:55
  0.5 1.0 %broadcast_select_fusion.mine = f32[256,256]{1,0:T(8,128)S(1)} fusion(pred[]{:T(512)S(6)} %lt.3, f32[1,1,256,256]{3,2,1,0:T(8,128)} %param.2), kind=kLoop, calls=%fused_computation | loop fusion | flops 65536 | bytes 524289 | tf_op jit(solution)/shard_map/jit(_where)/select_n | solution.py:377
  1.4 0.4 %collective-permute-done.other = f32[256,256]{1,0:T(8,128)S(1)} collective-permute-done((f32[256,256]{1,0:T(8,128)}, f32[256,256]{1,0:T(8,128)S(1)}, u32[]{:S(2)}, u32[]{:S(2)}) %collective-permute-start) | collective-permute-done | bytes 262176 | tf_op jit(solution)/shard_map/ppermute | solution.py:55
  1.8 0.3 shard_map.28.chip
  2.1 2.9 %collective-permute-start.2 = (f32[256,256]{1,0:T(8,128)S(1)}, f32[256,256]{1,0:T(8,128)S(1)}, u32[]{:S(2)}, u32[]{:S(2)}) collective-permute-start(f32[256,256]{1,0:T(8,128)S(1)} %shard_map.28.chip), channel_id=1, source_target_pairs={{0,16},{8,9},{16,0},{24,25},{1,17},{9,8},{17,1},{25,24},{2,18},{10... | collective-permute-start | bytes 786440 | tf_op jit(solution)/shard_map/ppermute | solution.py:55
  5.0 1.5 %collective-permute-start.1 = (f32[256,256]{1,0:T(8,128)S(1)}, f32[256,256]{1,0:T(8,128)S(1)}, u32[]{:S(2)}, u32[]{:S(2)}) collective-permute-start(f32[256,256]{1,0:T(8,128)S(1)} %shard_map.28.chip), channel_id=1, source_target_pairs={{0,17},{8,14},{16,1},{24,30},{1,16},{9,15},{17,0},{25,31},{2,19},{... | collective-permute-start | bytes 786440 | tf_op jit(solution)/shard_map/ppermute | solution.py:55
  6.5 2.9 %collective-permute-done.2.by_x = f32[256,256]{1,0:T(8,128)S(1)} collective-permute-done((f32[256,256]{1,0:T(8,128)S(1)}, f32[256,256]{1,0:T(8,128)S(1)}, u32[]{:S(2)}, u32[]{:S(2)}) %collective-permute-start.2) | collective-permute-done | bytes 262176 | tf_op jit(solution)/shard_map/ppermute | solution.py:55
  9.5 0.5 %collective-permute-start.4 = (f32[128,256]{1,0:T(8,128)S(1)}, f32[128,256]{1,0:T(8,128)S(1)}, u32[]{:S(2)}, u32[]{:S(2)}) collective-permute-start(f32[128,256]{1,0:T(8,128)S(1)} %get-tuple-element.45), channel_id=1, source_target_pairs={{0,8},{8,0},{16,24},{24,16},{1,9},{9,1},{17,25},{25,17},{2,10},{10... | collective-permute-start | bytes 393224 | tf_op jit(solution)/shard_map/ppermute | solution.py:55
  10.0 0.8 %collective-permute-done.3.top = f32[128,256]{1,0:T(8,128)S(1)} collective-permute-done((f32[128,256]{1,0:T(8,128)S(1)}, f32[128,256]{1,0:T(8,128)S(1)}, u32[]{:S(2)}, u32[]{:S(2)}) %collective-permute-start.3) | collective-permute-done | bytes 131104 | tf_op jit(solution)/shard_map/ppermute | solution.py:55
  10.8 0.2 collective-permute-done.4.bottom
  11.0 0.6 %shard_map.29 = (f32[256,256]{1,0:T(8,128)S(1)}, f32[256,256]{1,0:T(8,128)S(1)}, f32[256,256]{1,0:T(8,128)S(1)}) custom-call(f32[256,256]{1,0:T(8,128)S(1)} %shard_map.28.chip, f32[256,256]{1,0:T(8,128)S(1)} %collective-permute-done.2.by_x, f32[128,256]{1,0:T(8,128)S(1)} %collective-permute-done.3.top, f32[128,256]{1,0:T(8,128)S(1)} %collective-permute-done.4.bottom), custom_call_target="tpu_custom_call" | custom-call | flops 100663296 | tf_op jit(solution)/shard_map/pallas_call | solution.py:64
  11.6 2.1 %collective-permute-done.1.wide = f32[256,256]{1,0:T(8,128)S(1)} collective-permute-done((f32[256,256]{1,0:T(8,128)S(1)}, f32[256,256]{1,0:T(8,128)S(1)}, u32[]{:S(2)}, u32[]{:S(2)}) %collective-permute-start.1) | collective-permute-done | bytes 262176 | tf_op jit(solution)/shard_map/ppermute | solution.py:55
  13.7 0.3 %shard_map.33 = (f32[256,256]{1,0:T(8,128)S(1)}, f32[256,256]{1,0:T(8,128)S(1)}) custom-call(f32[256,256]{1,0:T(8,128)S(1)} %collective-permute-done.1.wide, f32[256,256]{1,0:T(8,128)S(1)} %get-tuple-element.29.close, f32[256,256]{1,0:T(8,128)S(1)} %get-tuple-element.35.near, f32[256,256]{1,0:T(8,128)S(1)} %get-tuple-element.36.three), custom_call_target="tpu_custom_call" | custom-call | flops 100663296 | tf_op jit(solution)/shard_map/pallas_call | solution.py:64
  14.0 2.7 %collective-permute-start.8 = (f32[256,256]{1,0:T(8,128)S(1)}, f32[256,256]{1,0:T(8,128)S(1)}, u32[]{:S(2)}, u32[]{:S(2)}) collective-permute-start(f32[256,256]{1,0:T(8,128)S(1)} %get-tuple-element.38), channel_id=1, source_target_pairs={{0,4},{8,25},{16,20},{24,9},{1,5},{9,24},{17,21},{25,8},{2,6},{10,... | collective-permute-start | bytes 786440 | tf_op jit(solution)/shard_map/ppermute | solution.py:55
  16.6 1.6 %collective-permute-start.7 = (f32[256,256]{1,0:T(8,128)S(1)}, f32[256,256]{1,0:T(8,128)S(1)}, u32[]{:S(2)}, u32[]{:S(2)}) collective-permute-start(f32[256,256]{1,0:T(8,128)S(1)} %get-tuple-element.37), channel_id=1, source_target_pairs={{0,2},{8,9},{16,18},{24,25},{1,3},{9,8},{17,19},{25,24},{2,0},{10,... | collective-permute-start | bytes 786440 | tf_op jit(solution)/shard_map/ppermute | solution.py:55
  18.2 1.3 %collective-permute-done.5.crossed = f32[256,256]{1,0:T(8,128)S(1)} collective-permute-done((f32[256,256]{1,0:T(8,128)S(1)}, f32[256,256]{1,0:T(8,128)S(1)}, u32[]{:S(2)}, u32[]{:S(2)}) %collective-permute-start.5) | collective-permute-done | bytes 262176 | tf_op jit(solution)/shard_map/ppermute | solution.py:55
  19.5 1.1 %shard_map.30 = (f32[256,256]{1,0:T(8,128)S(1)}, f32[256,256]{1,0:T(8,128)S(1)}) custom-call(f32[256,256]{1,0:T(8,128)S(1)} %broadcast_select_fusion.mine, f32[256,256]{1,0:T(8,128)S(1)} %collective-permute-done.other, f32[256,256]{1,0:T(8,128)S(1)} %shard_map.28.chip, f32[256,256]{1,0:T(8,128)S(1)} %get-tuple-element.29.close, ...), custom_call_target="tpu_custom_call" | custom-call | flops 301989888 | tf_op jit(solution)/shard_map/pallas_call | solution.py:64
  20.7 3.5 %collective-permute-done.8.value = f32[256,256]{1,0:T(8,128)S(1)} collective-permute-done((f32[256,256]{1,0:T(8,128)S(1)}, f32[256,256]{1,0:T(8,128)S(1)}, u32[]{:S(2)}, u32[]{:S(2)}) %collective-permute-start.8) | collective-permute-done | bytes 262176 | tf_op jit(solution)/shard_map/ppermute | solution.py:55
  24.3 0.4 %collective-permute-done.7.by_y = f32[256,256]{1,0:T(8,128)S(1)} collective-permute-done((f32[256,256]{1,0:T(8,128)S(1)}, f32[256,256]{1,0:T(8,128)S(1)}, u32[]{:S(2)}, u32[]{:S(2)}) %collective-permute-start.7) | collective-permute-done | bytes 262176 | tf_op jit(solution)/shard_map/ppermute | solution.py:55
  24.7 0.1 collective-permute-start.10
  24.8 0.3 shard_map.32.near
  25.1 1.0 %shard_map.35 = (f32[256,256]{1,0:T(8,128)S(1)}, f32[256,256]{1,0:T(8,128)S(1)}) custom-call(f32[256,256]{1,0:T(8,128)S(1)} %get-tuple-element.32.after, f32[256,256]{1,0:T(8,128)S(1)} %get-tuple-element.33.wp, f32[256,256]{1,0:T(8,128)S(1)} %shard_map.32.near, f32[256,256]{1,0:T(8,128)S(1)} %shard_map.34.by_d, f32[256,256]{1,0:T(8,128)S(1)} %collective-permute-done.7.by_y), custom_call_target="tpu_custom_call" | custom-call | flops 402653184 | tf_op jit(solution)/shard_map/pallas_call | solution.py:64
  26.1 0.4 %shard_map.36 = (f32[256,256]{1,0:T(8,128)S(1)}, f32[256,256]{1,0:T(8,128)S(1)}) custom-call(f32[256,256]{1,0:T(8,128)S(1)} %get-tuple-element.41.a, f32[256,256]{1,0:T(8,128)S(1)} %get-tuple-element.42.b, f32[256,256]{1,0:T(8,128)S(1)} %collective-permute-done.9.come), custom_call_target="tpu_custom_call" | custom-call | flops 100663296 | tf_op jit(solution)/shard_map/pallas_call | solution.py:64
  26.5 1.3 %shard_map.37 = f32[256,256]{1,0:T(8,128)} custom-call(f32[256,256]{1,0:T(8,128)S(1)} %get-tuple-element.43.a, f32[256,256]{1,0:T(8,128)S(1)} %get-tuple-element.44.b, f32[256,256]{1,0:T(8,128)S(1)} %collective-permute-done.10.come), custom_call_target="tpu_custom_call" | custom-call | flops 201326592 | tf_op jit(solution)/shard_map/pallas_call | solution.py:64
  (12 shorter events, 0.2 us)
Async XLA Ops:
  0.0 1.8 %collective-permute-start = (f32[256,256]{1,0:T(8,128)}, f32[256,256]{1,0:T(8,128)S(1)}, u32[]{:S(2)}, u32[]{:S(2)}) collective-permute-start(f32[256,256]{1,0:T(8,128)} %bitcast.5), channel_id=1, source_target_pairs={{0,8},{8,0},{16,24},{24,16},{1,9},{9,1},{17,25},{25,17},{2,10},{10... | collective-permute-start | bytes 786440 | tf_op jit(solution)/shard_map/ppermute | solution.py:55
  2.1 7.3 %collective-permute-start.2 = (f32[256,256]{1,0:T(8,128)S(1)}, f32[256,256]{1,0:T(8,128)S(1)}, u32[]{:S(2)}, u32[]{:S(2)}) collective-permute-start(f32[256,256]{1,0:T(8,128)S(1)} %shard_map.28.chip), channel_id=1, source_target_pairs={{0,16},{8,9},{16,0},{24,25},{1,17},{9,8},{17,1},{25,24},{2,18},{10... | collective-permute-start | bytes 786440 | tf_op jit(solution)/shard_map/ppermute | solution.py:55
  5.0 8.6 %collective-permute-start.1 = (f32[256,256]{1,0:T(8,128)S(1)}, f32[256,256]{1,0:T(8,128)S(1)}, u32[]{:S(2)}, u32[]{:S(2)}) collective-permute-start(f32[256,256]{1,0:T(8,128)S(1)} %shard_map.28.chip), channel_id=1, source_target_pairs={{0,17},{8,14},{16,1},{24,30},{1,16},{9,15},{17,0},{25,31},{2,19},{... | collective-permute-start | bytes 786440 | tf_op jit(solution)/shard_map/ppermute | solution.py:55
  9.4 1.4 %collective-permute-start.3 = (f32[128,256]{1,0:T(8,128)S(1)}, f32[128,256]{1,0:T(8,128)S(1)}, u32[]{:S(2)}, u32[]{:S(2)}) collective-permute-start(f32[128,256]{1,0:T(8,128)S(1)} %get-tuple-element.46), channel_id=1, source_target_pairs={{0,8},{8,0},{16,24},{24,16},{1,9},{9,1},{17,25},{25,17},{2,10},{10... | collective-permute-start | bytes 393224 | tf_op jit(solution)/shard_map/ppermute | solution.py:55
  9.5 1.5 %collective-permute-start.4 = (f32[128,256]{1,0:T(8,128)S(1)}, f32[128,256]{1,0:T(8,128)S(1)}, u32[]{:S(2)}, u32[]{:S(2)}) collective-permute-start(f32[128,256]{1,0:T(8,128)S(1)} %get-tuple-element.45), channel_id=1, source_target_pairs={{0,8},{8,0},{16,24},{24,16},{1,9},{9,1},{17,25},{25,17},{2,10},{10... | collective-permute-start | bytes 393224 | tf_op jit(solution)/shard_map/ppermute | solution.py:55
  13.7 5.8 %copy-start = (f32[1,1,256,256]{3,2,1,0:T(8,128)S(1)}, f32[1,1,256,256]{3,2,1,0:T(8,128)}, u32[]{:S(2)}) copy-start(f32[1,1,256,256]{3,2,1,0:T(8,128)} %param.3) | copy-start | bytes 786436
  13.7 5.8 %collective-permute-start.5 = (f32[256,256]{1,0:T(8,128)S(1)}, f32[256,256]{1,0:T(8,128)S(1)}, u32[]{:S(2)}, u32[]{:S(2)}) collective-permute-start(f32[256,256]{1,0:T(8,128)S(1)} %collective-permute-done.1.wide), channel_id=1, source_target_pairs={{0,8},{8,16},{16,24},{24,0},{1,9},{9,17},{17,25},{25,1},{2,10},{10... | collective-permute-start | bytes 786440 | tf_op jit(solution)/shard_map/ppermute | solution.py:55
  14.0 10.3 %collective-permute-start.8 = (f32[256,256]{1,0:T(8,128)S(1)}, f32[256,256]{1,0:T(8,128)S(1)}, u32[]{:S(2)}, u32[]{:S(2)}) collective-permute-start(f32[256,256]{1,0:T(8,128)S(1)} %get-tuple-element.38), channel_id=1, source_target_pairs={{0,4},{8,25},{16,20},{24,9},{1,5},{9,24},{17,21},{25,8},{2,6},{10,... | collective-permute-start | bytes 786440 | tf_op jit(solution)/shard_map/ppermute | solution.py:55
  16.6 8.1 %collective-permute-start.7 = (f32[256,256]{1,0:T(8,128)S(1)}, f32[256,256]{1,0:T(8,128)S(1)}, u32[]{:S(2)}, u32[]{:S(2)}) collective-permute-start(f32[256,256]{1,0:T(8,128)S(1)} %get-tuple-element.37), channel_id=1, source_target_pairs={{0,2},{8,9},{16,18},{24,25},{1,3},{9,8},{17,19},{25,24},{2,0},{10,... | collective-permute-start | bytes 786440 | tf_op jit(solution)/shard_map/ppermute | solution.py:55
  20.7 4.2 %collective-permute-start.6 = (f32[256,256]{1,0:T(8,128)S(1)}, f32[256,256]{1,0:T(8,128)S(1)}, u32[]{:S(2)}, u32[]{:S(2)}) collective-permute-start(f32[256,256]{1,0:T(8,128)S(1)} %shard_map.31.raw), channel_id=1, source_target_pairs={{0,8},{8,0},{16,24},{24,16},{1,9},{9,1},{17,25},{25,17},{2,10},{10... | collective-permute-start | bytes 786440 | tf_op jit(solution)/shard_map/ppermute | solution.py:55
  24.2 1.9 %collective-permute-start.9 = (f32[256,256]{1,0:T(8,128)S(1)}, f32[256,256]{1,0:T(8,128)S(1)}, u32[]{:S(2)}, u32[]{:S(2)}) collective-permute-start(f32[256,256]{1,0:T(8,128)S(1)} %collective-permute-done.8.value), channel_id=1, source_target_pairs={{0,8},{8,0},{16,24},{24,16},{1,9},{9,1},{17,25},{25,17},{2,10},{10... | collective-permute-start | bytes 786440 | tf_op jit(solution)/shard_map/ppermute | solution.py:55
  24.7 1.8 %collective-permute-start.10 = (f32[256,256]{1,0:T(8,128)S(1)}, f32[256,256]{1,0:T(8,128)S(1)}, u32[]{:S(2)}, u32[]{:S(2)}) collective-permute-start(f32[256,256]{1,0:T(8,128)S(1)} %collective-permute-done.7.by_y), channel_id=1, source_target_pairs={{0,8},{8,0},{16,24},{24,16},{1,9},{9,1},{17,25},{25,17},{2,10},{10... | collective-permute-start | bytes 786440 | tf_op jit(solution)/shard_map/ppermute | solution.py:55

commit v6 on v5

--- a/solution.py
+++ b/solution.py
@@ -178,21 +178,29 @@
     wp[...] = mul(w[...], before[...])
 
 
-def raw_kernel(group, wide, crossed, raw):
-    def first():
-        raw[...] = crossed[...]
-
-    def second():
-        raw[...] = wide[...]
-
-    when(group.bit(0), second, first)
-
-
-def opposite_near_kernel(group, raw, come, near):
-    in_order(group.bit(1) == group.bit(0), near, raw, come)
-
-
-def sides_kernel(group, after, wp, near, by_d, by_y, a, b, three, held):
+def raw_kernel(group, wide, crossed, top, bottom):
+    rows = top.shape[0]
+
+    def send(value):
+        top[...] = value[pl.ds(0, rows)]
+        bottom[...] = value[pl.ds(rows, rows)]
+
+    when(group.bit(0), lambda: send(wide), lambda: send(crossed))
+
+
+def opposite_near_kernel(group, crossed, top, bottom, near):
+    rows = top.shape[0]
+    near[pl.ds(0, rows)] = top[...]
+    near[pl.ds(rows, rows)] = bottom[...]
+
+    @pl.when(jnp.logical_not(group.bit(0)))
+    def _():
+        left = jnp.where(group.bit(1), near[...], crossed[...])
+        right = jnp.where(group.bit(1), crossed[...], near[...])
+        near[...] = mul(left, right)
+
+
+def sides_kernel(group, after, wp, near, wide, by_d, by_y, a, b, three, held, opposite):
     second, near_left, odd, upper = jnp.logical_not(group.bit(0)), group.bit(2), group.bit(3), group.bit(4)
 
     def four_side():
@@ -248,8 +256,9 @@
         when(upper, early, late)
 
     def opposite_side():
-        in_order(group.bit(1), held, by_y, by_d)
-        in_order(near_left, three, near, held)
+        in_order(group.bit(1), held, by_d, by_y)
+        in_order(group.bit(1), opposite, wide, near)
+        in_order(near_left, three, opposite, held)
 
         def early():
             def odd_four():
@@ -280,7 +289,7 @@
 
 def closer_kernel(group, a, b, come, new_a, new_b):
     first, x_bit, near_left, odd, upper = (group.bit(k) for k in range(5))
-    second = jnp.logical_not(first)
+    second, x_bit = jnp.logical_not(first), jnp.logical_not(x_bit)
     new_a[...] = a[...]
     new_b[...] = b[...]
 
@@ -331,7 +340,7 @@
 
 def result_kernel(group, a, b, come, result, mid):
     first, x_bit, near_left, odd, upper = (group.bit(k) for k in range(5))
-    second = jnp.logical_not(first)
+    second, x_bit = jnp.logical_not(first), jnp.logical_not(x_bit)
     plain = jnp.where(second, upper, odd)
     alone = odd & jnp.where(second, upper & near_left & jnp.logical_not(x_bit), jnp.logical_not(upper))
 
@@ -382,7 +391,7 @@
     wide, near, three, close = lax.optimization_barrier((wide, near, three, close))
     crossed = group.send(wide, 1, 3)
     four, to_y = run(four_kernel, group, [square] * 2, wide, close, near, three, scratch=[square])
-    by_d, far_y = group.send(four, 16, 6), group.send(to_y, 8, 4)
+    by_d, far_y = group.send(four, 16, 4), group.send(to_y, 8, 6)
     after, wp = run(
         own_kernel,
         group,
@@ -392,15 +401,17 @@
         weight=3,
     )
     crossed, after, wp = lax.optimization_barrier((crossed, after, wp))
-    (raw,) = run(raw_kernel, group, [square], wide, crossed)
-    (near,) = run(opposite_near_kernel, group, [square], raw, group.swap(raw, 1))
+    half = (square[0] // 2, square[1])
+    pieces = [group.swap(piece, 1) for piece in run(raw_kernel, group, [half] * 2, wide, crossed)]
+    (near,) = run(opposite_near_kernel, group, [square], crossed, *pieces)
     their_d = group.swap(by_d, 1)
-    by_y, by_d = lax.optimization_barrier((far_y, *run(keep_kernel, group, [square], by_d)))
+    by_y, by_d, near = lax.optimization_barrier((far_y, *run(keep_kernel, group, [square], by_d), near))
     their_y = group.swap(by_y, 1)
     if bits > 5:
         second = jnp.logical_not(group.bit(0))
         one, two = jnp.where(second, by_y, their_y), jnp.where(second, by_d, their_d)
-        far = dot(*ordered(group.bit(1), jnp.where(second, their_y, by_y), jnp.where(second, their_d, by_d)))
+        far = dot(*ordered(group.bit(1), jnp.where(second, their_d, by_d), jnp.where(second, their_y, by_y)))
+        near = jnp.where(second, near, dot(*ordered(group.bit(1), wide, near)))
         three = dot(*ordered(group.bit(2), near, far))
         four = jnp.where(second, four, group.swap(four, 1))
         eight = dot(*ordered(group.bit(3), four, one))
@@ -410,7 +421,7 @@
         total = dot(*ordered(group.bit(4), eight, others))
         return pairwise(group, range(5, bits), total, wp, after)[None, None]
     a, b = run(
-        sides_kernel, group, [square] * 2, after, wp, near, by_d, by_y, scratch=[square] * 2, weight=4
+        sides_kernel, group, [square] * 2, after, wp, near, wide, by_d, by_y, scratch=[square] * 3, weight=4
     )
     a, b = run(closer_kernel, group, [square] * 2, a, b, their_d)
     (result,) = run(result_kernel, group, [square], a, b, their_y, scratch=[square], weight=2)

time: 27.9 us -> 27.8 us (level)
  waiting for transfers between devices: 11.6 us -> 10.8 us
  starting transfers between devices: 9.88 us -> 10.4 us
    ppermute x11 -> x12, waiting for transfers between devices: 11.6 us -> 10.8 us  [send(): return lax.ppermute(value, ('inner', 'outer'), pairs)]
    ppermute x11 -> x12, starting transfers between devices: 9.88 us -> 10.4 us  [send(): return lax.ppermute(value, ('inner', 'outer'), pairs)]
  transfers between devices with their start and end apart: 11 -> 12, of which waited for: 8 -> 8; matrix products, arithmetic and copies ran while one was open for 4% -> 4% of each run, Pallas kernels for 13% -> 13%
where the time goes in v6:
time: 27.8 us; the launch traced here: 27.5 us
  waiting for transfers between devices  10.8 us (39%)
  starting transfers between devices  10.4 us (37%)
  Pallas kernels  5.24 us (19%)
  other arithmetic  0.97 us (3%)
    ppermute x12, waiting for transfers between devices, send(): return lax.ppermute(value, ('inner', 'outer'), pairs)  10.8 us
    ppermute x12, starting transfers between devices, send(): return lax.ppermute(value, ('inner', 'outer'), pairs)  10.4 us
    pallas_call x10, Pallas kernels, run(): pl.pallas_call(functools.partial(body, group), out_shape=[jax.ShapeDtypeS...  5.24 us
    select_n x1, other arithmetic, body(): jnp.where(lax.axis_index('inner') < n_in, mine, 0.0)  0.97 us
  transfers between devices with their start and end apart: 12, of which 8 were waited for; matrix products, arithmetic and copies ran while one was open for 4% of the time, Pallas kernels for 13%

profile of v6, /device:TPU:0, one launch (start us, length us, event | category | flops | bytes accessed | tf_op | source)
XLA Modules:
  0.0 27.5 jit_solution(4051171305672626185)
XLA Ops:
  0.0 0.5 %collective-permute-start = (f32[256,256]{1,0:T(8,128)}, f32[256,256]{1,0:T(8,128)S(1)}, u32[]{:S(2)}, u32[]{:S(2)}) collective-permute-start(f32[256,256]{1,0:T(8,128)} %bitcast.5), channel_id=1, source_target_pairs={{0,8},{8,0},{16,24},{24,16},{1,9},{9,1},{17,25},{25,17},{2,10},{10... | collective-permute-start | bytes 786440 | tf_op jit(solution)/shard_map/ppermute | solution.py:55
  0.5 1.0 %broadcast_select_fusion.mine = f32[256,256]{1,0:T(8,128)S(1)} fusion(pred[]{:T(512)S(6)} %lt.3, f32[1,1,256,256]{3,2,1,0:T(8,128)} %param.2), kind=kLoop, calls=%fused_computation | loop fusion | flops 65536 | bytes 524289 | tf_op jit(solution)/shard_map/jit(_where)/select_n | solution.py:386
  1.4 0.4 %collective-permute-done.other = f32[256,256]{1,0:T(8,128)S(1)} collective-permute-done((f32[256,256]{1,0:T(8,128)}, f32[256,256]{1,0:T(8,128)S(1)}, u32[]{:S(2)}, u32[]{:S(2)}) %collective-permute-start) | collective-permute-done | bytes 262176 | tf_op jit(solution)/shard_map/ppermute | solution.py:55
  1.8 0.3 shard_map.28.chip
  2.1 2.9 %collective-permute-start.2 = (f32[256,256]{1,0:T(8,128)S(1)}, f32[256,256]{1,0:T(8,128)S(1)}, u32[]{:S(2)}, u32[]{:S(2)}) collective-permute-start(f32[256,256]{1,0:T(8,128)S(1)} %shard_map.28.chip), channel_id=1, source_target_pairs={{0,16},{8,9},{16,0},{24,25},{1,17},{9,8},{17,1},{25,24},{2,18},{10... | collective-permute-start | bytes 786440 | tf_op jit(solution)/shard_map/ppermute | solution.py:55
  5.0 1.5 %collective-permute-start.1 = (f32[256,256]{1,0:T(8,128)S(1)}, f32[256,256]{1,0:T(8,128)S(1)}, u32[]{:S(2)}, u32[]{:S(2)}) collective-permute-start(f32[256,256]{1,0:T(8,128)S(1)} %shard_map.28.chip), channel_id=1, source_target_pairs={{0,17},{8,14},{16,1},{24,30},{1,16},{9,15},{17,0},{25,31},{2,19},{... | collective-permute-start | bytes 786440 | tf_op jit(solution)/shard_map/ppermute | solution.py:55
  6.5 2.9 %collective-permute-done.2.by_x = f32[256,256]{1,0:T(8,128)S(1)} collective-permute-done((f32[256,256]{1,0:T(8,128)S(1)}, f32[256,256]{1,0:T(8,128)S(1)}, u32[]{:S(2)}, u32[]{:S(2)}) %collective-permute-start.2) | collective-permute-done | bytes 262176 | tf_op jit(solution)/shard_map/ppermute | solution.py:55
  9.5 0.5 %collective-permute-start.4 = (f32[128,256]{1,0:T(8,128)S(1)}, f32[128,256]{1,0:T(8,128)S(1)}, u32[]{:S(2)}, u32[]{:S(2)}) collective-permute-start(f32[128,256]{1,0:T(8,128)S(1)} %get-tuple-element.51), channel_id=1, source_target_pairs={{0,8},{8,0},{16,24},{24,16},{1,9},{9,1},{17,25},{25,17},{2,10},{10... | collective-permute-start | bytes 393224 | tf_op jit(solution)/shard_map/ppermute | solution.py:55
  10.0 0.8 %collective-permute-done.3.top = f32[128,256]{1,0:T(8,128)S(1)} collective-permute-done((f32[128,256]{1,0:T(8,128)S(1)}, f32[128,256]{1,0:T(8,128)S(1)}, u32[]{:S(2)}, u32[]{:S(2)}) %collective-permute-start.3) | collective-permute-done | bytes 131104 | tf_op jit(solution)/shard_map/ppermute | solution.py:55
  10.8 0.2 collective-permute-done.4.bottom
  11.0 0.6 %shard_map.29 = (f32[256,256]{1,0:T(8,128)S(1)}, f32[256,256]{1,0:T(8,128)S(1)}, f32[256,256]{1,0:T(8,128)S(1)}) custom-call(f32[256,256]{1,0:T(8,128)S(1)} %shard_map.28.chip, f32[256,256]{1,0:T(8,128)S(1)} %collective-permute-done.2.by_x, f32[128,256]{1,0:T(8,128)S(1)} %collective-permute-done.3.top, f32[128,256]{1,0:T(8,128)S(1)} %collective-permute-done.4.bottom), custom_call_target="tpu_custom_call" | custom-call | flops 100663296 | tf_op jit(solution)/shard_map/pallas_call | solution.py:64
  11.6 2.1 %collective-permute-done.1.wide = f32[256,256]{1,0:T(8,128)S(1)} collective-permute-done((f32[256,256]{1,0:T(8,128)S(1)}, f32[256,256]{1,0:T(8,128)S(1)}, u32[]{:S(2)}, u32[]{:S(2)}) %collective-permute-start.1) | collective-permute-done | bytes 262176 | tf_op jit(solution)/shard_map/ppermute | solution.py:55
  13.7 0.3 %shard_map.31 = (f32[256,256]{1,0:T(8,128)S(1)}, f32[256,256]{1,0:T(8,128)S(1)}) custom-call(f32[256,256]{1,0:T(8,128)S(1)} %collective-permute-done.1.wide, f32[256,256]{1,0:T(8,128)S(1)} %get-tuple-element.32.close, f32[256,256]{1,0:T(8,128)S(1)} %get-tuple-element.37.near, f32[256,256]{1,0:T(8,128)S(1)} %get-tuple-element.38.three), custom_call_target="tpu_custom_call" | custom-call | flops 100663296 | tf_op jit(solution)/shard_map/pallas_call | solution.py:64
  14.0 2.7 %collective-permute-start.7 = (f32[256,256]{1,0:T(8,128)S(1)}, f32[256,256]{1,0:T(8,128)S(1)}, u32[]{:S(2)}, u32[]{:S(2)}) collective-permute-start(f32[256,256]{1,0:T(8,128)S(1)} %get-tuple-element.40), channel_id=1, source_target_pairs={{0,4},{8,9},{16,20},{24,25},{1,5},{9,8},{17,21},{25,24},{2,6},{10,... | collective-permute-start | bytes 786440 | tf_op jit(solution)/shard_map/ppermute | solution.py:55
  16.6 1.6 %collective-permute-start.6 = (f32[256,256]{1,0:T(8,128)S(1)}, f32[256,256]{1,0:T(8,128)S(1)}, u32[]{:S(2)}, u32[]{:S(2)}) collective-permute-start(f32[256,256]{1,0:T(8,128)S(1)} %get-tuple-element.39), channel_id=1, source_target_pairs={{0,2},{8,25},{16,18},{24,9},{1,3},{9,24},{17,19},{25,8},{2,0},{10,... | collective-permute-start | bytes 786440 | tf_op jit(solution)/shard_map/ppermute | solution.py:55
  18.2 1.3 %collective-permute-done.5.crossed = f32[256,256]{1,0:T(8,128)S(1)} collective-permute-done((f32[256,256]{1,0:T(8,128)S(1)}, f32[256,256]{1,0:T(8,128)S(1)}, u32[]{:S(2)}, u32[]{:S(2)}) %collective-permute-start.5) | collective-permute-done | bytes 262176 | tf_op jit(solution)/shard_map/ppermute | solution.py:55
  19.5 1.1 %shard_map.30 = (f32[256,256]{1,0:T(8,128)S(1)}, f32[256,256]{1,0:T(8,128)S(1)}) custom-call(f32[256,256]{1,0:T(8,128)S(1)} %broadcast_select_fusion.mine, f32[256,256]{1,0:T(8,128)S(1)} %collective-permute-done.other, f32[256,256]{1,0:T(8,128)S(1)} %shard_map.28.chip, f32[256,256]{1,0:T(8,128)S(1)} %get-tuple-element.32.close, ...), custom_call_target="tpu_custom_call" | custom-call | flops 301989888 | tf_op jit(solution)/shard_map/pallas_call | solution.py:64
  20.7 0.5 %collective-permute-start.9 = (f32[128,256]{1,0:T(8,128)S(1)}, f32[128,256]{1,0:T(8,128)S(1)}, u32[]{:S(2)}, u32[]{:S(2)}) collective-permute-start(f32[128,256]{1,0:T(8,128)S(1)} %get-tuple-element.43), channel_id=1, source_target_pairs={{0,8},{8,0},{16,24},{24,16},{1,9},{9,1},{17,25},{25,17},{2,10},{10... | collective-permute-start | bytes 393224 | tf_op jit(solution)/shard_map/ppermute | solution.py:55
  21.2 3.0 %collective-permute-done.7.value = f32[256,256]{1,0:T(8,128)S(1)} collective-permute-done((f32[256,256]{1,0:T(8,128)S(1)}, f32[256,256]{1,0:T(8,128)S(1)}, u32[]{:S(2)}, u32[]{:S(2)}) %collective-permute-start.7) | collective-permute-done | bytes 262176 | tf_op jit(solution)/shard_map/ppermute | solution.py:55
  24.3 0.3 %shard_map.34.near = f32[256,256]{1,0:T(8,128)S(1)} custom-call(f32[256,256]{1,0:T(8,128)S(1)} %collective-permute-done.5.crossed, f32[128,256]{1,0:T(8,128)S(1)} %collective-permute-done.8.top, f32[128,256]{1,0:T(8,128)S(1)} %collective-permute-done.9.bottom), custom_call_target="tpu_custom_call" | custom-call | flops 100663296 | tf_op jit(solution)/shard_map/pallas_call | solution.py:64
  24.7 0.2 collective-permute-start.11
  24.9 0.9 %shard_map.35 = (f32[256,256]{1,0:T(8,128)S(1)}, f32[256,256]{1,0:T(8,128)S(1)}) custom-call(f32[256,256]{1,0:T(8,128)S(1)} %get-tuple-element.35.after, f32[256,256]{1,0:T(8,128)S(1)} %get-tuple-element.36.wp, f32[256,256]{1,0:T(8,128)S(1)} %shard_map.34.near, f32[256,256]{1,0:T(8,128)S(1)} %collective-permute-done.1.wide, f32[256,256]{1,0:T(8,128)S(1)} %shard_map.32.by_d, ...), custom_call_target="tpu_custom_call" | custom-call | flops 402653184 | tf_op jit(solution)/shard_map/pallas_call | solution.py:64
  25.9 0.4 %shard_map.36 = (f32[256,256]{1,0:T(8,128)S(1)}, f32[256,256]{1,0:T(8,128)S(1)}) custom-call(f32[256,256]{1,0:T(8,128)S(1)} %get-tuple-element.47.a, f32[256,256]{1,0:T(8,128)S(1)} %get-tuple-element.48.b, f32[256,256]{1,0:T(8,128)S(1)} %collective-permute-done.10.come), custom_call_target="tpu_custom_call" | custom-call | flops 100663296 | tf_op jit(solution)/shard_map/pallas_call | solution.py:64
  26.2 1.3 %shard_map.37 = f32[256,256]{1,0:T(8,128)} custom-call(f32[256,256]{1,0:T(8,128)S(1)} %get-tuple-element.49.a, f32[256,256]{1,0:T(8,128)S(1)} %get-tuple-element.50.b, f32[256,256]{1,0:T(8,128)S(1)} %collective-permute-done.11.come), custom_call_target="tpu_custom_call" | custom-call | flops 201326592 | tf_op jit(solution)/shard_map/pallas_call | solution.py:64
  (14 shorter events, 0.3 us)
Async XLA Ops:
  0.0 1.8 %collective-permute-start = (f32[256,256]{1,0:T(8,128)}, f32[256,256]{1,0:T(8,128)S(1)}, u32[]{:S(2)}, u32[]{:S(2)}) collective-permute-start(f32[256,256]{1,0:T(8,128)} %bitcast.5), channel_id=1, source_target_pairs={{0,8},{8,0},{16,24},{24,16},{1,9},{9,1},{17,25},{25,17},{2,10},{10... | collective-permute-start | bytes 786440 | tf_op jit(solution)/shard_map/ppermute | solution.py:55
  2.1 7.3 %collective-permute-start.2 = (f32[256,256]{1,0:T(8,128)S(1)}, f32[256,256]{1,0:T(8,128)S(1)}, u32[]{:S(2)}, u32[]{:S(2)}) collective-permute-start(f32[256,256]{1,0:T(8,128)S(1)} %shard_map.28.chip), channel_id=1, source_target_pairs={{0,16},{8,9},{16,0},{24,25},{1,17},{9,8},{17,1},{25,24},{2,18},{10... | collective-permute-start | bytes 786440 | tf_op jit(solution)/shard_map/ppermute | solution.py:55
  5.0 8.6 %collective-permute-start.1 = (f32[256,256]{1,0:T(8,128)S(1)}, f32[256,256]{1,0:T(8,128)S(1)}, u32[]{:S(2)}, u32[]{:S(2)}) collective-permute-start(f32[256,256]{1,0:T(8,128)S(1)} %shard_map.28.chip), channel_id=1, source_target_pairs={{0,17},{8,14},{16,1},{24,30},{1,16},{9,15},{17,0},{25,31},{2,19},{... | collective-permute-start | bytes 786440 | tf_op jit(solution)/shard_map/ppermute | solution.py:55
  9.4 1.4 %collective-permute-start.3 = (f32[128,256]{1,0:T(8,128)S(1)}, f32[128,256]{1,0:T(8,128)S(1)}, u32[]{:S(2)}, u32[]{:S(2)}) collective-permute-start(f32[128,256]{1,0:T(8,128)S(1)} %get-tuple-element.52), channel_id=1, source_target_pairs={{0,8},{8,0},{16,24},{24,16},{1,9},{9,1},{17,25},{25,17},{2,10},{10... | collective-permute-start | bytes 393224 | tf_op jit(solution)/shard_map/ppermute | solution.py:55
  9.5 1.5 %collective-permute-start.4 = (f32[128,256]{1,0:T(8,128)S(1)}, f32[128,256]{1,0:T(8,128)S(1)}, u32[]{:S(2)}, u32[]{:S(2)}) collective-permute-start(f32[128,256]{1,0:T(8,128)S(1)} %get-tuple-element.51), channel_id=1, source_target_pairs={{0,8},{8,0},{16,24},{24,16},{1,9},{9,1},{17,25},{25,17},{2,10},{10... | collective-permute-start | bytes 393224 | tf_op jit(solution)/shard_map/ppermute | solution.py:55
  13.7 5.8 %copy-start = (f32[1,1,256,256]{3,2,1,0:T(8,128)S(1)}, f32[1,1,256,256]{3,2,1,0:T(8,128)}, u32[]{:S(2)}) copy-start(f32[1,1,256,256]{3,2,1,0:T(8,128)} %param.3) | copy-start | bytes 786436
  13.7 5.8 %collective-permute-start.5 = (f32[256,256]{1,0:T(8,128)S(1)}, f32[256,256]{1,0:T(8,128)S(1)}, u32[]{:S(2)}, u32[]{:S(2)}) collective-permute-start(f32[256,256]{1,0:T(8,128)S(1)} %collective-permute-done.1.wide), channel_id=1, source_target_pairs={{0,8},{8,16},{16,24},{24,0},{1,9},{9,17},{17,25},{25,1},{2,10},{10... | collective-permute-start | bytes 786440 | tf_op jit(solution)/shard_map/ppermute | solution.py:55
  14.0 10.3 %collective-permute-start.7 = (f32[256,256]{1,0:T(8,128)S(1)}, f32[256,256]{1,0:T(8,128)S(1)}, u32[]{:S(2)}, u32[]{:S(2)}) collective-permute-start(f32[256,256]{1,0:T(8,128)S(1)} %get-tuple-element.40), channel_id=1, source_target_pairs={{0,4},{8,9},{16,20},{24,25},{1,5},{9,8},{17,21},{25,24},{2,6},{10,... | collective-permute-start | bytes 786440 | tf_op jit(solution)/shard_map/ppermute | solution.py:55
  16.6 8.1 %collective-permute-start.6 = (f32[256,256]{1,0:T(8,128)S(1)}, f32[256,256]{1,0:T(8,128)S(1)}, u32[]{:S(2)}, u32[]{:S(2)}) collective-permute-start(f32[256,256]{1,0:T(8,128)S(1)} %get-tuple-element.39), channel_id=1, source_target_pairs={{0,2},{8,25},{16,18},{24,9},{1,3},{9,24},{17,19},{25,8},{2,0},{10,... | collective-permute-start | bytes 786440 | tf_op jit(solution)/shard_map/ppermute | solution.py:55
  20.7 3.6 %collective-permute-start.8 = (f32[128,256]{1,0:T(8,128)S(1)}, f32[128,256]{1,0:T(8,128)S(1)}, u32[]{:S(2)}, u32[]{:S(2)}) collective-permute-start(f32[128,256]{1,0:T(8,128)S(1)} %get-tuple-element.42), channel_id=1, source_target_pairs={{0,8},{8,0},{16,24},{24,16},{1,9},{9,1},{17,25},{25,17},{2,10},{10... | collective-permute-start | bytes 393224 | tf_op jit(solution)/shard_map/ppermute | solution.py:55
  20.7 3.5 %collective-permute-start.9 = (f32[128,256]{1,0:T(8,128)S(1)}, f32[128,256]{1,0:T(8,128)S(1)}, u32[]{:S(2)}, u32[]{:S(2)}) collective-permute-start(f32[128,256]{1,0:T(8,128)S(1)} %get-tuple-element.43), channel_id=1, source_target_pairs={{0,8},{8,0},{16,24},{24,16},{1,9},{9,1},{17,25},{25,17},{2,10},{10... | collective-permute-start | bytes 393224 | tf_op jit(solution)/shard_map/ppermute | solution.py:55
  24.2 1.6 %collective-permute-start.10 = (f32[256,256]{1,0:T(8,128)S(1)}, f32[256,256]{1,0:T(8,128)S(1)}, u32[]{:S(2)}, u32[]{:S(2)}) collective-permute-start(f32[256,256]{1,0:T(8,128)S(1)} %collective-permute-done.7.value), channel_id=1, source_target_pairs={{0,8},{8,0},{16,24},{24,16},{1,9},{9,1},{17,25},{25,17},{2,10},{10... | collective-permute-start | bytes 786440 | tf_op jit(solution)/shard_map/ppermute | solution.py:55
  24.7 1.5 %collective-permute-start.11 = (f32[256,256]{1,0:T(8,128)S(1)}, f32[256,256]{1,0:T(8,128)S(1)}, u32[]{:S(2)}, u32[]{:S(2)}) collective-permute-start(f32[256,256]{1,0:T(8,128)S(1)} %collective-permute-done.6.by_y), channel_id=1, source_target_pairs={{0,8},{8,0},{16,24},{24,16},{1,9},{9,1},{17,25},{25,17},{2,10},{10... | collective-permute-start | bytes 786440 | tf_op jit(solution)/shard_map/ppermute | solution.py:55

commit v7 on v6

--- a/solution.py
+++ b/solution.py
@@ -206,7 +206,7 @@
     def four_side():
         two, one = by_d, by_y
 
-        @pl.when(jnp.logical_not(odd))
+        @pl.when(jnp.logical_not(odd) & (upper | near_left))
         def _():
             held[...] = mul(one[...], after[...])
 
@@ -235,29 +235,36 @@
             when(near_left, left, right)
 
         def late():
+            def right():
+                b[...] = mul_tn(near[...], b[...])
+
+            def left():
+                a[...] = mul_nt(a[...], near[...])
+
             def odd_four():
                 a[...] = after[...].T
                 b[...] = mul_tn(two[...], mul(wp[...], one[...]))
+                when(near_left, right, left)
+
+            def even_right():
+                b[...] = mul_tn(near[...], wp[...])
+                a[...] = mul(two[...], held[...]).T
+
+            def even_left():
+                b[...] = wp[...]
+                a[...] = mul(mul(near[...], two[...]), mul(one[...], after[...])).T
 
             def even_four():
-                a[...] = mul(two[...], held[...]).T
-                b[...] = wp[...]
+                when(near_left, even_right, even_left)
 
             when(odd, odd_four, even_four)
 
-            def right():
-                b[...] = mul_tn(near[...], b[...])
-
-            def left():
-                a[...] = mul_nt(a[...], near[...])
-
-            when(near_left, right, left)
-
         when(upper, early, late)
 
     def opposite_side():
-        in_order(group.bit(1), held, by_d, by_y)
-        in_order(group.bit(1), opposite, wide, near)
+        x_bit = group.bit(1)
+        held[...] = mul(*ordered(x_bit, by_d[...], by_y[...]))
+        opposite[...] = mul(*ordered(x_bit, wide[...], near[...]))
         in_order(near_left, three, opposite, held)
 
         def early():

time: 27.8 us -> 27.7 us (level)
  transfers between devices with their start and end apart: 12 -> 12, of which waited for: 8 -> 9; matrix products, arithmetic and copies ran while one was open for 4% -> 4% of each run, Pallas kernels for 13% -> 13%
where the time goes in v7:
time: 27.7 us; the launch traced here: 27.5 us
  waiting for transfers between devices  10.8 us (39%)
  starting transfers between devices  10.4 us (38%)
  Pallas kernels  5.16 us (19%)
  other arithmetic  0.97 us (4%)
    ppermute x12, waiting for transfers between devices, send(): return lax.ppermute(value, ('inner', 'outer'), pairs)  10.8 us
    ppermute x12, starting transfers between devices, send(): return lax.ppermute(value, ('inner', 'outer'), pairs)  10.4 us
    pallas_call x10, Pallas kernels, run(): pl.pallas_call(functools.partial(body, group), out_shape=[jax.ShapeDtypeS...  5.16 us
    select_n x1, other arithmetic, body(): jnp.where(lax.axis_index('inner') < n_in, mine, 0.0)  0.97 us
  transfers between devices with their start and end apart: 12, of which 9 were waited for; matrix products, arithmetic and copies ran while one was open for 4% of the time, Pallas kernels for 13%

profile of v7, /device:TPU:0, one launch (start us, length us, event | category | flops | bytes accessed | tf_op | source)
XLA Modules:
  0.0 27.5 jit_solution(2199110430085962282)
XLA Ops:
  0.0 0.5 %collective-permute-start = (f32[256,256]{1,0:T(8,128)}, f32[256,256]{1,0:T(8,128)S(1)}, u32[]{:S(2)}, u32[]{:S(2)}) collective-permute-start(f32[256,256]{1,0:T(8,128)} %bitcast.5), channel_id=1, source_target_pairs={{0,8},{8,0},{16,24},{24,16},{1,9},{9,1},{17,25},{25,17},{2,10},{10... | collective-permute-start | bytes 786440 | tf_op jit(solution)/shard_map/ppermute | solution.py:55
  0.5 1.0 %broadcast_select_fusion.mine = f32[256,256]{1,0:T(8,128)S(1)} fusion(pred[]{:T(512)S(6)} %lt.3, f32[1,1,256,256]{3,2,1,0:T(8,128)} %param.2), kind=kLoop, calls=%fused_computation | loop fusion | flops 65536 | bytes 524289 | tf_op jit(solution)/shard_map/jit(_where)/select_n | solution.py:393
  1.4 0.4 %collective-permute-done.other = f32[256,256]{1,0:T(8,128)S(1)} collective-permute-done((f32[256,256]{1,0:T(8,128)}, f32[256,256]{1,0:T(8,128)S(1)}, u32[]{:S(2)}, u32[]{:S(2)}) %collective-permute-start) | collective-permute-done | bytes 262176 | tf_op jit(solution)/shard_map/ppermute | solution.py:55
  1.8 0.3 shard_map.28.chip
  2.1 2.9 %collective-permute-start.2 = (f32[256,256]{1,0:T(8,128)S(1)}, f32[256,256]{1,0:T(8,128)S(1)}, u32[]{:S(2)}, u32[]{:S(2)}) collective-permute-start(f32[256,256]{1,0:T(8,128)S(1)} %shard_map.28.chip), channel_id=1, source_target_pairs={{0,16},{8,9},{16,0},{24,25},{1,17},{9,8},{17,1},{25,24},{2,18},{10... | collective-permute-start | bytes 786440 | tf_op jit(solution)/shard_map/ppermute | solution.py:55
  5.0 1.5 %collective-permute-start.1 = (f32[256,256]{1,0:T(8,128)S(1)}, f32[256,256]{1,0:T(8,128)S(1)}, u32[]{:S(2)}, u32[]{:S(2)}) collective-permute-start(f32[256,256]{1,0:T(8,128)S(1)} %shard_map.28.chip), channel_id=1, source_target_pairs={{0,17},{8,14},{16,1},{24,30},{1,16},{9,15},{17,0},{25,31},{2,19},{... | collective-permute-start | bytes 786440 | tf_op jit(solution)/shard_map/ppermute | solution.py:55
  6.5 2.9 %collective-permute-done.2.by_x = f32[256,256]{1,0:T(8,128)S(1)} collective-permute-done((f32[256,256]{1,0:T(8,128)S(1)}, f32[256,256]{1,0:T(8,128)S(1)}, u32[]{:S(2)}, u32[]{:S(2)}) %collective-permute-start.2) | collective-permute-done | bytes 262176 | tf_op jit(solution)/shard_map/ppermute | solution.py:55
  9.5 0.5 %collective-permute-start.4 = (f32[128,256]{1,0:T(8,128)S(1)}, f32[128,256]{1,0:T(8,128)S(1)}, u32[]{:S(2)}, u32[]{:S(2)}) collective-permute-start(f32[128,256]{1,0:T(8,128)S(1)} %get-tuple-element.51), channel_id=1, source_target_pairs={{0,8},{8,0},{16,24},{24,16},{1,9},{9,1},{17,25},{25,17},{2,10},{10... | collective-permute-start | bytes 393224 | tf_op jit(solution)/shard_map/ppermute | solution.py:55
  10.0 0.8 %collective-permute-done.3.top = f32[128,256]{1,0:T(8,128)S(1)} collective-permute-done((f32[128,256]{1,0:T(8,128)S(1)}, f32[128,256]{1,0:T(8,128)S(1)}, u32[]{:S(2)}, u32[]{:S(2)}) %collective-permute-start.3) | collective-permute-done | bytes 131104 | tf_op jit(solution)/shard_map/ppermute | solution.py:55
  10.8 0.2 collective-permute-done.4.bottom
  11.0 0.6 %shard_map.29 = (f32[256,256]{1,0:T(8,128)S(1)}, f32[256,256]{1,0:T(8,128)S(1)}, f32[256,256]{1,0:T(8,128)S(1)}) custom-call(f32[256,256]{1,0:T(8,128)S(1)} %shard_map.28.chip, f32[256,256]{1,0:T(8,128)S(1)} %collective-permute-done.2.by_x, f32[128,256]{1,0:T(8,128)S(1)} %collective-permute-done.3.top, f32[128,256]{1,0:T(8,128)S(1)} %collective-permute-done.4.bottom), custom_call_target="tpu_custom_call" | custom-call | flops 100663296 | tf_op jit(solution)/shard_map/pallas_call | solution.py:64
  11.6 2.1 %collective-permute-done.1.wide = f32[256,256]{1,0:T(8,128)S(1)} collective-permute-done((f32[256,256]{1,0:T(8,128)S(1)}, f32[256,256]{1,0:T(8,128)S(1)}, u32[]{:S(2)}, u32[]{:S(2)}) %collective-permute-start.1) | collective-permute-done | bytes 262176 | tf_op jit(solution)/shard_map/ppermute | solution.py:55
  13.7 0.3 %shard_map.31 = (f32[256,256]{1,0:T(8,128)S(1)}, f32[256,256]{1,0:T(8,128)S(1)}) custom-call(f32[256,256]{1,0:T(8,128)S(1)} %collective-permute-done.1.wide, f32[256,256]{1,0:T(8,128)S(1)} %get-tuple-element.32.close, f32[256,256]{1,0:T(8,128)S(1)} %get-tuple-element.37.near, f32[256,256]{1,0:T(8,128)S(1)} %get-tuple-element.38.three), custom_call_target="tpu_custom_call" | custom-call | flops 100663296 | tf_op jit(solution)/shard_map/pallas_call | solution.py:64
  14.0 2.7 %collective-permute-start.7 = (f32[256,256]{1,0:T(8,128)S(1)}, f32[256,256]{1,0:T(8,128)S(1)}, u32[]{:S(2)}, u32[]{:S(2)}) collective-permute-start(f32[256,256]{1,0:T(8,128)S(1)} %get-tuple-element.40), channel_id=1, source_target_pairs={{0,4},{8,9},{16,20},{24,25},{1,5},{9,8},{17,21},{25,24},{2,6},{10,... | collective-permute-start | bytes 786440 | tf_op jit(solution)/shard_map/ppermute | solution.py:55
  16.6 1.6 %collective-permute-start.6 = (f32[256,256]{1,0:T(8,128)S(1)}, f32[256,256]{1,0:T(8,128)S(1)}, u32[]{:S(2)}, u32[]{:S(2)}) collective-permute-start(f32[256,256]{1,0:T(8,128)S(1)} %get-tuple-element.39), channel_id=1, source_target_pairs={{0,2},{8,25},{16,18},{24,9},{1,3},{9,24},{17,19},{25,8},{2,0},{10,... | collective-permute-start | bytes 786440 | tf_op jit(solution)/shard_map/ppermute | solution.py:55
  18.2 1.3 %collective-permute-done.5.crossed = f32[256,256]{1,0:T(8,128)S(1)} collective-permute-done((f32[256,256]{1,0:T(8,128)S(1)}, f32[256,256]{1,0:T(8,128)S(1)}, u32[]{:S(2)}, u32[]{:S(2)}) %collective-permute-start.5) | collective-permute-done | bytes 262176 | tf_op jit(solution)/shard_map/ppermute | solution.py:55
  19.5 1.1 %shard_map.30 = (f32[256,256]{1,0:T(8,128)S(1)}, f32[256,256]{1,0:T(8,128)S(1)}) custom-call(f32[256,256]{1,0:T(8,128)S(1)} %broadcast_select_fusion.mine, f32[256,256]{1,0:T(8,128)S(1)} %collective-permute-done.other, f32[256,256]{1,0:T(8,128)S(1)} %shard_map.28.chip, f32[256,256]{1,0:T(8,128)S(1)} %get-tuple-element.32.close, ...), custom_call_target="tpu_custom_call" | custom-call | flops 301989888 | tf_op jit(solution)/shard_map/pallas_call | solution.py:64
  20.7 0.5 %collective-permute-start.9 = (f32[128,256]{1,0:T(8,128)S(1)}, f32[128,256]{1,0:T(8,128)S(1)}, u32[]{:S(2)}, u32[]{:S(2)}) collective-permute-start(f32[128,256]{1,0:T(8,128)S(1)} %get-tuple-element.43), channel_id=1, source_target_pairs={{0,8},{8,0},{16,24},{24,16},{1,9},{9,1},{17,25},{25,17},{2,10},{10... | collective-permute-start | bytes 393224 | tf_op jit(solution)/shard_map/ppermute | solution.py:55
  21.2 3.0 %collective-permute-done.7.value = f32[256,256]{1,0:T(8,128)S(1)} collective-permute-done((f32[256,256]{1,0:T(8,128)S(1)}, f32[256,256]{1,0:T(8,128)S(1)}, u32[]{:S(2)}, u32[]{:S(2)}) %collective-permute-start.7) | collective-permute-done | bytes 262176 | tf_op jit(solution)/shard_map/ppermute | solution.py:55
  24.3 0.3 %shard_map.34.near = f32[256,256]{1,0:T(8,128)S(1)} custom-call(f32[256,256]{1,0:T(8,128)S(1)} %collective-permute-done.5.crossed, f32[128,256]{1,0:T(8,128)S(1)} %collective-permute-done.8.top, f32[128,256]{1,0:T(8,128)S(1)} %collective-permute-done.9.bottom), custom_call_target="tpu_custom_call" | custom-call | flops 100663296 | tf_op jit(solution)/shard_map/pallas_call | solution.py:64
  24.7 0.2 collective-permute-start.11
  24.9 0.9 %shard_map.35 = (f32[256,256]{1,0:T(8,128)S(1)}, f32[256,256]{1,0:T(8,128)S(1)}) custom-call(f32[256,256]{1,0:T(8,128)S(1)} %get-tuple-element.35.after, f32[256,256]{1,0:T(8,128)S(1)} %get-tuple-element.36.wp, f32[256,256]{1,0:T(8,128)S(1)} %shard_map.34.near, f32[256,256]{1,0:T(8,128)S(1)} %collective-permute-done.1.wide, f32[256,256]{1,0:T(8,128)S(1)} %shard_map.32.by_d, ...), custom_call_target="tpu_custom_call" | custom-call | flops 402653184 | tf_op jit(solution)/shard_map/pallas_call | solution.py:64
  25.8 0.4 %shard_map.36 = (f32[256,256]{1,0:T(8,128)S(1)}, f32[256,256]{1,0:T(8,128)S(1)}) custom-call(f32[256,256]{1,0:T(8,128)S(1)} %get-tuple-element.47.a, f32[256,256]{1,0:T(8,128)S(1)} %get-tuple-element.48.b, f32[256,256]{1,0:T(8,128)S(1)} %collective-permute-done.10.come), custom_call_target="tpu_custom_call" | custom-call | flops 100663296 | tf_op jit(solution)/shard_map/pallas_call | solution.py:64
  26.2 1.3 %shard_map.37 = f32[256,256]{1,0:T(8,128)} custom-call(f32[256,256]{1,0:T(8,128)S(1)} %get-tuple-element.49.a, f32[256,256]{1,0:T(8,128)S(1)} %get-tuple-element.50.b, f32[256,256]{1,0:T(8,128)S(1)} %collective-permute-done.11.come), custom_call_target="tpu_custom_call" | custom-call | flops 201326592 | tf_op jit(solution)/shard_map/pallas_call | solution.py:64
  (14 shorter events, 0.4 us)
Async XLA Ops:
  0.0 1.8 %collective-permute-start = (f32[256,256]{1,0:T(8,128)}, f32[256,256]{1,0:T(8,128)S(1)}, u32[]{:S(2)}, u32[]{:S(2)}) collective-permute-start(f32[256,256]{1,0:T(8,128)} %bitcast.5), channel_id=1, source_target_pairs={{0,8},{8,0},{16,24},{24,16},{1,9},{9,1},{17,25},{25,17},{2,10},{10... | collective-permute-start | bytes 786440 | tf_op jit(solution)/shard_map/ppermute | solution.py:55
  2.1 7.3 %collective-permute-start.2 = (f32[256,256]{1,0:T(8,128)S(1)}, f32[256,256]{1,0:T(8,128)S(1)}, u32[]{:S(2)}, u32[]{:S(2)}) collective-permute-start(f32[256,256]{1,0:T(8,128)S(1)} %shard_map.28.chip), channel_id=1, source_target_pairs={{0,16},{8,9},{16,0},{24,25},{1,17},{9,8},{17,1},{25,24},{2,18},{10... | collective-permute-start | bytes 786440 | tf_op jit(solution)/shard_map/ppermute | solution.py:55
  5.0 8.6 %collective-permute-start.1 = (f32[256,256]{1,0:T(8,128)S(1)}, f32[256,256]{1,0:T(8,128)S(1)}, u32[]{:S(2)}, u32[]{:S(2)}) collective-permute-start(f32[256,256]{1,0:T(8,128)S(1)} %shard_map.28.chip), channel_id=1, source_target_pairs={{0,17},{8,14},{16,1},{24,30},{1,16},{9,15},{17,0},{25,31},{2,19},{... | collective-permute-start | bytes 786440 | tf_op jit(solution)/shard_map/ppermute | solution.py:55
  9.4 1.4 %collective-permute-start.3 = (f32[128,256]{1,0:T(8,128)S(1)}, f32[128,256]{1,0:T(8,128)S(1)}, u32[]{:S(2)}, u32[]{:S(2)}) collective-permute-start(f32[128,256]{1,0:T(8,128)S(1)} %get-tuple-element.52), channel_id=1, source_target_pairs={{0,8},{8,0},{16,24},{24,16},{1,9},{9,1},{17,25},{25,17},{2,10},{10... | collective-permute-start | bytes 393224 | tf_op jit(solution)/shard_map/ppermute | solution.py:55
  9.5 1.5 %collective-permute-start.4 = (f32[128,256]{1,0:T(8,128)S(1)}, f32[128,256]{1,0:T(8,128)S(1)}, u32[]{:S(2)}, u32[]{:S(2)}) collective-permute-start(f32[128,256]{1,0:T(8,128)S(1)} %get-tuple-element.51), channel_id=1, source_target_pairs={{0,8},{8,0},{16,24},{24,16},{1,9},{9,1},{17,25},{25,17},{2,10},{10... | collective-permute-start | bytes 393224 | tf_op jit(solution)/shard_map/ppermute | solution.py:55
  13.7 5.8 %copy-start = (f32[1,1,256,256]{3,2,1,0:T(8,128)S(1)}, f32[1,1,256,256]{3,2,1,0:T(8,128)}, u32[]{:S(2)}) copy-start(f32[1,1,256,256]{3,2,1,0:T(8,128)} %param.3) | copy-start | bytes 786436
  13.7 5.8 %collective-permute-start.5 = (f32[256,256]{1,0:T(8,128)S(1)}, f32[256,256]{1,0:T(8,128)S(1)}, u32[]{:S(2)}, u32[]{:S(2)}) collective-permute-start(f32[256,256]{1,0:T(8,128)S(1)} %collective-permute-done.1.wide), channel_id=1, source_target_pairs={{0,8},{8,16},{16,24},{24,0},{1,9},{9,17},{17,25},{25,1},{2,10},{10... | collective-permute-start | bytes 786440 | tf_op jit(solution)/shard_map/ppermute | solution.py:55
  14.0 10.3 %collective-permute-start.7 = (f32[256,256]{1,0:T(8,128)S(1)}, f32[256,256]{1,0:T(8,128)S(1)}, u32[]{:S(2)}, u32[]{:S(2)}) collective-permute-start(f32[256,256]{1,0:T(8,128)S(1)} %get-tuple-element.40), channel_id=1, source_target_pairs={{0,4},{8,9},{16,20},{24,25},{1,5},{9,8},{17,21},{25,24},{2,6},{10,... | collective-permute-start | bytes 786440 | tf_op jit(solution)/shard_map/ppermute | solution.py:55
  16.6 8.1 %collective-permute-start.6 = (f32[256,256]{1,0:T(8,128)S(1)}, f32[256,256]{1,0:T(8,128)S(1)}, u32[]{:S(2)}, u32[]{:S(2)}) collective-permute-start(f32[256,256]{1,0:T(8,128)S(1)} %get-tuple-element.39), channel_id=1, source_target_pairs={{0,2},{8,25},{16,18},{24,9},{1,3},{9,24},{17,19},{25,8},{2,0},{10,... | collective-permute-start | bytes 786440 | tf_op jit(solution)/shard_map/ppermute | solution.py:55
  20.7 3.6 %collective-permute-start.8 = (f32[128,256]{1,0:T(8,128)S(1)}, f32[128,256]{1,0:T(8,128)S(1)}, u32[]{:S(2)}, u32[]{:S(2)}) collective-permute-start(f32[128,256]{1,0:T(8,128)S(1)} %get-tuple-element.42), channel_id=1, source_target_pairs={{0,8},{8,0},{16,24},{24,16},{1,9},{9,1},{17,25},{25,17},{2,10},{10... | collective-permute-start | bytes 393224 | tf_op jit(solution)/shard_map/ppermute | solution.py:55
  20.7 3.5 %collective-permute-start.9 = (f32[128,256]{1,0:T(8,128)S(1)}, f32[128,256]{1,0:T(8,128)S(1)}, u32[]{:S(2)}, u32[]{:S(2)}) collective-permute-start(f32[128,256]{1,0:T(8,128)S(1)} %get-tuple-element.43), channel_id=1, source_target_pairs={{0,8},{8,0},{16,24},{24,16},{1,9},{9,1},{17,25},{25,17},{2,10},{10... | collective-permute-start | bytes 393224 | tf_op jit(solution)/shard_map/ppermute | solution.py:55
  24.2 1.5 %collective-permute-start.10 = (f32[256,256]{1,0:T(8,128)S(1)}, f32[256,256]{1,0:T(8,128)S(1)}, u32[]{:S(2)}, u32[]{:S(2)}) collective-permute-start(f32[256,256]{1,0:T(8,128)S(1)} %collective-permute-done.7.value), channel_id=1, source_target_pairs={{0,8},{8,0},{16,24},{24,16},{1,9},{9,1},{17,25},{25,17},{2,10},{10... | collective-permute-start | bytes 786440 | tf_op jit(solution)/shard_map/ppermute | solution.py:55
  24.7 1.5 %collective-permute-start.11 = (f32[256,256]{1,0:T(8,128)S(1)}, f32[256,256]{1,0:T(8,128)S(1)}, u32[]{:S(2)}, u32[]{:S(2)}) collective-permute-start(f32[256,256]{1,0:T(8,128)S(1)} %collective-permute-done.6.by_y), channel_id=1, source_target_pairs={{0,8},{8,0},{16,24},{24,16},{1,9},{9,1},{17,25},{25,17},{2,10},{10... | collective-permute-start | bytes 786440 | tf_op jit(solution)/shard_map/ppermute | solution.py:55

commit v8 on v7

--- a/solution.py
+++ b/solution.py
@@ -263,7 +263,7 @@
 
     def opposite_side():
         x_bit = group.bit(1)
-        held[...] = mul(*ordered(x_bit, by_d[...], by_y[...]))
+        held[...] = mul(*ordered(x_bit, by_y[...], by_d[...]))
         opposite[...] = mul(*ordered(x_bit, wide[...], near[...]))
         in_order(near_left, three, opposite, held)
 
@@ -296,7 +296,7 @@
 
 def closer_kernel(group, a, b, come, new_a, new_b):
     first, x_bit, near_left, odd, upper = (group.bit(k) for k in range(5))
-    second, x_bit = jnp.logical_not(first), jnp.logical_not(x_bit)
+    second = jnp.logical_not(first)
     new_a[...] = a[...]
     new_b[...] = b[...]
 
@@ -347,7 +347,7 @@
 
 def result_kernel(group, a, b, come, result, mid):
     first, x_bit, near_left, odd, upper = (group.bit(k) for k in range(5))
-    second, x_bit = jnp.logical_not(first), jnp.logical_not(x_bit)
+    second = jnp.logical_not(first)
     plain = jnp.where(second, upper, odd)
     alone = odd & jnp.where(second, upper & near_left & jnp.logical_not(x_bit), jnp.logical_not(upper))
 
@@ -398,7 +398,7 @@
     wide, near, three, close = lax.optimization_barrier((wide, near, three, close))
     crossed = group.send(wide, 1, 3)
     four, to_y = run(four_kernel, group, [square] * 2, wide, close, near, three, scratch=[square])
-    by_d, far_y = group.send(four, 16, 4), group.send(to_y, 8, 6)
+    by_d, far_y = group.send(four, 16, 6), group.send(to_y, 8, 4)
     after, wp = run(
         own_kernel,
         group,
@@ -417,7 +417,7 @@
     if bits > 5:
         second = jnp.logical_not(group.bit(0))
         one, two = jnp.where(second, by_y, their_y), jnp.where(second, by_d, their_d)
-        far = dot(*ordered(group.bit(1), jnp.where(second, their_d, by_d), jnp.where(second, their_y, by_y)))
+        far = dot(*ordered(group.bit(1), jnp.where(second, their_y, by_y), jnp.where(second, their_d, by_d)))
         near = jnp.where(second, near, dot(*ordered(group.bit(1), wide, near)))
         three = dot(*ordered(group.bit(2), near, far))
         four = jnp.where(second, four, group.swap(four, 1))

time: 27.7 us -> 27.7 us (level)
  no operation moved by 1% of the time
where the time goes in v8:
time: 27.7 us; the launch traced here: 27.5 us
  waiting for transfers between devices  10.8 us (39%)
  starting transfers between devices  10.4 us (38%)
  Pallas kernels  5.16 us (19%)
  other arithmetic  0.97 us (4%)
    ppermute x12, waiting for transfers between devices, send(): return lax.ppermute(value, ('inner', 'outer'), pairs)  10.8 us
    ppermute x12, starting transfers between devices, send(): return lax.ppermute(value, ('inner', 'outer'), pairs)  10.4 us
    pallas_call x10, Pallas kernels, run(): pl.pallas_call(functools.partial(body, group), out_shape=[jax.ShapeDtypeS...  5.16 us
    select_n x1, other arithmetic, body(): jnp.where(lax.axis_index('inner') < n_in, mine, 0.0)  0.97 us
  transfers between devices with their start and end apart: 12, of which 9 were waited for; matrix products, arithmetic and copies ran while one was open for 4% of the time, Pallas kernels for 13%

profile of v8, /device:TPU:0, one launch (start us, length us, event | category | flops | bytes accessed | tf_op | source)
XLA Modules:
  0.0 27.5 jit_solution(15073482282379256898)
XLA Ops:
  0.0 0.5 %collective-permute-start = (f32[256,256]{1,0:T(8,128)}, f32[256,256]{1,0:T(8,128)S(1)}, u32[]{:S(2)}, u32[]{:S(2)}) collective-permute-start(f32[256,256]{1,0:T(8,128)} %bitcast.5), channel_id=1, source_target_pairs={{0,8},{8,0},{16,24},{24,16},{1,9},{9,1},{17,25},{25,17},{2,10},{10... | collective-permute-start | bytes 786440 | tf_op jit(solution)/shard_map/ppermute | solution.py:55
  0.5 1.0 %broadcast_select_fusion.mine = f32[256,256]{1,0:T(8,128)S(1)} fusion(pred[]{:T(512)S(6)} %lt.3, f32[1,1,256,256]{3,2,1,0:T(8,128)} %param.2), kind=kLoop, calls=%fused_computation | loop fusion | flops 65536 | bytes 524289 | tf_op jit(solution)/shard_map/jit(_where)/select_n | solution.py:393
  1.4 0.4 %collective-permute-done.other = f32[256,256]{1,0:T(8,128)S(1)} collective-permute-done((f32[256,256]{1,0:T(8,128)}, f32[256,256]{1,0:T(8,128)S(1)}, u32[]{:S(2)}, u32[]{:S(2)}) %collective-permute-start) | collective-permute-done | bytes 262176 | tf_op jit(solution)/shard_map/ppermute | solution.py:55
  1.8 0.3 shard_map.28.chip
  2.1 2.9 %collective-permute-start.2 = (f32[256,256]{1,0:T(8,128)S(1)}, f32[256,256]{1,0:T(8,128)S(1)}, u32[]{:S(2)}, u32[]{:S(2)}) collective-permute-start(f32[256,256]{1,0:T(8,128)S(1)} %shard_map.28.chip), channel_id=1, source_target_pairs={{0,16},{8,9},{16,0},{24,25},{1,17},{9,8},{17,1},{25,24},{2,18},{10... | collective-permute-start | bytes 786440 | tf_op jit(solution)/shard_map/ppermute | solution.py:55
  5.0 1.5 %collective-permute-start.1 = (f32[256,256]{1,0:T(8,128)S(1)}, f32[256,256]{1,0:T(8,128)S(1)}, u32[]{:S(2)}, u32[]{:S(2)}) collective-permute-start(f32[256,256]{1,0:T(8,128)S(1)} %shard_map.28.chip), channel_id=1, source_target_pairs={{0,17},{8,14},{16,1},{24,30},{1,16},{9,15},{17,0},{25,31},{2,19},{... | collective-permute-start | bytes 786440 | tf_op jit(solution)/shard_map/ppermute | solution.py:55
  6.5 2.9 %collective-permute-done.2.by_x = f32[256,256]{1,0:T(8,128)S(1)} collective-permute-done((f32[256,256]{1,0:T(8,128)S(1)}, f32[256,256]{1,0:T(8,128)S(1)}, u32[]{:S(2)}, u32[]{:S(2)}) %collective-permute-start.2) | collective-permute-done | bytes 262176 | tf_op jit(solution)/shard_map/ppermute | solution.py:55
  9.5 0.5 %collective-permute-start.4 = (f32[128,256]{1,0:T(8,128)S(1)}, f32[128,256]{1,0:T(8,128)S(1)}, u32[]{:S(2)}, u32[]{:S(2)}) collective-permute-start(f32[128,256]{1,0:T(8,128)S(1)} %get-tuple-element.51), channel_id=1, source_target_pairs={{0,8},{8,0},{16,24},{24,16},{1,9},{9,1},{17,25},{25,17},{2,10},{10... | collective-permute-start | bytes 393224 | tf_op jit(solution)/shard_map/ppermute | solution.py:55
  10.0 0.8 %collective-permute-done.3.top = f32[128,256]{1,0:T(8,128)S(1)} collective-permute-done((f32[128,256]{1,0:T(8,128)S(1)}, f32[128,256]{1,0:T(8,128)S(1)}, u32[]{:S(2)}, u32[]{:S(2)}) %collective-permute-start.3) | collective-permute-done | bytes 131104 | tf_op jit(solution)/shard_map/ppermute | solution.py:55
  10.8 0.2 collective-permute-done.4.bottom
  11.0 0.6 %shard_map.29 = (f32[256,256]{1,0:T(8,128)S(1)}, f32[256,256]{1,0:T(8,128)S(1)}, f32[256,256]{1,0:T(8,128)S(1)}) custom-call(f32[256,256]{1,0:T(8,128)S(1)} %shard_map.28.chip, f32[256,256]{1,0:T(8,128)S(1)} %collective-permute-done.2.by_x, f32[128,256]{1,0:T(8,128)S(1)} %collective-permute-done.3.top, f32[128,256]{1,0:T(8,128)S(1)} %collective-permute-done.4.bottom), custom_call_target="tpu_custom_call" | custom-call | flops 100663296 | tf_op jit(solution)/shard_map/pallas_call | solution.py:64
  11.6 2.1 %collective-permute-done.1.wide = f32[256,256]{1,0:T(8,128)S(1)} collective-permute-done((f32[256,256]{1,0:T(8,128)S(1)}, f32[256,256]{1,0:T(8,128)S(1)}, u32[]{:S(2)}, u32[]{:S(2)}) %collective-permute-start.1) | collective-permute-done | bytes 262176 | tf_op jit(solution)/shard_map/ppermute | solution.py:55
  13.7 0.3 %shard_map.31 = (f32[256,256]{1,0:T(8,128)S(1)}, f32[256,256]{1,0:T(8,128)S(1)}) custom-call(f32[256,256]{1,0:T(8,128)S(1)} %collective-permute-done.1.wide, f32[256,256]{1,0:T(8,128)S(1)} %get-tuple-element.32.close, f32[256,256]{1,0:T(8,128)S(1)} %get-tuple-element.37.near, f32[256,256]{1,0:T(8,128)S(1)} %get-tuple-element.38.three), custom_call_target="tpu_custom_call" | custom-call | flops 100663296 | tf_op jit(solution)/shard_map/pallas_call | solution.py:64
  14.0 2.7 %collective-permute-start.7 = (f32[256,256]{1,0:T(8,128)S(1)}, f32[256,256]{1,0:T(8,128)S(1)}, u32[]{:S(2)}, u32[]{:S(2)}) collective-permute-start(f32[256,256]{1,0:T(8,128)S(1)} %get-tuple-element.40), channel_id=1, source_target_pairs={{0,4},{8,25},{16,20},{24,9},{1,5},{9,24},{17,21},{25,8},{2,6},{10,... | collective-permute-start | bytes 786440 | tf_op jit(solution)/shard_map/ppermute | solution.py:55
  16.6 1.6 %collective-permute-start.6 = (f32[256,256]{1,0:T(8,128)S(1)}, f32[256,256]{1,0:T(8,128)S(1)}, u32[]{:S(2)}, u32[]{:S(2)}) collective-permute-start(f32[256,256]{1,0:T(8,128)S(1)} %get-tuple-element.39), channel_id=1, source_target_pairs={{0,2},{8,9},{16,18},{24,25},{1,3},{9,8},{17,19},{25,24},{2,0},{10,... | collective-permute-start | bytes 786440 | tf_op jit(solution)/shard_map/ppermute | solution.py:55
  18.2 1.3 %collective-permute-done.5.crossed = f32[256,256]{1,0:T(8,128)S(1)} collective-permute-done((f32[256,256]{1,0:T(8,128)S(1)}, f32[256,256]{1,0:T(8,128)S(1)}, u32[]{:S(2)}, u32[]{:S(2)}) %collective-permute-start.5) | collective-permute-done | bytes 262176 | tf_op jit(solution)/shard_map/ppermute | solution.py:55
  19.5 1.1 %shard_map.30 = (f32[256,256]{1,0:T(8,128)S(1)}, f32[256,256]{1,0:T(8,128)S(1)}) custom-call(f32[256,256]{1,0:T(8,128)S(1)} %broadcast_select_fusion.mine, f32[256,256]{1,0:T(8,128)S(1)} %collective-permute-done.other, f32[256,256]{1,0:T(8,128)S(1)} %shard_map.28.chip, f32[256,256]{1,0:T(8,128)S(1)} %get-tuple-element.32.close, ...), custom_call_target="tpu_custom_call" | custom-call | flops 301989888 | tf_op jit(solution)/shard_map/pallas_call | solution.py:64
  20.7 0.5 %collective-permute-start.9 = (f32[128,256]{1,0:T(8,128)S(1)}, f32[128,256]{1,0:T(8,128)S(1)}, u32[]{:S(2)}, u32[]{:S(2)}) collective-permute-start(f32[128,256]{1,0:T(8,128)S(1)} %get-tuple-element.43), channel_id=1, source_target_pairs={{0,8},{8,0},{16,24},{24,16},{1,9},{9,1},{17,25},{25,17},{2,10},{10... | collective-permute-start | bytes 393224 | tf_op jit(solution)/shard_map/ppermute | solution.py:55
  21.2 3.0 %collective-permute-done.7.value = f32[256,256]{1,0:T(8,128)S(1)} collective-permute-done((f32[256,256]{1,0:T(8,128)S(1)}, f32[256,256]{1,0:T(8,128)S(1)}, u32[]{:S(2)}, u32[]{:S(2)}) %collective-permute-start.7) | collective-permute-done | bytes 262176 | tf_op jit(solution)/shard_map/ppermute | solution.py:55
  24.3 0.3 %shard_map.34.near = f32[256,256]{1,0:T(8,128)S(1)} custom-call(f32[256,256]{1,0:T(8,128)S(1)} %collective-permute-done.5.crossed, f32[128,256]{1,0:T(8,128)S(1)} %collective-permute-done.8.top, f32[128,256]{1,0:T(8,128)S(1)} %collective-permute-done.9.bottom), custom_call_target="tpu_custom_call" | custom-call | flops 100663296 | tf_op jit(solution)/shard_map/pallas_call | solution.py:64
  24.7 0.2 collective-permute-start.11
  24.9 0.9 %shard_map.35 = (f32[256,256]{1,0:T(8,128)S(1)}, f32[256,256]{1,0:T(8,128)S(1)}) custom-call(f32[256,256]{1,0:T(8,128)S(1)} %get-tuple-element.35.after, f32[256,256]{1,0:T(8,128)S(1)} %get-tuple-element.36.wp, f32[256,256]{1,0:T(8,128)S(1)} %shard_map.34.near, f32[256,256]{1,0:T(8,128)S(1)} %collective-permute-done.1.wide, f32[256,256]{1,0:T(8,128)S(1)} %shard_map.32.by_d, ...), custom_call_target="tpu_custom_call" | custom-call | flops 402653184 | tf_op jit(solution)/shard_map/pallas_call | solution.py:64
  25.8 0.4 %shard_map.36 = (f32[256,256]{1,0:T(8,128)S(1)}, f32[256,256]{1,0:T(8,128)S(1)}) custom-call(f32[256,256]{1,0:T(8,128)S(1)} %get-tuple-element.47.a, f32[256,256]{1,0:T(8,128)S(1)} %get-tuple-element.48.b, f32[256,256]{1,0:T(8,128)S(1)} %collective-permute-done.10.come), custom_call_target="tpu_custom_call" | custom-call | flops 100663296 | tf_op jit(solution)/shard_map/pallas_call | solution.py:64
  26.2 1.3 %shard_map.37 = f32[256,256]{1,0:T(8,128)} custom-call(f32[256,256]{1,0:T(8,128)S(1)} %get-tuple-element.49.a, f32[256,256]{1,0:T(8,128)S(1)} %get-tuple-element.50.b, f32[256,256]{1,0:T(8,128)S(1)} %collective-permute-done.11.come), custom_call_target="tpu_custom_call" | custom-call | flops 201326592 | tf_op jit(solution)/shard_map/pallas_call | solution.py:64
  (14 shorter events, 0.4 us)
Async XLA Ops:
  0.0 1.8 %collective-permute-start = (f32[256,256]{1,0:T(8,128)}, f32[256,256]{1,0:T(8,128)S(1)}, u32[]{:S(2)}, u32[]{:S(2)}) collective-permute-start(f32[256,256]{1,0:T(8,128)} %bitcast.5), channel_id=1, source_target_pairs={{0,8},{8,0},{16,24},{24,16},{1,9},{9,1},{17,25},{25,17},{2,10},{10... | collective-permute-start | bytes 786440 | tf_op jit(solution)/shard_map/ppermute | solution.py:55
  2.1 7.3 %collective-permute-start.2 = (f32[256,256]{1,0:T(8,128)S(1)}, f32[256,256]{1,0:T(8,128)S(1)}, u32[]{:S(2)}, u32[]{:S(2)}) collective-permute-start(f32[256,256]{1,0:T(8,128)S(1)} %shard_map.28.chip), channel_id=1, source_target_pairs={{0,16},{8,9},{16,0},{24,25},{1,17},{9,8},{17,1},{25,24},{2,18},{10... | collective-permute-start | bytes 786440 | tf_op jit(solution)/shard_map/ppermute | solution.py:55
  5.0 8.6 %collective-permute-start.1 = (f32[256,256]{1,0:T(8,128)S(1)}, f32[256,256]{1,0:T(8,128)S(1)}, u32[]{:S(2)}, u32[]{:S(2)}) collective-permute-start(f32[256,256]{1,0:T(8,128)S(1)} %shard_map.28.chip), channel_id=1, source_target_pairs={{0,17},{8,14},{16,1},{24,30},{1,16},{9,15},{17,0},{25,31},{2,19},{... | collective-permute-start | bytes 786440 | tf_op jit(solution)/shard_map/ppermute | solution.py:55
  9.4 1.4 %collective-permute-start.3 = (f32[128,256]{1,0:T(8,128)S(1)}, f32[128,256]{1,0:T(8,128)S(1)}, u32[]{:S(2)}, u32[]{:S(2)}) collective-permute-start(f32[128,256]{1,0:T(8,128)S(1)} %get-tuple-element.52), channel_id=1, source_target_pairs={{0,8},{8,0},{16,24},{24,16},{1,9},{9,1},{17,25},{25,17},{2,10},{10... | collective-permute-start | bytes 393224 | tf_op jit(solution)/shard_map/ppermute | solution.py:55
  9.5 1.5 %collective-permute-start.4 = (f32[128,256]{1,0:T(8,128)S(1)}, f32[128,256]{1,0:T(8,128)S(1)}, u32[]{:S(2)}, u32[]{:S(2)}) collective-permute-start(f32[128,256]{1,0:T(8,128)S(1)} %get-tuple-element.51), channel_id=1, source_target_pairs={{0,8},{8,0},{16,24},{24,16},{1,9},{9,1},{17,25},{25,17},{2,10},{10... | collective-permute-start | bytes 393224 | tf_op jit(solution)/shard_map/ppermute | solution.py:55
  13.7 5.8 %copy-start = (f32[1,1,256,256]{3,2,1,0:T(8,128)S(1)}, f32[1,1,256,256]{3,2,1,0:T(8,128)}, u32[]{:S(2)}) copy-start(f32[1,1,256,256]{3,2,1,0:T(8,128)} %param.3) | copy-start | bytes 786436
  13.7 5.8 %collective-permute-start.5 = (f32[256,256]{1,0:T(8,128)S(1)}, f32[256,256]{1,0:T(8,128)S(1)}, u32[]{:S(2)}, u32[]{:S(2)}) collective-permute-start(f32[256,256]{1,0:T(8,128)S(1)} %collective-permute-done.1.wide), channel_id=1, source_target_pairs={{0,8},{8,16},{16,24},{24,0},{1,9},{9,17},{17,25},{25,1},{2,10},{10... | collective-permute-start | bytes 786440 | tf_op jit(solution)/shard_map/ppermute | solution.py:55
  14.0 10.3 %collective-permute-start.7 = (f32[256,256]{1,0:T(8,128)S(1)}, f32[256,256]{1,0:T(8,128)S(1)}, u32[]{:S(2)}, u32[]{:S(2)}) collective-permute-start(f32[256,256]{1,0:T(8,128)S(1)} %get-tuple-element.40), channel_id=1, source_target_pairs={{0,4},{8,25},{16,20},{24,9},{1,5},{9,24},{17,21},{25,8},{2,6},{10,... | collective-permute-start | bytes 786440 | tf_op jit(solution)/shard_map/ppermute | solution.py:55
  16.6 8.1 %collective-permute-start.6 = (f32[256,256]{1,0:T(8,128)S(1)}, f32[256,256]{1,0:T(8,128)S(1)}, u32[]{:S(2)}, u32[]{:S(2)}) collective-permute-start(f32[256,256]{1,0:T(8,128)S(1)} %get-tuple-element.39), channel_id=1, source_target_pairs={{0,2},{8,9},{16,18},{24,25},{1,3},{9,8},{17,19},{25,24},{2,0},{10,... | collective-permute-start | bytes 786440 | tf_op jit(solution)/shard_map/ppermute | solution.py:55
  20.7 3.6 %collective-permute-start.8 = (f32[128,256]{1,0:T(8,128)S(1)}, f32[128,256]{1,0:T(8,128)S(1)}, u32[]{:S(2)}, u32[]{:S(2)}) collective-permute-start(f32[128,256]{1,0:T(8,128)S(1)} %get-tuple-element.42), channel_id=1, source_target_pairs={{0,8},{8,0},{16,24},{24,16},{1,9},{9,1},{17,25},{25,17},{2,10},{10... | collective-permute-start | bytes 393224 | tf_op jit(solution)/shard_map/ppermute | solution.py:55
  20.7 3.5 %collective-permute-start.9 = (f32[128,256]{1,0:T(8,128)S(1)}, f32[128,256]{1,0:T(8,128)S(1)}, u32[]{:S(2)}, u32[]{:S(2)}) collective-permute-start(f32[128,256]{1,0:T(8,128)S(1)} %get-tuple-element.43), channel_id=1, source_target_pairs={{0,8},{8,0},{16,24},{24,16},{1,9},{9,1},{17,25},{25,17},{2,10},{10... | collective-permute-start | bytes 393224 | tf_op jit(solution)/shard_map/ppermute | solution.py:55
  24.2 1.5 %collective-permute-start.10 = (f32[256,256]{1,0:T(8,128)S(1)}, f32[256,256]{1,0:T(8,128)S(1)}, u32[]{:S(2)}, u32[]{:S(2)}) collective-permute-start(f32[256,256]{1,0:T(8,128)S(1)} %collective-permute-done.7.value), channel_id=1, source_target_pairs={{0,8},{8,0},{16,24},{24,16},{1,9},{9,1},{17,25},{25,17},{2,10},{10... | collective-permute-start | bytes 786440 | tf_op jit(solution)/shard_map/ppermute | solution.py:55
  24.7 1.5 %collective-permute-start.11 = (f32[256,256]{1,0:T(8,128)S(1)}, f32[256,256]{1,0:T(8,128)S(1)}, u32[]{:S(2)}, u32[]{:S(2)}) collective-permute-start(f32[256,256]{1,0:T(8,128)S(1)} %collective-permute-done.6.by_y), channel_id=1, source_target_pairs={{0,8},{8,0},{16,24},{24,16},{1,9},{9,1},{17,25},{25,17},{2,10},{10... | collective-permute-start | bytes 786440 | tf_op jit(solution)/shard_map/ppermute | solution.py:55
